TPU v7x, 32 devices: a whole 2x2x4 slice. The times are simulated.
32 devices in a mesh: section: 2 (over x), dp: 16 (over z, y, core).
Axes of the slice: x: 2, y: 2, z: 4, core: 2. Of those that a mesh axis runs over, the one named last changes fastest.
Arguments:
- tokens: bfloat16 [8192, 1024], P('dp'), may hold values from -6 to 6
- segment_ids: int32 [32, 256], P('dp'), may hold values from 0 to 3, never falling along the last dimension, each value on 1 to 128 neighbouring positions
- cotangent: bfloat16 [8192, 1024], P('dp'), may hold values from -6 to 6
- w_qkv: bfloat16 [2, 1024, 3072], P('section', 'dp'), may hold values from -0.1875 to 0.1875
- w_attn_out: bfloat16 [2, 1024, 1024], P('section', 'dp'), may hold values from -0.75 to 0.75
- w_fc: bfloat16 [2, 1024, 4096], P('section', 'dp'), may hold values from -0.1875 to 0.1875
- w_proj: bfloat16 [2, 4096, 1024], P('section', 'dp'), may hold values from -0.09375 to 0.09375
- gains: bfloat16 [2, 2, 1024], P('section', None, 'dp'), may hold values from 0.5 to 1.5
- biases: bfloat16 [2, 11264], P('section', 'dp'), may hold values from -1.1953125 to 1.1953125
- prefix_embed: bfloat16 [10, 1024], replicated, may hold values from -6 to 6
- reparam_in: bfloat16 [1024, 512], replicated, may hold values from -0.1875 to 0.1875
- reparam_in_bias: bfloat16 [512], replicated, may hold values from -3 to 3
- reparam_out: bfloat16 [512, 4096], P(None, 'section'), may hold values from -0.25 to 0.25
- reparam_out_bias: bfloat16 [4096], P('section'), may hold values from -3 to 3
Outputs:
- layer_outs: bfloat16 [2, 8192, 1024], P('section', 'dp')
- input_grads: bfloat16 [2, 8192, 1024], P('section', 'dp')
- grad_w_qkv: float32 [2, 1024, 3072], P('section', 'dp')
- grad_w_attn_out: float32 [2, 1024, 1024], P('section', 'dp')
- grad_w_fc: float32 [2, 1024, 4096], P('section', 'dp')
- grad_w_proj: float32 [2, 4096, 1024], P('section', 'dp')
- grad_gains: float32 [2, 2, 1024], P('section', None, 'dp')
- grad_biases: float32 [2, 11264], P('section', 'dp')
- grad_prefix_embed: float32 [10, 1024], replicated
- grad_reparam_in: float32 [1024, 512], replicated
- grad_reparam_in_bias: float32 [512], replicated
- grad_reparam_out: float32 [512, 4096], P(None, 'section')
- grad_reparam_out_bias: float32 [4096], P('section')
Inputs may be any that keep to these rules, and one draw needn't show every extreme that they name: `segment_ids`: within each packed row the ids never fall, every id appears, each segment has 1 to 128 tokens and one has exactly 128.
All inputs are finite; a program needn't handle non-finite values.
Results may differ from a plain program's by a relative error of at most 0.019.
Values may be sent and summed in bfloat16 or wider, within the bound.
A program may use at most 320 MiB of HBM per device.

v0:
```python
import math

import jax
import jax.numpy as jnp
from jax import lax
from jax.sharding import PartitionSpec as P

HEADS = 16


EPS = 1e-05
NEG = -1000000000.0


def passed_along(shard, axis, by):
    size = lax.axis_size(axis)
    pairs = [(i, i + by) for i in range(size) if 0 <= i + by < size]
    return lax.ppermute(shard, axis, pairs)


def norm_rows(v, gain, shift):
    mean = jnp.mean(v, axis=-1, keepdims=True)
    cent = v - mean
    var = jnp.mean(cent * cent, axis=-1, keepdims=True)
    return cent * lax.rsqrt(var + EPS) * gain + shift


def gelu_tanh(v):
    return jax.nn.gelu(v, approximate=True)


def forward_layer(h_b, segs, pkey, pval, params):
    w_q, w_o, w_f, w_p, gain_pair, bias_all = params
    width = w_o.shape[0]
    length = h_b.shape[0]
    heads, head_dim = (pkey.shape[1], pkey.shape[2])
    scale = 1.0 / math.sqrt(head_dim)
    gain_f = gain_pair.astype(jnp.float32)
    bias_f = bias_all.astype(jnp.float32)
    hf = h_b.astype(jnp.float32)
    a1b = norm_rows(hf, gain_f[0], bias_f[9 * width : 10 * width]).astype(jnp.bfloat16)
    qkv_b = (jnp.dot(a1b, w_q, preferred_element_type=jnp.float32) + bias_f[: 3 * width]).astype(
        jnp.bfloat16
    )
    split = qkv_b.reshape(length, 3, heads, head_dim)
    query, keys, values = (split[:, 0], split[:, 1], split[:, 2])
    s_tok = jnp.einsum("lhe,mhe->hlm", query, keys, preferred_element_type=jnp.float32) * scale
    s_pre = jnp.einsum("lhe,phe->hlp", query, pkey, preferred_element_type=jnp.float32) * scale
    place = jnp.arange(length)
    allowed = (segs[:, None] == segs[None, :]) & (place[None, :] <= place[:, None])
    s_tok = jnp.where(allowed[None], s_tok, NEG)
    top = jnp.maximum(
        jnp.max(s_tok, axis=-1, keepdims=True), jnp.max(s_pre, axis=-1, keepdims=True)
    )
    e_tok = jnp.exp(s_tok - top)
    e_pre = jnp.exp(s_pre - top)
    total = jnp.sum(e_tok, axis=-1, keepdims=True) + jnp.sum(e_pre, axis=-1, keepdims=True)
    p_tok = e_tok / total
    p_pre = e_pre / total
    mixed = jnp.einsum(
        "hlm,mhe->lhe", p_tok.astype(jnp.bfloat16), values, preferred_element_type=jnp.float32
    ) + jnp.einsum(
        "hlp,phe->lhe", p_pre.astype(jnp.bfloat16), pval, preferred_element_type=jnp.float32
    )
    attn_b = mixed.reshape(length, width).astype(jnp.bfloat16)
    resid = hf + (
        jnp.dot(attn_b, w_o, preferred_element_type=jnp.float32) + bias_f[3 * width : 4 * width]
    )
    a2b = norm_rows(resid, gain_f[1], bias_f[10 * width : 11 * width]).astype(jnp.bfloat16)
    pre_act = jnp.dot(a2b, w_f, preferred_element_type=jnp.float32) + bias_f[4 * width : 8 * width]
    act_b = gelu_tanh(pre_act).astype(jnp.bfloat16)
    result = resid + (
        jnp.dot(act_b, w_p, preferred_element_type=jnp.float32) + bias_f[8 * width : 9 * width]
    )
    return (result, (hf, a1b, qkv_b, p_tok, p_pre, attn_b, resid, a2b, pre_act, act_b))


def backward_ffn(grad_out, keep, params):
    w_q, w_o, w_f, w_p, gain_pair, bias_all = params
    hf, a1b, qkv_b, p_tok, p_pre, attn_b, resid, a2b, pre_act, act_b = keep
    width = w_o.shape[0]
    gain_f = gain_pair.astype(jnp.float32)
    bias_f = bias_all.astype(jnp.float32)
    dm_b = grad_out.astype(jnp.bfloat16)
    grad_wp = jnp.einsum("lf,ld->fd", act_b, dm_b, preferred_element_type=jnp.float32)
    grad_bp = jnp.sum(dm_b.astype(jnp.float32), axis=0)
    d_act = jnp.dot(dm_b, w_p.T, preferred_element_type=jnp.float32)
    dpre_b = jax.vjp(gelu_tanh, pre_act)[1](d_act)[0].astype(jnp.bfloat16)
    grad_wf = jnp.einsum("ld,lf->df", a2b, dpre_b, preferred_element_type=jnp.float32)
    grad_bf = jnp.sum(dpre_b.astype(jnp.float32), axis=0)
    d_a2 = jnp.dot(dpre_b, w_f.T, preferred_element_type=jnp.float32)
    norm_back = jax.vjp(norm_rows, resid, gain_f[1], bias_f[10 * width : 11 * width])[1]
    d_resid_norm, grad_g2, grad_c2 = norm_back(d_a2)
    d_resid = grad_out + d_resid_norm
    return (d_resid, (grad_wf, grad_wp), (grad_bf, grad_bp, grad_g2, grad_c2))


def backward_attn(d_resid, keep, pkey, pval, params):
    w_q, w_o, w_f, w_p, gain_pair, bias_all = params
    hf, a1b, qkv_b, p_tok, p_pre, attn_b, resid, a2b, pre_act, act_b = keep
    width = w_o.shape[0]
    length = hf.shape[0]
    heads, head_dim = (pkey.shape[1], pkey.shape[2])
    prefix_len = pkey.shape[0]
    scale = 1.0 / math.sqrt(head_dim)
    gain_f = gain_pair.astype(jnp.float32)
    bias_f = bias_all.astype(jnp.float32)
    split = qkv_b.reshape(length, 3, heads, head_dim)
    query, keys, values = (split[:, 0], split[:, 1], split[:, 2])
    dat_b = d_resid.astype(jnp.bfloat16)
    grad_wo = jnp.einsum("ld,le->de", attn_b, dat_b, preferred_element_type=jnp.float32)
    grad_bo = jnp.sum(dat_b.astype(jnp.float32), axis=0)
    dattn_b = jnp.dot(dat_b, w_o.T, preferred_element_type=jnp.float32).astype(jnp.bfloat16)
    dattn_b = dattn_b.reshape(length, heads, head_dim)
    dp_tok = jnp.einsum("lhe,mhe->hlm", dattn_b, values, preferred_element_type=jnp.float32)
    dp_pre = jnp.einsum("lhe,phe->hlp", dattn_b, pval, preferred_element_type=jnp.float32)
    row_dot = jnp.sum(p_tok * dp_tok, axis=-1, keepdims=True) + jnp.sum(
        p_pre * dp_pre, axis=-1, keepdims=True
    )
    ds_tok = (p_tok * (dp_tok - row_dot)).astype(jnp.bfloat16)
    ds_pre = (p_pre * (dp_pre - row_dot)).astype(jnp.bfloat16)
    d_query = (
        jnp.einsum("hlm,mhe->lhe", ds_tok, keys, preferred_element_type=jnp.float32)
        + jnp.einsum("hlp,phe->lhe", ds_pre, pkey, preferred_element_type=jnp.float32)
    ) * scale
    d_keys = jnp.einsum("hlm,lhe->mhe", ds_tok, query, preferred_element_type=jnp.float32) * scale
    d_values = jnp.einsum(
        "hlm,lhe->mhe", p_tok.astype(jnp.bfloat16), dattn_b, preferred_element_type=jnp.float32
    )
    grad_pkey = (
        jnp.einsum("hlp,lhe->phe", ds_pre, query, preferred_element_type=jnp.float32) * scale
    )
    grad_pval = jnp.einsum(
        "hlp,lhe->phe", p_pre.astype(jnp.bfloat16), dattn_b, preferred_element_type=jnp.float32
    )
    dqkv_b = (
        jnp.stack([d_query, d_keys, d_values], axis=1)
        .reshape(length, 3 * width)
        .astype(jnp.bfloat16)
    )
    grad_wq = jnp.einsum("ld,lc->dc", a1b, dqkv_b, preferred_element_type=jnp.float32)
    grad_bq = jnp.sum(dqkv_b.astype(jnp.float32), axis=0)
    d_a1 = jnp.dot(dqkv_b, w_q.T, preferred_element_type=jnp.float32)
    norm_back_first = jax.vjp(norm_rows, hf, gain_f[0], bias_f[9 * width : 10 * width])[1]
    d_in_norm, grad_g1, grad_c1 = norm_back_first(d_a1)
    d_input = d_resid + d_in_norm
    grad_prefix = jnp.concatenate(
        [grad_pkey.reshape(prefix_len, width), grad_pval.reshape(prefix_len, width)], axis=1
    )
    return (d_input, (grad_wq, grad_wo), (grad_bq, grad_bo, grad_g1, grad_c1), grad_prefix)


def assemble(ffn_mats, ffn_small, attn_mats, attn_small):
    grad_bf, grad_bp, grad_g2, grad_c2 = ffn_small
    grad_bq, grad_bo, grad_g1, grad_c1 = attn_small
    grad_gains = jnp.stack([grad_g1, grad_g2])
    grad_bias = jnp.concatenate([grad_bq, grad_bo, grad_bf, grad_bp, grad_c1, grad_c2])
    return (attn_mats[0], attn_mats[1], ffn_mats[0], ffn_mats[1], grad_gains, grad_bias)


def on_device(
    tokens,
    segment_ids,
    cotangent,
    w_qkv,
    w_attn_out,
    w_fc,
    w_proj,
    gains,
    biases,
    prefix_embed,
    reparam_in,
    reparam_in_bias,
    reparam_out,
    reparam_out_bias,
):
    section = lax.axis_index("section")
    micro, row_len = segment_ids.shape
    width = tokens.shape[1]
    prefix_len = prefix_embed.shape[0]
    head_dim = width // HEADS
    gathered = (
        lax.all_gather(w_qkv, "dp", axis=1, tiled=True),
        lax.all_gather(w_attn_out, "dp", axis=1, tiled=True),
        lax.all_gather(w_fc, "dp", axis=1, tiled=True),
        lax.all_gather(w_proj, "dp", axis=1, tiled=True),
        lax.all_gather(gains, "dp", axis=2, tiled=True),
        lax.all_gather(biases, "dp", axis=1, tiled=True),
    )
    params = tuple((item[0] for item in gathered))
    pre_hidden = jnp.dot(
        prefix_embed, reparam_in, preferred_element_type=jnp.float32
    ) + reparam_in_bias.astype(jnp.float32)
    hidden = jnp.tanh(pre_hidden)
    hidden_b = hidden.astype(jnp.bfloat16)
    prefix_kv = (
        jnp.dot(hidden_b, reparam_out, preferred_element_type=jnp.float32)
        + reparam_out_bias.astype(jnp.float32)
    ).astype(jnp.bfloat16)
    pkey = prefix_kv[:, :width].reshape(prefix_len, HEADS, head_dim)
    pval = prefix_kv[:, width:].reshape(prefix_len, HEADS, head_dim)
    token_rows = tokens.reshape(micro, row_len, width)
    cot_rows = cotangent.reshape(micro, row_len, width)
    received = jnp.zeros((row_len, width), jnp.bfloat16)
    outputs = jnp.zeros((micro, row_len, width), jnp.bfloat16)
    stored = []
    for tick in range(micro + 1):
        index = tick - section
        active = (index >= 0) & (index < micro)
        slot = jnp.clip(index, 0, micro - 1)
        segs = segment_ids[slot]
        h_b = jnp.where(section == 0, token_rows[slot], received)
        result, keep = forward_layer(h_b, segs, pkey, pval, params)
        result_b = result.astype(jnp.bfloat16)
        outputs = jnp.where(active, outputs.at[slot].set(result_b), outputs)
        stored.append(keep)
        if tick < micro:
            received = passed_along(result_b, "section", 1)
    regathered = (
        lax.all_gather(w_qkv, "dp", axis=1, tiled=True),
        lax.all_gather(w_attn_out, "dp", axis=1, tiled=True),
        lax.all_gather(w_fc, "dp", axis=1, tiled=True),
        lax.all_gather(w_proj, "dp", axis=1, tiled=True),
        lax.all_gather(gains, "dp", axis=2, tiled=True),
        lax.all_gather(biases, "dp", axis=1, tiled=True),
    )
    params_back = tuple((item[0] for item in regathered))
    stacked = jax.tree.map(lambda *items: jnp.stack(items), *stored)
    coming = jnp.zeros((row_len, width), jnp.bfloat16)
    in_grads = jnp.zeros((micro, row_len, width), jnp.bfloat16)
    grad_total = None
    prefix_total = None
    for tick in range(micro + 1):
        index = micro - tick - section
        active = (index >= 0) & (index < micro)
        slot = jnp.clip(index, 0, micro - 1)
        segs = segment_ids[slot]
        saved = jax.tree.map(lambda item: item[slot + section], stacked)
        grad_out = jnp.where(
            section == 1, cot_rows[slot].astype(jnp.float32), coming.astype(jnp.float32)
        )
        keep = saved
        d_resid, ffn_mats, ffn_small = backward_ffn(grad_out, keep, params_back)
        ffn_mats = jax.tree.map(
            lambda item: jnp.where(active, item, jnp.zeros_like(item)), ffn_mats
        )
        ffn_small = jax.tree.map(
            lambda item: jnp.where(active, item, jnp.zeros_like(item)), ffn_small
        )
        d_input, attn_mats, attn_small, grad_prefix = backward_attn(
            d_resid, keep, pkey, pval, params_back
        )
        attn_mats = jax.tree.map(
            lambda item: jnp.where(active, item, jnp.zeros_like(item)), attn_mats
        )
        attn_small = jax.tree.map(
            lambda item: jnp.where(active, item, jnp.zeros_like(item)), attn_small
        )
        grad_prefix = jnp.where(active, grad_prefix, jnp.zeros_like(grad_prefix))
        grads = assemble(ffn_mats, ffn_small, attn_mats, attn_small)
        if grad_total is None:
            grad_total = grads
            prefix_total = grad_prefix
        else:
            grad_total = jax.tree.map(lambda left, right: left + right, grad_total, grads)
            prefix_total = prefix_total + grad_prefix
        d_input_b = d_input.astype(jnp.bfloat16)
        in_grads = jnp.where(active, in_grads.at[slot].set(d_input_b), in_grads)
        if tick < micro:
            coming = passed_along(d_input_b, "section", -1)
    lifted = tuple((item[None] for item in grad_total))
    weight_grads = (
        lax.psum_scatter(lifted[0], "dp", scatter_dimension=1, tiled=True),
        lax.psum_scatter(lifted[1], "dp", scatter_dimension=1, tiled=True),
        lax.psum_scatter(lifted[2], "dp", scatter_dimension=1, tiled=True),
        lax.psum_scatter(lifted[3], "dp", scatter_dimension=1, tiled=True),
        lax.psum_scatter(lifted[4], "dp", scatter_dimension=2, tiled=True),
        lax.psum_scatter(lifted[5], "dp", scatter_dimension=1, tiled=True),
    )
    prefix_grad = lax.psum(prefix_total, "dp")
    prefix_grad_b = prefix_grad.astype(jnp.bfloat16)
    grad_reparam_out = jnp.einsum(
        "pr,pc->rc", hidden_b, prefix_grad_b, preferred_element_type=jnp.float32
    )
    grad_reparam_out_bias = jnp.sum(prefix_grad_b.astype(jnp.float32), axis=0)
    hidden_part = jnp.dot(prefix_grad_b, reparam_out.T, preferred_element_type=jnp.float32)
    hidden_grad = lax.psum(hidden_part, "section")
    dpre_hidden_b = (hidden_grad * (1.0 - hidden * hidden)).astype(jnp.bfloat16)
    grad_reparam_in = jnp.einsum(
        "pd,pr->dr", prefix_embed, dpre_hidden_b, preferred_element_type=jnp.float32
    )
    grad_reparam_in_bias = jnp.sum(dpre_hidden_b.astype(jnp.float32), axis=0)
    grad_prefix_embed = jnp.dot(dpre_hidden_b, reparam_in.T, preferred_element_type=jnp.float32)
    layer_outs = outputs.reshape(1, micro * row_len, width)
    input_grads = in_grads.reshape(1, micro * row_len, width)
    return (
        layer_outs,
        input_grads,
        weight_grads[0],
        weight_grads[1],
        weight_grads[2],
        weight_grads[3],
        weight_grads[4],
        weight_grads[5],
        grad_prefix_embed,
        grad_reparam_in,
        grad_reparam_in_bias,
        grad_reparam_out,
        grad_reparam_out_bias,
    )


def solution(mesh):
    return jax.shard_map(
        on_device,
        mesh=mesh,
        in_specs=(
            P("dp", None),
            P("dp", None),
            P("dp", None),
            P("section", "dp", None),
            P("section", "dp", None),
            P("section", "dp", None),
            P("section", "dp", None),
            P("section", None, "dp"),
            P("section", "dp"),
            P(),
            P(),
            P(),
            P(None, "section"),
            P("section"),
        ),
        out_specs=(
            P("section", "dp", None),
            P("section", "dp", None),
            P("section", "dp", None),
            P("section", "dp", None),
            P("section", "dp", None),
            P("section", "dp", None),
            P("section", None, "dp"),
            P("section", "dp"),
            P(),
            P(),
            P(),
            P(None, "section"),
            P("section"),
        ),
        check_vma=False,
    )
```

profile of v0, /device:TPU:0, one launch (start us, length us, event | category | flops | bytes accessed | tf_op | source)
XLA Modules:
  0.0 1316.1 jit_solution(17992378972701188129)
XLA Ops:
  13.0 64.3 %all-reduce = bf16[11264]{0:T(1024)(128)(2,1)S(1)} all-reduce(bf16[11264]{0:T(1024)(128)(2,1)S(1)} %dynamic-update-slice.24), channel_id=1, replica_groups=mesh['section'=2,'dp'=16] {'dp'}, use_global_device_ids=true, to_apply=%add | all-reduce | flops 11264 | bytes 45056
  82.3 19.6 %all_gather.23 = bf16[1,2,1024]{1,0,2:T(2,128)(2,1)S(1)} all-gather(bf16[1,2,64]{1,0,2:T(2,128)(2,1)S(1)} %copy.154), channel_id=1, replica_groups=mesh['section'=2,'dp'=16] {'dp'}, dimensions={2}, use_global_device_ids=true | all-gather | bytes 4352 | tf_op jit(solution)/shard_map/all_gather | solution.py:187
  107.8 8.0 slice_reduce_fusion
  116.8 6.0 fusion.117
  131.0 3.1 fusion.244
  139.1 55.1 %all-gather.9.cloned.1.call-done = bf16[1,1024,4096]{2,1,0:T(8,128)(2,1)} async-done(((bf16[1,64,4096]{2,1,0:T(8,128)(2,1)}), bf16[1,1024,4096]{2,1,0:T(8,128)(2,1)}) %all-gather.9.cloned.1.call-update) | async-done | bytes 8388624 | tf_op jit(solution)/shard_map/all_gather | solution.py:185
  194.2 7.9 fusion.36
  202.1 67.3 %all-gather.11.cloned.1.call-done = bf16[1,4096,1024]{2,1,0:T(8,128)(2,1)} async-done(((bf16[1,256,1024]{2,1,0:T(8,128)(2,1)}), bf16[1,4096,1024]{2,1,0:T(8,128)(2,1)}) %all-gather.11.cloned.1.call-update) | async-done | bytes 8388624 | tf_op jit(solution)/shard_map/all_gather | solution.py:186
  269.6 8.5 bitcast_dynamic-update-slice_fusion.1
  278.1 3.5 collective-permute-start
  284.6 8.7 collective-permute-done
  295.1 5.9 fusion.114
  301.0 3.0 copy.159
  316.9 3.7 fusion.296
  320.7 4.7 collective-permute-start.1
  328.3 7.7 collective-permute-done.1
  337.9 3.1 fusion.111
  350.3 3.0 fusion.289
  359.5 4.0 fusion.238
  365.8 8.3 fusion.42
  374.1 10.8 pad_maximum_fusion
  384.9 11.5 convert_reduce_fusion.2
  396.6 7.5 multiply_reduce_fusion.4
  415.1 10.7 pad_maximum_fusion.1
  425.8 3.8 fusion.254
  429.6 3.0 fusion.98
  432.6 3.2 fusion.99
  441.6 3.0 copy.181
  450.6 4.3 fusion.318
  458.6 6.1 multiply_reduce_fusion.5
  465.4 3.0 fusion.426
  472.5 11.8 collective-permute-done.2
  484.6 12.4 convert_reduce_fusion.1
  498.4 3.2 multiply_reduce_fusion.2
  509.1 3.1 fusion.255
  512.3 3.0 fusion.94
  515.3 3.2 fusion.95
  524.0 6.2 multiply_reduce_fusion.3
  535.8 3.9 fusion.316
  539.7 7.0 collective-permute-done.3
  547.1 7.7 convert_reduce_fusion
  556.2 6.6 multiply_reduce_fusion
  570.3 3.1 fusion.256
  573.5 3.0 fusion.90
  576.5 3.2 fusion.91
  583.6 5.3 multiply_reduce_fusion.1
  590.4 3.4 copy.209
  593.9 5.4 add_bitcast_fusion.3
  601.4 6.4 fusion.323
  607.8 6.3 fusion.321
  614.1 8.7 add_bitcast_fusion.2
  625.0 8.1 fusion.313
  633.1 8.1 fusion.311
  641.3 16.8 %add_bitcast_fusion.1 = f32[1,1024,4096]{2,1,0:T(8,128)} fusion(f32[1024,4096]{1,0:T(8,128)} %fusion.311, f32[1024,4096]{1,0:T(8,128)} %fusion.313, bf16[256,4096]{1,0:T(8,128)(2,1)} %copy-done.75, pred[]{:T(512)S(6)} %and.61, pred[]{:T(512)S(6)} %and.64, pred[]{:T(512)S(6)} %and.67, bf16[3,256,1024]{2,1,0:T(8,128)(2,1)} %copy-done.47, s32[]{:T(128)S(6)} %select_n.606), kind=kOutput, calls=%fused_computation.1 | convolution fusion | flops 2168455168 | bytes 52953096 | tf_op jit(solution)/shard_map/ld,lf->df/dot_general | solution.py:89
  658.2 3.9 fusion.437
  667.1 8.1 fusion.142
  675.2 8.1 fusion.140
  683.3 16.2 %add_bitcast_fusion = f32[1,4096,1024]{2,1,0:T(8,128)} fusion(f32[4096,1024]{1,0:T(8,128)} %fusion.140, f32[4096,1024]{1,0:T(8,128)} %fusion.142, bf16[256,1024]{1,0:T(8,128)(2,1)} %copy-done.70, pred[]{:T(512)S(6)} %and.61, pred[]{:T(512)S(6)} %and.64, pred[]{:T(512)S(6)} %and.67, bf16[3,256,4096]{2,1,0:T(8,128)(2,1)} %copy-done.9, s32[]{:T(128)S(6)} %select_n.606), kind=kOutput, calls=%fused_computation | convolution fusion | flops 2168455168 | bytes 52953096 | tf_op jit(solution)/shard_map/lf,ld->fd/dot_general | solution.py:85
  703.7 9.5 fusion.269
  724.8 59.7 %psum.14 = bf16[10,2048]{1,0:T(8,128)(2,1)S(1)} all-reduce(f32[10,2048]{1,0:T(8,128)S(1)} %fusion.355), channel_id=1, replica_groups=mesh['section'=2,'dp'=16] {'dp'}, use_global_device_ids=true, to_apply=%region_87.88 | all-reduce | flops 20480 | bytes 122880 | tf_op jit(solution)/shard_map/psum | solution.py:280
  785.2 24.1 %psum.15 = f32[10,512]{1,0:T(8,128)S(1)} all-reduce(f32[10,512]{1,0:T(8,128)S(1)} %fusion.459), channel_id=1, replica_groups=mesh['section'=2,'dp'=16] {'section'}, use_global_device_ids=true, to_apply=%region_88.89 | all-reduce | flops 5120 | bytes 40960 | tf_op jit(solution)/shard_map/psum | solution.py:287
  828.0 116.3 %reduce-scatter.11.cloned.1.call-done = f32[1,64,3072]{2,1,0:T(8,128)} async-done(((f32[1,1024,3072]{2,1,0:T(8,128)}), f32[1,64,3072]{2,1,0:T(8,128)}) %reduce-scatter.11.cloned.1.call-update) | async-done | bytes 786448 | tf_op jit(solution)/shard_map/reduce_scatter | solution.py:273
  944.3 182.4 %reduce-scatter.15.cloned.1.call-done = f32[1,64,4096]{2,1,0:T(8,128)} async-done(((f32[1,1024,4096]{2,1,0:T(8,128)}), f32[1,64,4096]{2,1,0:T(8,128)}) %reduce-scatter.15.cloned.1.call-update) | async-done | bytes 1048592 | tf_op jit(solution)/shard_map/reduce_scatter | solution.py:275
  1126.7 182.1 %reduce-scatter.17.cloned.1.call-done = f32[1,256,1024]{2,1,0:T(8,128)} async-done(((f32[1,4096,1024]{2,1,0:T(8,128)}), f32[1,256,1024]{2,1,0:T(8,128)}) %reduce-scatter.17.cloned.1.call-update) | async-done | bytes 1048592 | tf_op jit(solution)/shard_map/reduce_scatter | solution.py:276
  (654 shorter events, 179.4 us)
Async XLA Ops:
  7.2 74.3 %copy-start = (bf16[512,2048]{1,0:T(8,128)(2,1)S(1)}, bf16[512,2048]{1,0:T(8,128)(2,1)}, u32[]{:S(2)}) copy-start(bf16[512,2048]{1,0:T(8,128)(2,1)} %param.38) | copy-start | bytes 6291460
  7.2 96.2 %copy-start.182 = (s32[3]{0:T(128)S(1)}, s32[3]{0:T(128)}, u32[]{:S(2)}) copy-start(s32[3]{0:T(128)} %constant.203.clone.1) | copy-start | bytes 40
  7.2 96.0 %copy-start.35 = (bf16[512,1024]{1,0:T(8,128)(2,1)S(1)}, bf16[512,1024]{1,0:T(8,128)(2,1)}, u32[]{:S(2)}) copy-start(bf16[512,1024]{1,0:T(8,128)(2,1)} %param.26) | copy-start | bytes 3145732
  7.2 96.2 %copy-start.146 = (s32[2,256]{1,0:T(2,128)S(1)}, s32[2,256]{1,0:T(2,128)}, u32[]{:S(2)}) copy-start(s32[2,256]{1,0:T(2,128)} %param.27) | copy-start | bytes 6148
  7.2 109.6 %all-gather.5.cloned.1.call-start = ((), (), s32[]{:S(2)}) async-start(), calls=%async_computation.6 | async-start | bytes 6684672 | tf_op jit(solution)/shard_map/all_gather | solution.py:183
  8.0 126.2 %all-gather.7.cloned.1.call-start = ((), (), s32[]{:S(2)}) async-start(), calls=%async_computation.7 | async-start | bytes 2228224 | tf_op jit(solution)/shard_map/all_gather | solution.py:184
  8.7 185.5 %all-gather.9.cloned.1.call-start = ((), (), s32[]{:S(2)}) async-start(), calls=%async_computation.8 | async-start | bytes 8912896 | tf_op jit(solution)/shard_map/all_gather | solution.py:185
  9.4 259.9 %all-gather.11.cloned.1.call-start = ((), (), s32[]{:S(2)}) async-start(), calls=%async_computation.9 | async-start | bytes 8912896 | tf_op jit(solution)/shard_map/all_gather | solution.py:186
  10.0 814.8 %reduce-scatter.19.cloned.1.call-start = ((), (), s32[]{:S(2)}) async-start(), calls=%async_computation.14 | async-start | bytes 557056
  77.2 39.6 %copy-start.132 = (f32[1,3072]{1,0:T(1,128)}, f32[1,3072]{1,0:T(1,128)S(1)}, u32[]{:S(2)}) copy-start(f32[1,3072]{1,0:T(1,128)S(1)} %slice.276) | copy-start | bytes 36868
  106.2 16.6 %copy-start.120 = (f32[1,1024]{1,0:T(1,128)}, f32[1,1024]{1,0:T(1,128)S(1)}, u32[]{:S(2)}) copy-start(f32[1,1024]{1,0:T(1,128)S(1)} %get-tuple-element.216) | copy-start | bytes 12292
  136.8 132.7 %copy-start.19 = (f32[256,1024]{1,0:T(8,128)}, f32[256,1024]{1,0:T(8,128)S(1)}, u32[]{:S(2)}) copy-start(f32[256,1024]{1,0:T(8,128)S(1)} %get-tuple-element.235) | copy-start | bytes 3145732
  194.2 75.3 %copy-start.174 = (f32[1,1024]{1,0:T(1,128)S(1)}, f32[1,1024]{1,0:T(1,128)}, u32[]{:S(2)}) copy-start(f32[1,1024]{1,0:T(1,128)} %get-tuple-element.214) | copy-start | bytes 12292
  269.5 12.2 copy-start.2
  269.5 12.2 copy-start.88
  269.5 12.2 copy-start.95
  269.6 12.2 copy-start.106
  278.1 15.1 %copy-start.36 = (bf16[512,1024]{1,0:T(8,128)(2,1)S(1)}, bf16[512,1024]{1,0:T(8,128)(2,1)}, u32[]{:S(2)}) copy-start(bf16[512,1024]{1,0:T(8,128)(2,1)} %param.26) | copy-start | bytes 3145732
  278.1 17.0 %copy-start.111 = (f32[1024]{0:T(1024)S(1)}, f32[1024]{0:T(1024)}, u32[]{:S(2)}) copy-start(f32[1024]{0:T(1024)} %copy-done.110) | copy-start | bytes 12292
  278.1 17.0 %copy-start.121 = (f32[1,1024]{1,0:T(1,128)S(1)}, f32[1,1024]{1,0:T(1,128)}, u32[]{:S(2)}) copy-start(f32[1,1024]{1,0:T(1,128)} %copy-done.120) | copy-start | bytes 12292
  278.1 17.0 %copy-start.133 = (f32[1,3072]{1,0:T(1,128)S(1)}, f32[1,3072]{1,0:T(1,128)}, u32[]{:S(2)}) copy-start(f32[1,3072]{1,0:T(1,128)} %copy-done.132) | copy-start | bytes 36868
  278.1 15.1 %collective-permute-start = (bf16[256,1024]{1,0:T(8,128)(2,1)S(1)}, bf16[256,1024]{1,0:T(8,128)(2,1)S(1)}, u32[]{:S(2)}, u32[]{:S(2)}) collective-permute-start(bf16[256,1024]{1,0:T(8,128)(2,1)S(1)} %get-tuple-element.237), channel_id=1, source_target_pairs={{0,16},{1,17},{2,18},{3,19},{4,20},{5,21},{6,22},{7,23},{8,24},{9,... | collective-permute-start | bytes 1572872 | tf_op jit(solution)/shard_map/ppermute | solution.py:18
  312.9 51.8 %copy-start.17 = (f32[256,1024]{1,0:T(8,128)}, f32[256,1024]{1,0:T(8,128)S(1)}, u32[]{:S(2)}) copy-start(f32[256,1024]{1,0:T(8,128)S(1)} %get-tuple-element.243) | copy-start | bytes 3145732
  313.7 24.2 %slice-start.8 = ((s8[6291456]{0:T(1024)(128)(4,1)}), s8[2097152]{0:T(1024)(128)(4,1)S(1)}, s32[]{:S(2)}) async-start(s8[6291456]{0:T(1024)(128)(4,1)} %bitcast.874), calls=%async_computation.24 | async-start | bytes 4194304
  316.9 21.0 %slice-start.9 = ((s8[6291456]{0:T(1024)(128)(4,1)}), s8[4194304]{0:T(1024)(128)(4,1)S(1)}, s32[]{:S(2)}) async-start(s8[6291456]{0:T(1024)(128)(4,1)} %bitcast.874), calls=%async_computation.25 | async-start | bytes 8388608
  320.7 15.3 %copy-start.37 = (bf16[512,1024]{1,0:T(8,128)(2,1)S(1)}, bf16[512,1024]{1,0:T(8,128)(2,1)}, u32[]{:S(2)}) copy-start(bf16[512,1024]{1,0:T(8,128)(2,1)} %param.26) | copy-start | bytes 3145732
  320.7 15.3 %collective-permute-start.1 = (bf16[256,1024]{1,0:T(8,128)(2,1)S(1)}, bf16[256,1024]{1,0:T(8,128)(2,1)S(1)}, u32[]{:S(2)}, u32[]{:S(2)}) collective-permute-start(bf16[256,1024]{1,0:T(8,128)(2,1)S(1)} %get-tuple-element.245), channel_id=1, source_target_pairs={{0,16},{1,17},{2,18},{3,19},{4,20},{5,21},{6,22},{7,23},{8,24},{9,... | collective-permute-start | bytes 1572872 | tf_op jit(solution)/shard_map/ppermute | solution.py:18
  365.2 38.8 %copy-start.5 = (f32[3,256,1024]{2,1,0:T(8,128)}, f32[3,256,1024]{2,1,0:T(8,128)S(1)}, u32[]{:S(2)}) copy-start(f32[3,256,1024]{2,1,0:T(8,128)S(1)} %pad_maximum_fusion.4) | copy-start | bytes 9437188
  365.5 31.0 %copy-start.153 = (f32[256]{0:T(256)}, f32[256]{0:T(256)S(1)}, u32[]{:S(2)}) copy-start(f32[256]{0:T(256)S(1)} %broadcast_multiply_fusion.3) | copy-start | bytes 3076
  374.1 10.8 copy-start.8
  404.0 43.8 %copy-start.162 = (f32[256]{0:T(256)}, f32[256]{0:T(256)S(1)}, u32[]{:S(2)}) copy-start(f32[256]{0:T(256)S(1)} %get-tuple-element.152) | copy-start | bytes 3076
  415.1 10.7 copy-start.25
  415.1 14.5 %copy-start.48 = (bf16[1,256,3072]{1,2,0:T(8,128)(2,1)S(1)}, bf16[1,256,3072]{1,2,0:T(8,128)(2,1)}, u32[]{:S(2)}) copy-start(bf16[1,256,3072]{1,2,0:T(8,128)(2,1)} %copy.167) | copy-start | bytes 4718596
  468.6 29.8 %slice-start.6 = ((s8[8388608]{0:T(1024)(128)(4,1)}), s8[4194304]{0:T(1024)(128)(4,1)S(1)}, s32[]{:S(2)}) async-start(s8[8388608]{0:T(1024)(128)(4,1)} %bitcast.872), calls=%async_computation.22 | async-start | bytes 8388608
  469.8 14.8 %copy-start.65 = (bf16[2,256,1024]{2,1,0:T(8,128)(2,1)}, bf16[2,256,1024]{2,1,0:T(8,128)(2,1)S(1)}, u32[]{:S(2)}) copy-start(bf16[2,256,1024]{2,1,0:T(8,128)(2,1)S(1)} %get-tuple-element.197) | copy-start | bytes 3145732
  469.8 14.5 %collective-permute-start.2 = (bf16[256,1024]{1,0:T(8,128)(2,1)S(1)}, bf16[256,1024]{1,0:T(8,128)(2,1)S(1)}, u32[]{:S(2)}, u32[]{:S(2)}) collective-permute-start(bf16[256,1024]{1,0:T(8,128)(2,1)S(1)} %get-tuple-element.198), channel_id=1, source_target_pairs={{16,0},{17,1},{18,2},{19,3},{20,4},{21,5},{22,6},{23,7},{24,8},{25... | collective-permute-start | bytes 1572872 | tf_op jit(solution)/shard_map/ppermute | solution.py:18
  472.4 24.5 %copy-start.113 = (f32[1,11264]{1,0:T(1,128)}, f32[1,11264]{1,0:T(1,128)S(1)}, u32[]{:S(2)}) copy-start(f32[1,11264]{1,0:T(1,128)S(1)} %constant_dynamic-update-slice_fusion.3) | copy-start | bytes 135172
  484.3 17.8 %copy-start.59 = (bf16[256,1024]{1,0:T(8,128)(2,1)}, bf16[256,1024]{1,0:T(8,128)(2,1)S(1)}, u32[]{:S(2)}) copy-start(bf16[256,1024]{1,0:T(8,128)(2,1)S(1)} %collective-permute-done.2) | copy-start | bytes 1572868
  484.5 12.4 copy-start.77
  484.6 13.8 %copy-start.6 = (f32[3,256,1024]{2,1,0:T(8,128)S(1)}, f32[3,256,1024]{2,1,0:T(8,128)}, u32[]{:S(2)}) copy-start(f32[3,256,1024]{2,1,0:T(8,128)} %copy-done.5) | copy-start | bytes 9437188
  484.6 13.7 %copy-start.116 = (f32[1024]{0:T(1024)S(1)}, f32[1024]{0:T(1024)}, u32[]{:S(2)}) copy-start(f32[1024]{0:T(1024)} %get-tuple-element.165) | copy-start | bytes 12292
  484.6 13.7 %copy-start.151 = (f32[256]{0:T(256)S(1)}, f32[256]{0:T(256)}, u32[]{:S(2)}) copy-start(f32[256]{0:T(256)} %broadcast_multiply_fusion.1) | copy-start | bytes 3076
  484.6 13.7 %copy-start.154 = (f32[256]{0:T(256)S(1)}, f32[256]{0:T(256)}, u32[]{:S(2)}) copy-start(f32[256]{0:T(256)} %copy-done.153) | copy-start | bytes 3076
  484.6 13.7 %copy-start.159 = (f32[256]{0:T(256)S(1)}, f32[256]{0:T(256)}, u32[]{:S(2)}) copy-start(f32[256]{0:T(256)} %fusion.411) | copy-start | bytes 3076
  484.6 13.7 %slice-start.7 = ((s8[8388608]{0:T(1024)(128)(4,1)}), s8[4194304]{0:T(1024)(128)(4,1)S(1)}, s32[]{:S(2)}) async-start(s8[8388608]{0:T(1024)(128)(4,1)} %bitcast.872), calls=%async_computation.23 | async-start | bytes 8388608
  501.6 18.7 %copy-start.164 = (f32[256]{0:T(256)}, f32[256]{0:T(256)S(1)}, u32[]{:S(2)}) copy-start(f32[256]{0:T(256)S(1)} %get-tuple-element.150) | copy-start | bytes 3076
  530.2 16.8 %slice-start.2 = ((s8[8388608]{0:T(1024)(128)(4,1)}), s8[4194304]{0:T(1024)(128)(4,1)S(1)}, s32[]{:S(2)}) async-start(s8[8388608]{0:T(1024)(128)(4,1)} %bitcast.868), calls=%async_computation.18 | async-start | bytes 8388608
  533.2 13.8 %copy-start.67 = (bf16[2,256,1024]{2,1,0:T(8,128)(2,1)}, bf16[2,256,1024]{2,1,0:T(8,128)(2,1)S(1)}, u32[]{:S(2)}) copy-start(bf16[2,256,1024]{2,1,0:T(8,128)(2,1)S(1)} %get-tuple-element.191) | copy-start | bytes 3145732
  533.3 13.5 %collective-permute-start.3 = (bf16[256,1024]{1,0:T(8,128)(2,1)S(1)}, bf16[256,1024]{1,0:T(8,128)(2,1)S(1)}, u32[]{:S(2)}, u32[]{:S(2)}) collective-permute-start(bf16[256,1024]{1,0:T(8,128)(2,1)S(1)} %get-tuple-element.192), channel_id=1, source_target_pairs={{16,0},{17,1},{18,2},{19,3},{20,4},{21,5},{22,6},{23,7},{24,8},{25... | collective-permute-start | bytes 1572872 | tf_op jit(solution)/shard_map/ppermute | solution.py:18
  535.8 11.2 slice-start.3
  546.7 16.5 %copy-start.57 = (bf16[256,1024]{1,0:T(8,128)(2,1)}, bf16[256,1024]{1,0:T(8,128)(2,1)S(1)}, u32[]{:S(2)}) copy-start(bf16[256,1024]{1,0:T(8,128)(2,1)S(1)} %collective-permute-done.3) | copy-start | bytes 1572868
  590.1 236.0 %reduce-scatter.21.cloned.1.call-start = ((), (), s32[]{:S(2)}) async-start(), calls=%async_computation.15 | async-start | bytes 6127616
  593.8 234.1 %reduce-scatter.13.cloned.1.call-start = ((), (), s32[]{:S(2)}) async-start(), calls=%async_computation.11 | async-start | bytes 4456448 | tf_op jit(solution)/shard_map/reduce_scatter | solution.py:274
  599.3 345.0 %reduce-scatter.11.cloned.1.call-start = ((), (), s32[]{:S(2)}) async-start(), calls=%async_computation.10 | async-start | bytes 13369344 | tf_op jit(solution)/shard_map/reduce_scatter | solution.py:273
  622.9 503.9 %reduce-scatter.15.cloned.1.call-start = ((), (), s32[]{:S(2)}) async-start(), calls=%async_computation.12 | async-start | bytes 17825792 | tf_op jit(solution)/shard_map/reduce_scatter | solution.py:275
  658.1 650.7 %reduce-scatter.17.cloned.1.call-start = ((), (), s32[]{:S(2)}) async-start(), calls=%async_computation.13 | async-start | bytes 17825792 | tf_op jit(solution)/shard_map/reduce_scatter | solution.py:276
  703.7 13.0 copy-start.101
  703.7 18.7 %copy-start.103 = (bf16[16,256,10]{1,2,0:T(8,128)(2,1)S(1)}, bf16[16,256,10]{1,2,0:T(8,128)(2,1)}, u32[]{:S(2)}) copy-start(bf16[16,256,10]{1,2,0:T(8,128)(2,1)} %copy-done.102) | copy-start | bytes 245764
  713.2 96.1 %copy-start.97 = (f32[10,512]{1,0:T(8,128)S(1)}, f32[10,512]{1,0:T(8,128)}, u32[]{:S(2)}) copy-start(f32[10,512]{1,0:T(8,128)} %copy-done.96) | copy-start | bytes 61444
  713.2 96.7 %copy-start.109 = (bf16[10,1024]{1,0:T(8,128)(2,1)S(1)}, bf16[10,1024]{1,0:T(8,128)(2,1)}, u32[]{:S(2)}) copy-start(bf16[10,1024]{1,0:T(8,128)(2,1)} %param.35) | copy-start | bytes 61444
  784.5 30.7 %copy-start.161 = (f32[256]{0:T(256)S(1)}, f32[256]{0:T(256)}, u32[]{:S(2)}) copy-start(f32[256]{0:T(256)} %copy-done.160) | copy-start | bytes 3076
  784.6 30.7 %copy-start.181 = (f32[256]{0:T(256)S(1)}, f32[256]{0:T(256)}, u32[]{:S(2)}) copy-start(f32[256]{0:T(256)} %get-tuple-element.138) | copy-start | bytes 3076
  784.6 30.7 %copy-start.148 = (f32[256]{0:T(256)S(1)}, f32[256]{0:T(256)}, u32[]{:S(2)}) copy-start(f32[256]{0:T(256)} %broadcast_multiply_fusion) | copy-start | bytes 3076
  784.6 30.7 %copy-start.150 = (f32[256]{0:T(256)S(1)}, f32[256]{0:T(256)}, u32[]{:S(2)}) copy-start(f32[256]{0:T(256)} %fusion.414) | copy-start | bytes 3076
  (145 other events, 692.5 us)
Sparse Core Ops, SparseCore 0:
  10.3 65.0 all-gather.4
  77.6 40.6 all-gather.6
  120.5 73.6 all-gather.8
  196.2 73.1 all-gather.10
  590.3 53.0 reduce-scatter.18
  647.6 80.6 reduce-scatter.20
  733.2 72.4 reduce-scatter.12
  810.4 133.8 reduce-scatter.10
  949.0 177.7 reduce-scatter.14
  1131.2 177.5 reduce-scatter.16
where the time goes:
time: 1330 us; the launch traced here: 1320 us
  waiting for transfers between devices  641 us (48%)
  matrix products  300 us (23%)
  blocking collectives  168 us (13%)
  other arithmetic  106 us (8%)
  local copies, waits for them, and re-layouts  72.2 us (5%)
  between operations  18 us (1%)
    reduce_scatter x1, waiting for transfers between devices, on_device(): lax.psum_scatter(lifted[2], 'dp', scatter_dimension=1, tiled=True)  182 us
    reduce_scatter x1, waiting for transfers between devices, on_device(): lax.psum_scatter(lifted[3], 'dp', scatter_dimension=1, tiled=True)  182 us
    reduce_scatter x1, waiting for transfers between devices, on_device(): lax.psum_scatter(lifted[0], 'dp', scatter_dimension=1, tiled=True)  116 us
    all_gather x1, waiting for transfers between devices, on_device(): lax.all_gather(w_proj, 'dp', axis=1, tiled=True)  67.3 us
    unnamed x1, blocking collectives  64.3 us
    psum x1, blocking collectives, on_device(): prefix_grad = lax.psum(prefix_total, 'dp')  59.7 us
    all_gather x1, waiting for transfers between devices, on_device(): lax.all_gather(w_fc, 'dp', axis=1, tiled=True)  55.1 us
    another operation x23, other arithmetic, on_device(): stacked = jax.tree.map(lambda *items: jnp.stack(items), *stored)  54.7 us
  transfers between devices with their start and end apart: 14, of which 9 were waited for; matrix products, arithmetic and copies ran while one was open for 16% of the time, Pallas kernels for 0%

commit v1 on v0

--- a/solution.py
+++ b/solution.py
@@ -3,9 +3,283 @@
 import jax
 import jax.numpy as jnp
 from jax import lax
+from jax.experimental import pallas as pl
+from jax.experimental.pallas import tpu as pltpu
 from jax.sharding import PartitionSpec as P
 
 HEADS = 16
+MESH = pl.DeviceIdType.MESH
+
+NP = 12
+
+def place():
+    s = lax.axis_index("section"); d = lax.axis_index("dp")
+    return s, d, d // 4, (d // 2) % 2, d % 2
+
+def greet(s, z, y, c, cross=False):
+    bar = pltpu.get_barrier_semaphore()
+    def hello(dev):
+        pl.semaphore_signal(bar, 1, device_id=dev, device_id_type=MESH)
+    hello((s, z*4+y*2+(1-c)))
+    hello((s, z*4+(1-y)*2+c))
+    if cross: hello((1-s, z*4+y*2+c))
+    @pl.when(z > 0)
+    def _(): hello((s, (z-1)*4+y*2+c))
+    @pl.when(z < 3)
+    def _(): hello((s, (z+1)*4+y*2+c))
+    pl.semaphore_wait(bar, 3 + (1 if cross else 0) + ((z + 1) // 2) % 2)
+
+class Gather:
+    def __init__(self, W, ssem, rsem):
+        self.W, self.ssem, self.rsem = W, ssem, rsem
+        self.s, self.d, self.z, self.y, self.c = place()
+    def blk(self, k, d):
+        i = k // 8
+        row = (1-i)*(1024*k+64*d) + i*(8192+256*d+64*(k-8))
+        return self.W.at[pl.ds(pl.multiple_of(row, 64), 64)]
+    def cp(self, k, origin, target, slot):
+        b = self.blk(k, origin)
+        return pltpu.make_async_remote_copy(src_ref=b, dst_ref=b, send_sem=self.ssem.at[k, slot], recv_sem=self.rsem.at[k, origin],
+            device_id=(self.s, target), device_id_type=MESH)
+    def dev(self, z, y, c): return z*4+y*2+c
+    def arrived(self, k, origin): self.cp(k, origin, origin, 0).wait_recv()
+    def to_up(self, k, zo, op):
+        op(self.cp(k, self.dev(zo, self.y, self.c), self.dev(self.z+1, self.y, self.c), zo))
+    def to_down(self, k, zo, op):
+        op(self.cp(k, self.dev(zo, self.y, self.c), self.dev(self.z-1, self.y, self.c), 4+zo))
+    def to_y(self, k, zo, op):
+        op(self.cp(k, self.dev(zo, self.y, self.c), self.dev(self.z, 1-self.y, self.c), 8+zo))
+    def to_c(self, k, zo, yo, op):
+        op(self.cp(k, self.dev(zo, yo, self.c), self.dev(self.z, self.y, 1-self.c), 12+zo*2+yo))
+    def step(self, t, own):
+        z, y, c = self.z, self.y, self.c
+        start = lambda cp: cp.start()
+        @pl.when(t < NP)
+        def _():
+            own(t)
+            self.to_y(t, z, start)
+            @pl.when(z < 3)
+            def _(): self.to_up(t, z, start)
+            @pl.when(z > 0)
+            def _(): self.to_down(t, z, start)
+            self.to_c(t, z, y, start)
+        for q in (1, 2, 3, 4):
+            k = t - q
+            ok = (k >= 0) & (k < NP)
+            if q < 4:
+                @pl.when(ok & (z - q >= 0))
+                def _():
+                    self.arrived(k, self.dev(z-q, y, c))
+                    @pl.when(z < 3)
+                    def _(): self.to_up(k, z-q, start)
+                    self.to_y(k, z-q, start)
+                    self.to_c(k, z-q, y, start)
+                @pl.when(ok & (z + q <= 3))
+                def _():
+                    self.arrived(k, self.dev(z+q, y, c))
+                    @pl.when(z > 0)
+                    def _(): self.to_down(k, z+q, start)
+                    self.to_y(k, z+q, start)
+                    self.to_c(k, z+q, y, start)
+            e = q - 1
+            def side(zo):
+                self.arrived(k, self.dev(zo, 1-y, c))
+                self.to_c(k, zo, 1-y, start)
+            if e == 0:
+                @pl.when(ok)
+                def _(): side(z)
+            else:
+                @pl.when(ok & (z - e >= 0))
+                def _(): side(z-e)
+                @pl.when(ok & (z + e <= 3))
+                def _(): side(z+e)
+    def complete(self, k):
+        for i in range(8):
+            self.arrived(k, 2*i + 1-self.c)
+    def drain(self):
+        fin = lambda cp: cp.wait_send()
+        z, y = self.z, self.y
+        @pl.loop(0, NP)
+        def _(k):
+            for zo in range(4):
+                @pl.when((zo <= z) & (z < 3))
+                def _(): self.to_up(k, zo, fin)
+                @pl.when((zo >= z) & (z > 0))
+                def _(): self.to_down(k, zo, fin)
+                self.to_y(k, zo, fin)
+                for yo in range(2): self.to_c(k, zo, yo, fin)
+
+def own_copies(wq, wo, wf, wp, g, sem):
+    out = []
+    for k in range(NP):
+        if k < 3: src = wq.at[0, :, pl.ds(1024*k, 1024)]
+        elif k == 3: src = wo.at[0]
+        elif k < 8: src = wf.at[0, :, pl.ds(1024*(k-4), 1024)]
+        else: src = wp.at[0, pl.ds(64*(k-8), 64)]
+        out.append(pltpu.make_async_copy(src, g.blk(jnp.int32(k), g.d), sem.at[k]))
+    return out
+
+def ag_kernel(wq, wo, wf, wp, W, own_sem, ssem, rsem):
+    g = Gather(W, ssem, rsem)
+    for cp in own_copies(wq, wo, wf, wp, g, own_sem): cp.start()
+    greet(g.s, g.z, g.y, g.c)
+    def own(t):
+        b = g.blk(t, g.d)
+        pltpu.make_async_copy(b, b, own_sem.at[t]).wait()
+    @pl.loop(0, NP + 6)
+    def _(t):
+        g.step(t, own)
+        @pl.when(t >= 6)
+        def _(): g.complete(t - 6)
+    g.drain()
+
+def all_gather_weights(wq, wo, wf, wp):
+    any_ = pl.BlockSpec(memory_space=pl.ANY)
+    return pl.pallas_call(ag_kernel, out_shape=jax.ShapeDtypeStruct((NP*1024, 1024), jnp.bfloat16), in_specs=[any_]*4, out_specs=any_,
+        scratch_shapes=[pltpu.SemaphoreType.DMA((NP,)), pltpu.SemaphoreType.DMA((NP, 20)), pltpu.SemaphoreType.DMA((NP, 16))],
+        compiler_params=pltpu.CompilerParams(collective_id=0, has_side_effects=True))(wq, wo, wf, wp)
+
+def rs_kernel(G, oq, oo, of, op_, V, RC, RY, RU, RD, T, lsem, osem, cs, cr, ys, yr, us, ur, ds_, dr):
+    s, d, z, y, c = place()
+    loads = [pltpu.make_async_copy(G.at[k], V.at[k], lsem.at[k]) for k in range(NP)]
+    for cp in loads: cp.start()
+    greet(s, z, y, c)
+    F = jnp.float32
+    def C(k): return pltpu.make_async_remote_copy(V.at[k, :, 1-c], RC.at[k], cs.at[k], cr.at[k], device_id=(s, z*4+y*2+1-c), device_id_type=MESH)
+    def Y(k): return pltpu.make_async_remote_copy(V.at[k, pl.ds(4*(1-y), 4), c], RY.at[k], ys.at[k], yr.at[k], device_id=(s, z*4+(1-y)*2+c), device_id_type=MESH)
+    def U(k, n, zz):
+        return pltpu.make_async_remote_copy(V.at[k, pl.ds(4*y+zz+1, n), c], RU.at[k, pl.ds(zz, n)], us.at[k], ur.at[k], device_id=(s, (z+1)*4+y*2+c), device_id_type=MESH)
+    def D(k, n):
+        return pltpu.make_async_remote_copy(V.at[k, pl.ds(4*y, n), c], RD.at[k, pl.ds(0, n)], ds_.at[k], dr.at[k], device_id=(s, (z-1)*4+y*2+c), device_id_type=MESH)
+    def addc(k):
+        @pl.loop(0, 8)
+        def _(i): V[k, i, c] = (V[k, i, c].astype(F) + RC[k, i].astype(F)).astype(jnp.bfloat16)
+    def addy(k):
+        @pl.loop(0, 4)
+        def _(i): V[k, 4*y+i, c] = (V[k, 4*y+i, c].astype(F) + RY[k, i].astype(F)).astype(jnp.bfloat16)
+    def out_cp(k):
+        def q(): return pltpu.make_async_copy(T.at[k], oq.at[0, :, pl.ds(pl.multiple_of(1024*k, 1024), 1024)], osem.at[k])
+        def o(): return pltpu.make_async_copy(T.at[k], oo.at[0], osem.at[k])
+        def f(): return pltpu.make_async_copy(T.at[k], of.at[0, :, pl.ds(pl.multiple_of(1024*(k-4), 1024), 1024)], osem.at[k])
+        def p(): return pltpu.make_async_copy(T.at[k], op_.at[0, pl.ds(pl.multiple_of(64*(k-8), 64), 64)], osem.at[k])
+        return q, o, f, p
+    def each_out(k, act):
+        q, o, f, p = out_cp(k)
+        @pl.when(k < 3)
+        def _(): act(q())
+        @pl.when(k == 3)
+        def _(): act(o())
+        @pl.when((k > 3) & (k < 8))
+        def _(): act(f())
+        @pl.when(k >= 8)
+        def _(): act(p())
+    @pl.loop(0, NP + 6)
+    def _(t):
+        @pl.when(t < NP)
+        def _():
+            k = NP - 1 - t
+            pltpu.make_async_copy(G.at[k], V.at[k], lsem.at[k]).wait()
+            C(k).start()
+        @pl.when((t >= 1) & (t - 1 < NP))
+        def _():
+            k = NP - t
+            C(k).wait_recv(); addc(k); Y(k).start()
+        @pl.when((t >= 2) & (t - 2 < NP))
+        def _():
+            k = NP + 1 - t
+            Y(k).wait_recv(); addy(k)
+            @pl.when(z == 0)
+            def _(): U(k, 3, 0).start()
+            @pl.when(z == 3)
+            def _(): D(k, 3).start()
+        for q in (1, 2, 3):
+            @pl.when((t >= 2 + q) & (t - 2 - q < NP))
+            def _():
+                k = NP + 1 + q - t
+                @pl.when(z == q)
+                def _():
+                    n = 4 - q
+                    U(k, n, q - 1).wait_recv()
+                    for i in range(1, n):
+                        V[k, 4*y+q+i, c] = (V[k, 4*y+q+i, c].astype(F) + RU[k, q-1+i].astype(F)).astype(jnp.bfloat16)
+                    if n > 1: U(k, n-1, q).start()
+                @pl.when(z == 3 - q)
+                def _():
+                    n = 4 - q
+                    D(k, n).wait_recv()
+                    for i in range(0, n-1):
+                        V[k, 4*y+i, c] = (V[k, 4*y+i, c].astype(F) + RD[k, i].astype(F)).astype(jnp.bfloat16)
+                    if n > 1: D(k, n-1).start()
+        @pl.when(t >= 6)
+        def _(): pass
+        @pl.when((t >= 5) & (t - 5 < NP))
+        def _():
+            k = NP + 4 - t
+            T[k] = V[k, 4*y+z, c].astype(F)
+            @pl.when(z > 0)
+            def _(): T[k] += RU[k, z-1].astype(F)
+            @pl.when(z < 3)
+            def _(): T[k] += RD[k, z].astype(F)
+            each_out(k, lambda cp: cp.start())
+    @pl.loop(0, NP)
+    def _(k):
+        each_out(k, lambda cp: cp.wait())
+        C(k).wait_send(); Y(k).wait_send()
+        for q in range(3):
+            @pl.when(z == q)
+            def _(): U(k, 3-q, q).wait_send()
+            @pl.when(z == q + 1)
+            def _(): D(k, q+1).wait_send()
+
+def reduce_scatter_grads(G):
+    any_ = pl.BlockSpec(memory_space=pl.ANY)
+    B = jnp.bfloat16; Dm = pltpu.SemaphoreType.DMA
+    return pl.pallas_call(rs_kernel, out_shape=[jax.ShapeDtypeStruct(sh, jnp.float32) for sh in ((1,64,3072),(1,64,1024),(1,64,4096),(1,256,1024))],
+        in_specs=[any_], out_specs=[any_]*4,
+        scratch_shapes=[pltpu.VMEM((NP,8,2,64,1024),B), pltpu.VMEM((NP,8,64,1024),B), pltpu.VMEM((NP,4,64,1024),B), pltpu.VMEM((NP,3,64,1024),B), pltpu.VMEM((NP,3,64,1024),B),
+          pltpu.VMEM((NP,64,1024),jnp.float32)] + [Dm((NP,))]*10,
+        compiler_params=pltpu.CompilerParams(collective_id=1, has_side_effects=True, vmem_limit_bytes=62<<20))(G)
+
+
+def gather_params(w_qkv, w_attn_out, w_fc, w_proj, gains, biases, fused):
+    small = (
+        lax.all_gather(gains, "dp", axis=2, tiled=True)[0],
+        lax.all_gather(biases, "dp", axis=1, tiled=True)[0],
+    )
+    if not fused:
+        return tuple(
+            lax.all_gather(w, "dp", axis=1, tiled=True)[0] for w in (w_qkv, w_attn_out, w_fc, w_proj)
+        ) + small
+    W = all_gather_weights(w_qkv, w_attn_out, w_fc, w_proj)
+    part = [W[1024 * k : 1024 * (k + 1)] for k in range(8)]
+    return (
+        jnp.concatenate(part[:3], axis=1),
+        part[3],
+        jnp.concatenate(part[4:], axis=1),
+        W[8192:],
+    ) + small
+
+
+def scatter_grads(grads, fused):
+    gq, go, gf, gp, gg, gb = grads
+    small = (
+        lax.psum_scatter(gg[None], "dp", scatter_dimension=2, tiled=True),
+        lax.psum_scatter(gb[None], "dp", scatter_dimension=1, tiled=True),
+    )
+    if not fused:
+        return tuple(
+            lax.psum_scatter(g[None], "dp", scatter_dimension=1, tiled=True) for g in (gq, go, gf, gp)
+        ) + small
+
+    def cut(block):
+        block = block.astype(jnp.bfloat16).reshape(4, 2, 2, 64, 1024)
+        return block.transpose(1, 0, 2, 3, 4).reshape(8, 2, 64, 1024)
+
+    pieces = [cut(gq[:, 1024 * k : 1024 * (k + 1)]) for k in range(3)] + [cut(go)]
+    pieces += [cut(gf[:, 1024 * k : 1024 * (k + 1)]) for k in range(4)]
+    rows = gp.reshape(16, 4, 64, 1024)
+    pieces += [cut(rows[:, j].reshape(1024, 1024)) for j in range(4)]
+    return tuple(reduce_scatter_grads(jnp.stack(pieces))) + small
 
 
 EPS = 1e-05
@@ -179,15 +453,8 @@
     width = tokens.shape[1]
     prefix_len = prefix_embed.shape[0]
     head_dim = width // HEADS
-    gathered = (
-        lax.all_gather(w_qkv, "dp", axis=1, tiled=True),
-        lax.all_gather(w_attn_out, "dp", axis=1, tiled=True),
-        lax.all_gather(w_fc, "dp", axis=1, tiled=True),
-        lax.all_gather(w_proj, "dp", axis=1, tiled=True),
-        lax.all_gather(gains, "dp", axis=2, tiled=True),
-        lax.all_gather(biases, "dp", axis=1, tiled=True),
-    )
-    params = tuple((item[0] for item in gathered))
+    fused = lax.axis_size("dp") == 16
+    params = gather_params(w_qkv, w_attn_out, w_fc, w_proj, gains, biases, fused)
     pre_hidden = jnp.dot(
         prefix_embed, reparam_in, preferred_element_type=jnp.float32
     ) + reparam_in_bias.astype(jnp.float32)
@@ -216,15 +483,7 @@
         stored.append(keep)
         if tick < micro:
             received = passed_along(result_b, "section", 1)
-    regathered = (
-        lax.all_gather(w_qkv, "dp", axis=1, tiled=True),
-        lax.all_gather(w_attn_out, "dp", axis=1, tiled=True),
-        lax.all_gather(w_fc, "dp", axis=1, tiled=True),
-        lax.all_gather(w_proj, "dp", axis=1, tiled=True),
-        lax.all_gather(gains, "dp", axis=2, tiled=True),
-        lax.all_gather(biases, "dp", axis=1, tiled=True),
-    )
-    params_back = tuple((item[0] for item in regathered))
+    params_back = params
     stacked = jax.tree.map(lambda *items: jnp.stack(items), *stored)
     coming = jnp.zeros((row_len, width), jnp.bfloat16)
     in_grads = jnp.zeros((micro, row_len, width), jnp.bfloat16)
@@ -268,15 +527,7 @@
         in_grads = jnp.where(active, in_grads.at[slot].set(d_input_b), in_grads)
         if tick < micro:
             coming = passed_along(d_input_b, "section", -1)
-    lifted = tuple((item[None] for item in grad_total))
-    weight_grads = (
-        lax.psum_scatter(lifted[0], "dp", scatter_dimension=1, tiled=True),
-        lax.psum_scatter(lifted[1], "dp", scatter_dimension=1, tiled=True),
-        lax.psum_scatter(lifted[2], "dp", scatter_dimension=1, tiled=True),
-        lax.psum_scatter(lifted[3], "dp", scatter_dimension=1, tiled=True),
-        lax.psum_scatter(lifted[4], "dp", scatter_dimension=2, tiled=True),
-        lax.psum_scatter(lifted[5], "dp", scatter_dimension=1, tiled=True),
-    )
+    weight_grads = scatter_grads(grad_total, fused)
     prefix_grad = lax.psum(prefix_total, "dp")
     prefix_grad_b = prefix_grad.astype(jnp.bfloat16)
     grad_reparam_out = jnp.einsum(

time: 1330 us -> 1120 us (0.84)
  waiting for transfers between devices: 641 us -> 105 us
  Pallas kernels: 0 us -> 318 us
  local copies, waits for them, and re-layouts: 72.2 us -> 126 us
  matrix products: 300 us -> 272 us
  blocking collectives: 168 us -> 147 us
    reduce_scatter x4 -> x0, waiting for transfers between devices: 481 us -> none  [the longest x1 182 us: on_device(): lax.psum_scatter(lifted[2], 'dp', scatter_dimension=1, tiled=True)]
    pallas_call x0 -> x2, Pallas kernels: none -> 318 us  [the longest x1 168 us: reduce_scatter_grads(): pl.pallas_call(rs_kernel, out_shape=[jax.ShapeDtypeStruct(sh, jnp.float32...]
    all_gather x4 -> x0, waiting for transfers between devices: 122 us -> none  [the longest x1 67.3 us: on_device(): lax.all_gather(w_proj, 'dp', axis=1, tiled=True)]
    unnamed x12 -> x4, waiting for transfers between devices: 2.68 us -> 90.9 us
    unnamed x414 -> x497, local copies, waits for them, and re-layouts: 30.2 us -> 54.8 us
    ppermute x4, waiting for transfers between devices: 35.3 us -> 14.4 us  [passed_along(): return lax.ppermute(shard, axis, pairs)]
    slice x0 -> x4, local copies, waits for them, and re-layouts: none -> 20.8 us  [the longest x1 9.3 us: gather_params(): part = [W[1024 * k:1024 * (k + 1)] for k in range(8)]]
    psum x1, blocking collectives: 24.1 us -> 7.45 us  [on_device(): hidden_grad = lax.psum(hidden_part, 'section')]
  transfers between devices with their start and end apart: 14 -> 6, of which waited for: 9 -> 3; matrix products, arithmetic and copies ran while one was open for 16% -> 12% of each run, Pallas kernels for 0% -> 15%
where the time goes in v1:
time: 1120 us; the launch traced here: 1110 us
  Pallas kernels  318 us (28%)
  matrix products  272 us (24%)
  blocking collectives  147 us (13%)
  local copies, waits for them, and re-layouts  126 us (11%)
  other arithmetic  118 us (11%)
  waiting for transfers between devices  105 us (9%)
  between operations  18.2 us (2%)
    pallas_call x1, Pallas kernels, reduce_scatter_grads(): pl.pallas_call(rs_kernel, out_shape=[jax.ShapeDtypeStruct(sh, jnp.float32...  168 us
    pallas_call x1, Pallas kernels, all_gather_weights(): pl.pallas_call(ag_kernel, out_shape=jax.ShapeDtypeStruct((NP * 1024, 1024...  150 us
    unnamed x4, waiting for transfers between devices  90.9 us
    unnamed x1, blocking collectives  63 us
    psum x1, blocking collectives, on_device(): prefix_grad = lax.psum(prefix_total, 'dp')  58.4 us
    another operation x23, other arithmetic, on_device(): stacked = jax.tree.map(lambda *items: jnp.stack(items), *stored)  58.3 us
    unnamed x497, local copies, waits for them, and re-layouts  54.8 us
    dot_general x3, matrix products, backward_ffn(): jnp.einsum('lf,ld->fd', act_b, dm_b, preferred_element_type=jnp.float32)  28.6 us
  transfers between devices with their start and end apart: 6, of which 3 were waited for; matrix products, arithmetic and copies ran while one was open for 12% of the time, Pallas kernels for 15%

profile of v1, /device:TPU:0, one launch (start us, length us, event | category | flops | bytes accessed | tf_op | source)
XLA Modules:
  0.0 1114.5 jit_solution(13741594299098906781)
XLA Ops:
  10.2 63.0 %all-reduce = bf16[11264]{0:T(1024)(128)(2,1)S(1)} all-reduce(bf16[11264]{0:T(1024)(128)(2,1)S(1)} %dynamic-update-slice.24), channel_id=1, replica_groups=mesh['section'=2,'dp'=16] {'dp'}, use_global_device_ids=true, to_apply=%add | all-reduce | flops 11264 | bytes 45056
  83.1 18.7 %all_gather.6 = bf16[1,2,1024]{1,0,2:T(2,128)(2,1)S(1)} all-gather(bf16[1,2,64]{1,0,2:T(2,128)(2,1)S(1)} %copy.194), channel_id=1, replica_groups=mesh['section'=2,'dp'=16] {'dp'}, dimensions={2}, use_global_device_ids=true | all-gather | bytes 4352 | tf_op jit(solution)/shard_map/all_gather | solution.py:246
  102.3 6.2 slice_reduce_fusion
  108.5 150.0 %shard_map.237 = bf16[12288,1024]{1,0:T(8,128)(2,1)} custom-call(bf16[1,64,3072]{2,1,0:T(8,128)(2,1)} %wq.1, bf16[1,64,1024]{2,1,0:T(8,128)(2,1)} %wo.1, bf16[1,64,4096]{2,1,0:T(8,128)(2,1)} %wf.1, bf16[1,256,1024]{2,1,0:T(8,128)(2,1)} %wp.1), custom_call_target="tpu_custom_call" | custom-call | tf_op jit(solution)/shard_map/pallas_call | solution.py:138
  258.5 9.3 fusion.368
  270.4 3.0 fusion.57
  287.8 4.5 pad_maximum_fusion.2
  296.0 8.3 bitcast_dynamic-update-slice_fusion.5
  305.3 3.4 collective-permute-start
  313.1 4.9 fusion.352
  318.2 5.2 fusion.204
  325.0 3.1 fusion.58
  328.1 3.0 copy.199
  347.1 7.0 fusion.207
  357.7 2.9 fusion.202
  360.6 8.3 collective-permute-done.1
  370.8 3.2 fusion.59
  381.9 2.8 fusion.200
  396.1 10.8 pad_maximum_fusion
  406.9 8.5 convert_reduce_fusion.2
  415.4 7.5 multiply_reduce_fusion.4
  427.6 3.1 convolution_convert_fusion.2
  441.5 3.0 copy.207
  444.5 10.7 pad_maximum_fusion.1
  455.2 3.8 fusion.107
  459.0 3.0 fusion.53
  462.6 3.1 fusion.54
  482.6 4.3 fusion.230
  495.2 5.5 multiply_reduce_fusion.5
  503.9 6.9 fusion.180
  514.9 6.4 fusion.235
  522.9 8.2 fusion.225
  532.7 8.2 fusion.94
  542.2 8.9 convert_reduce_fusion.1
  551.2 3.3 multiply_reduce_fusion.2
  556.6 3.1 convolution_convert_fusion.1
  562.1 3.7 fusion.106
  565.9 3.9 fusion.228
  569.8 3.0 fusion.49
  572.8 3.2 fusion.50
  579.0 9.3 fusion.223
  588.3 9.9 fusion.92
  607.8 6.1 multiply_reduce_fusion.3
  619.7 7.6 fusion.233
  627.3 6.2 collective-permute-done.3
  634.3 8.5 convert_reduce_fusion
  642.9 3.2 multiply_reduce_fusion
  651.2 3.7 fusion.105
  655.0 3.0 fusion.45
  658.0 3.2 fusion.46
  665.9 58.4 %psum.14 = bf16[10,2048]{1,0:T(8,128)(2,1)S(1)} all-reduce(f32[10,2048]{1,0:T(8,128)S(1)} %fusion.270), channel_id=1, replica_groups=mesh['section'=2,'dp'=16] {'dp'}, use_global_device_ids=true, to_apply=%region_83.84 | all-reduce | flops 20480 | bytes 122880 | tf_op jit(solution)/shard_map/psum | solution.py:531
  726.5 7.5 psum.15
  736.8 2.7 fusion.320
  739.6 3.4 add_convert_fusion.3
  752.8 11.1 add_convert_fusion.2
  763.9 3.6 fusion.371
  772.3 10.7 add_convert_fusion.1
  783.0 3.9 fusion.370
  793.3 10.5 add_convert_fusion
  803.8 3.9 fusion.369
  830.2 3.4 copy.265
  833.6 168.3 %shard_map.238 = (f32[1,64,3072]{2,1,0:T(8,128)}, f32[1,64,1024]{2,1,0:T(8,128)}, f32[1,64,4096]{2,1,0:T(8,128)}, f32[1,256,1024]{2,1,0:T(8,128)}) custom-call(bf16[12,8,2,64,1024]{4,3,2,1,0:T(8,128)(2,1)} %bitcast_dynamic-update-slice_fusion.G), custom_call_target="tpu_custom_call" | custom-call | tf_op jit(solution)/shard_map/pallas_call | solution.py:237
  1003.5 3.4 fusion.209
  1008.9 90.8 %reduce-scatter.9.cloned.1.call-done = f32[704,1]{1,0:T(8,128)} async-done(((f32[11264,1]{1,0:T(8,128)}), f32[704,1]{1,0:T(8,128)}) %reduce-scatter.9.cloned.1.call-update) | async-done | bytes 2832
  (730 shorter events, 225.4 us)
Async XLA Ops:
  7.2 71.9 %copy-start = (bf16[1024,512]{1,0:T(8,128)(2,1)S(1)}, bf16[1024,512]{1,0:T(8,128)(2,1)}, u32[]{:S(2)}) copy-start(bf16[1024,512]{1,0:T(8,128)(2,1)} %param.36) | copy-start | bytes 3145732
  7.2 75.2 %copy-start.184 = (s32[2,256]{1,0:T(2,128)S(1)}, s32[2,256]{1,0:T(2,128)}, u32[]{:S(2)}) copy-start(s32[2,256]{1,0:T(2,128)} %param.27) | copy-start | bytes 6148
  7.2 1000.3 %reduce-scatter.7.cloned.1.call-start = ((), (), s32[]{:S(2)}) async-start(), calls=%async_computation.2 | async-start | bytes 557056
  73.2 194.6 %copy-start.162 = (f32[1,3072]{1,0:T(1,128)}, f32[1,3072]{1,0:T(1,128)S(1)}, u32[]{:S(2)}) copy-start(f32[1,3072]{1,0:T(1,128)S(1)} %slice.367) | copy-start | bytes 36868
  74.4 193.4 %copy-start.143 = (f32[1,1024]{1,0:T(1,128)}, f32[1,1024]{1,0:T(1,128)S(1)}, u32[]{:S(2)}) copy-start(f32[1,1024]{1,0:T(1,128)S(1)} %get-tuple-element.242) | copy-start | bytes 12292
  75.6 192.2 %copy-start.168 = (f32[256]{0:T(256)}, f32[256]{0:T(256)S(1)}, u32[]{:S(2)}) copy-start(f32[256]{0:T(256)S(1)} %broadcast_multiply_fusion.11) | copy-start | bytes 3076
  76.9 190.9 %copy-start.197 = (f32[256]{0:T(256)}, f32[256]{0:T(256)S(1)}, u32[]{:S(2)}) copy-start(f32[256]{0:T(256)S(1)} %add_rsqrt_fusion.5) | copy-start | bytes 3076
  108.5 159.4 %copy-start.129 = (f32[1024]{0:T(1024)}, f32[1024]{0:T(1024)S(1)}, u32[]{:S(2)}) copy-start(f32[1024]{0:T(1024)S(1)} %get-tuple-element.174) | copy-start | bytes 12292
  258.5 11.9 %copy-start.25 = (bf16[512,1024]{1,0:T(8,128)(2,1)S(1)}, bf16[512,1024]{1,0:T(8,128)(2,1)}, u32[]{:S(2)}) copy-start(bf16[512,1024]{1,0:T(8,128)(2,1)} %param.26) | copy-start | bytes 3145732
  286.3 9.7 copy-start.31
  305.3 18.1 %collective-permute-start = (bf16[256,1024]{1,0:T(8,128)(2,1)}, bf16[256,1024]{1,0:T(8,128)(2,1)S(1)}, u32[]{:S(2)}, u32[]{:S(2)}) collective-permute-start(bf16[256,1024]{1,0:T(8,128)(2,1)} %get-tuple-element.263), channel_id=1, source_target_pairs={{0,16},{1,17},{2,18},{3,19},{4,20},{5,21},{6,22},{7,23},{8,24},{9,... | collective-permute-start | bytes 1572872 | tf_op jit(solution)/shard_map/ppermute | solution.py:292
  324.5 14.6 %copy-start.18 = (bf16[256,1024]{1,0:T(8,128)(2,1)}, bf16[256,1024]{1,0:T(8,128)(2,1)S(1)}, u32[]{:S(2)}) copy-start(bf16[256,1024]{1,0:T(8,128)(2,1)S(1)} %get-tuple-element.210) | copy-start | bytes 1572868
  341.7 48.4 %copy-start.11 = (f32[256,1024]{1,0:T(8,128)}, f32[256,1024]{1,0:T(8,128)S(1)}, u32[]{:S(2)}) copy-start(f32[256,1024]{1,0:T(8,128)S(1)} %get-tuple-element.269) | copy-start | bytes 3145732
  344.5 9.6 copy-start.16
  355.1 13.8 %copy-start.26 = (bf16[512,1024]{1,0:T(8,128)(2,1)S(1)}, bf16[512,1024]{1,0:T(8,128)(2,1)}, u32[]{:S(2)}) copy-start(bf16[512,1024]{1,0:T(8,128)(2,1)} %param.26) | copy-start | bytes 3145732
  355.1 15.7 %copy-start.72 = (bf16[1024,1024]{1,0:T(8,128)(2,1)S(1)}, bf16[1024,1024]{1,0:T(8,128)(2,1)}, u32[]{:S(2)}) copy-start(bf16[1024,1024]{1,0:T(8,128)(2,1)} %copy-done.70) | copy-start | bytes 6291460
  355.1 15.7 %copy-start.76 = (bf16[1024,1024]{1,0:T(8,128)(2,1)S(1)}, bf16[1024,1024]{1,0:T(8,128)(2,1)}, u32[]{:S(2)}) copy-start(bf16[1024,1024]{1,0:T(8,128)(2,1)} %copy-done.74) | copy-start | bytes 6291460
  355.1 15.7 %copy-start.80 = (bf16[1024,1024]{1,0:T(8,128)(2,1)S(1)}, bf16[1024,1024]{1,0:T(8,128)(2,1)}, u32[]{:S(2)}) copy-start(bf16[1024,1024]{1,0:T(8,128)(2,1)} %copy-done.78) | copy-start | bytes 6291460
  355.1 13.7 %collective-permute-start.1 = (bf16[256,1024]{1,0:T(8,128)(2,1)S(1)}, bf16[256,1024]{1,0:T(8,128)(2,1)S(1)}, u32[]{:S(2)}, u32[]{:S(2)}) collective-permute-start(bf16[256,1024]{1,0:T(8,128)(2,1)S(1)} %get-tuple-element.271), channel_id=1, source_target_pairs={{0,16},{1,17},{2,18},{3,19},{4,20},{5,21},{6,22},{7,23},{8,24},{9,... | collective-permute-start | bytes 1572872 | tf_op jit(solution)/shard_map/ppermute | solution.py:292
  381.9 9.0 slice-start.2
  390.3 32.6 %copy-start.4 = (f32[3,256,1024]{2,1,0:T(8,128)}, f32[3,256,1024]{2,1,0:T(8,128)S(1)}, u32[]{:S(2)}) copy-start(f32[3,256,1024]{2,1,0:T(8,128)S(1)} %pad_maximum_fusion.6) | copy-start | bytes 9437188
  390.6 24.8 %copy-start.188 = (f32[256]{0:T(256)}, f32[256]{0:T(256)S(1)}, u32[]{:S(2)}) copy-start(f32[256]{0:T(256)S(1)} %broadcast_multiply_fusion.3) | copy-start | bytes 3076
  396.1 10.8 copy-start.9
  422.9 55.0 %copy-start.198 = (f32[256]{0:T(256)}, f32[256]{0:T(256)S(1)}, u32[]{:S(2)}) copy-start(f32[256]{0:T(256)S(1)} %get-tuple-element.160) | copy-start | bytes 3076
  444.5 10.7 copy-start.17
  444.5 14.5 %copy-start.56 = (bf16[1,256,3072]{1,2,0:T(8,128)(2,1)S(1)}, bf16[1,256,3072]{1,2,0:T(8,128)(2,1)}, u32[]{:S(2)}) copy-start(bf16[1,256,3072]{1,2,0:T(8,128)(2,1)} %copy.207) | copy-start | bytes 4718596
  500.8 10.1 copy-start.200
  510.8 10.4 copy-start.107
  513.4 28.0 %collective-permute-start.2 = (bf16[256,1024]{1,0:T(8,128)(2,1)S(1)}, bf16[256,1024]{1,0:T(8,128)(2,1)S(1)}, u32[]{:S(2)}, u32[]{:S(2)}) collective-permute-start(bf16[256,1024]{1,0:T(8,128)(2,1)S(1)} %get-tuple-element.206), channel_id=1, source_target_pairs={{16,0},{17,1},{18,2},{19,3},{20,4},{21,5},{22,6},{23,7},{24,8},{25... | collective-permute-start | bytes 1572872 | tf_op jit(solution)/shard_map/ppermute | solution.py:292
  522.9 8.9 copy-start.207
  522.9 8.9 copy-start.37
  522.9 8.9 copy-start.38
  522.9 8.9 copy-start.39
  532.7 8.7 copy-start.8
  532.7 18.4 %slice-start.4 = ((s8[8388608]{0:T(1024)(128)(4,1)}), s8[4194304]{0:T(1024)(128)(4,1)S(1)}, s32[]{:S(2)}) async-start(s8[8388608]{0:T(1024)(128)(4,1)} %bitcast.691), calls=%async_computation.8 | async-start | bytes 8388608
  541.4 13.6 %copy-start.60 = (bf16[256,1024]{1,0:T(8,128)(2,1)}, bf16[256,1024]{1,0:T(8,128)(2,1)S(1)}, u32[]{:S(2)}) copy-start(bf16[256,1024]{1,0:T(8,128)(2,1)S(1)} %collective-permute-done.2) | copy-start | bytes 1572868
  542.2 8.9 copy-start.96
  542.2 9.0 copy-start.5
  542.2 9.0 slice-start.5
  542.2 9.0 copy-start.140
  542.2 9.0 copy-start.186
  542.2 9.0 copy-start.189
  542.2 9.0 copy-start.195
  579.0 9.3 copy-start.97
  588.3 9.9 copy-start.157
  588.3 10.5 copy-start.204
  607.7 8.6 copy-start.35
  607.8 8.6 copy-start.61
  607.8 8.6 copy-start.67
  607.8 8.6 copy-start.181
  613.9 13.4 %copy-start.202 = (f32[256]{0:T(256)}, f32[256]{0:T(256)S(1)}, u32[]{:S(2)}) copy-start(f32[256]{0:T(256)S(1)} %get-tuple-element.157) | copy-start | bytes 3076
  617.6 16.7 %copy-start.68 = (bf16[2,256,1024]{2,1,0:T(8,128)(2,1)}, bf16[2,256,1024]{2,1,0:T(8,128)(2,1)S(1)}, u32[]{:S(2)}) copy-start(bf16[2,256,1024]{2,1,0:T(8,128)(2,1)S(1)} %get-tuple-element.199) | copy-start | bytes 3145732
  617.6 15.8 %collective-permute-start.3 = (bf16[256,1024]{1,0:T(8,128)(2,1)S(1)}, bf16[256,1024]{1,0:T(8,128)(2,1)S(1)}, u32[]{:S(2)}, u32[]{:S(2)}) collective-permute-start(bf16[256,1024]{1,0:T(8,128)(2,1)S(1)} %get-tuple-element.200), channel_id=1, source_target_pairs={{16,0},{17,1},{18,2},{19,3},{20,4},{21,5},{22,6},{23,7},{24,8},{25... | collective-permute-start | bytes 1572872 | tf_op jit(solution)/shard_map/ppermute | solution.py:292
  619.7 23.2 %slice-start.6 = ((s8[8388608]{0:T(1024)(128)(4,1)}), s8[4194304]{0:T(1024)(128)(4,1)S(1)}, s32[]{:S(2)}) async-start(s8[8388608]{0:T(1024)(128)(4,1)} %bitcast.693), calls=%async_computation.10 | async-start | bytes 8388608
  633.5 13.1 %copy-start.59 = (bf16[256,1024]{1,0:T(8,128)(2,1)}, bf16[256,1024]{1,0:T(8,128)(2,1)S(1)}, u32[]{:S(2)}) copy-start(bf16[256,1024]{1,0:T(8,128)(2,1)S(1)} %collective-permute-done.3) | copy-start | bytes 1572868
  634.3 8.6 copy-start.141
  634.3 8.6 copy-start.187
  634.3 8.6 copy-start.196
  662.7 71.2 %copy-start.112 = (f32[10,512]{1,0:T(8,128)S(1)}, f32[10,512]{1,0:T(8,128)}, u32[]{:S(2)}) copy-start(f32[10,512]{1,0:T(8,128)} %copy-done.111) | copy-start | bytes 61444
  664.3 70.2 %copy-start.113 = (bf16[16,256,10]{1,2,0:T(8,128)(2,1)}, bf16[16,256,10]{1,2,0:T(8,128)(2,1)S(1)}, u32[]{:S(2)}) copy-start(bf16[16,256,10]{1,2,0:T(8,128)(2,1)S(1)} %fusion.255) | copy-start | bytes 245764
  726.5 13.1 %copy-start.156 = (f32[4096]{0:T(1024)S(1)}, f32[4096]{0:T(1024)}, u32[]{:S(2)}) copy-start(f32[4096]{0:T(1024)} %get-tuple-element.296) | copy-start | bytes 49156
  752.8 346.9 %reduce-scatter.9.cloned.1.call-start = ((), (), s32[]{:S(2)}) async-start(), calls=%async_computation.3 | async-start | bytes 6127616
  1002.0 101.5 %copy-start.123 = (f32[1,64,1024]{2,1,0:T(8,128)S(1)}, f32[1,64,1024]{2,1,0:T(8,128)}, u32[]{:S(2)}) copy-start(f32[1,64,1024]{2,1,0:T(8,128)} %get-tuple-element.336) | copy-start | bytes 786436
  1006.8 99.6 %copy-start.102 = (f32[1,256,1024]{2,1,0:T(8,128)S(1)}, f32[1,256,1024]{2,1,0:T(8,128)}, u32[]{:S(2)}) copy-start(f32[1,256,1024]{2,1,0:T(8,128)} %get-tuple-element.338) | copy-start | bytes 3145732
  (171 other events, 726.0 us)
Sparse Core Ops, SparseCore 0:
  752.9 53.4 reduce-scatter.6
  1002.1 97.5 reduce-scatter.8

commit v2 on v0

--- a/solution.py
+++ b/solution.py
@@ -3,13 +3,960 @@
 import jax
 import jax.numpy as jnp
 from jax import lax
+from jax.experimental import pallas as pl
+from jax.experimental.pallas import tpu as pltpu
 from jax.sharding import PartitionSpec as P
 
 HEADS = 16
-
-
 EPS = 1e-05
 NEG = -1000000000.0
+MESH = pl.DeviceIdType.MESH
+F32 = jnp.float32
+B16 = jnp.bfloat16
+NP = 12
+
+
+def place():
+    s = lax.axis_index("section"); d = lax.axis_index("dp")
+    return s, d, d // 4, (d // 2) % 2, d % 2
+
+def greet(s, z, y, c, cross=False):
+    bar = pltpu.get_barrier_semaphore()
+    def hello(dev):
+        pl.semaphore_signal(bar, 1, device_id=dev, device_id_type=MESH)
+    hello((s, z*4+y*2+(1-c)))
+    hello((s, z*4+(1-y)*2+c))
+    if cross: hello((1-s, z*4+y*2+c))
+    @pl.when(z > 0)
+    def _(): hello((s, (z-1)*4+y*2+c))
+    @pl.when(z < 3)
+    def _(): hello((s, (z+1)*4+y*2+c))
+    pl.semaphore_wait(bar, 3 + (1 if cross else 0) + ((z + 1) // 2) % 2)
+
+class Gather:
+    def __init__(self, W, ssem, rsem):
+        self.W, self.ssem, self.rsem = W, ssem, rsem
+        self.s, self.d, self.z, self.y, self.c = place()
+    def blk(self, k, d):
+        i = k // 8
+        row = (1-i)*(1024*k+64*d) + i*(8192+256*d+64*(k-8))
+        return self.W.at[pl.ds(pl.multiple_of(row, 64), 64)]
+    def cp(self, k, origin, target, slot):
+        b = self.blk(k, origin)
+        return pltpu.make_async_remote_copy(src_ref=b, dst_ref=b, send_sem=self.ssem.at[k, slot], recv_sem=self.rsem.at[k, origin],
+            device_id=(self.s, target), device_id_type=MESH)
+    def dev(self, z, y, c): return z*4+y*2+c
+    def arrived(self, k, origin): self.cp(k, origin, origin, 0).wait_recv()
+    def to_up(self, k, zo, op):
+        op(self.cp(k, self.dev(zo, self.y, self.c), self.dev(self.z+1, self.y, self.c), zo))
+    def to_down(self, k, zo, op):
+        op(self.cp(k, self.dev(zo, self.y, self.c), self.dev(self.z-1, self.y, self.c), 4+zo))
+    def to_y(self, k, zo, op):
+        op(self.cp(k, self.dev(zo, self.y, self.c), self.dev(self.z, 1-self.y, self.c), 8+zo))
+    def to_c(self, k, zo, yo, op):
+        op(self.cp(k, self.dev(zo, yo, self.c), self.dev(self.z, self.y, 1-self.c), 12+zo*2+yo))
+    def step(self, t, own):
+        z, y, c = self.z, self.y, self.c
+        start = lambda cp: cp.start()
+        @pl.when(t < NP)
+        def _():
+            own(t)
+            self.to_y(t, z, start)
+            @pl.when(z < 3)
+            def _(): self.to_up(t, z, start)
+            @pl.when(z > 0)
+            def _(): self.to_down(t, z, start)
+            self.to_c(t, z, y, start)
+        for q in (1, 2, 3, 4):
+            k = t - q
+            ok = (k >= 0) & (k < NP)
+            if q < 4:
+                @pl.when(ok & (z - q >= 0))
+                def _():
+                    self.arrived(k, self.dev(z-q, y, c))
+                    @pl.when(z < 3)
+                    def _(): self.to_up(k, z-q, start)
+                    self.to_y(k, z-q, start)
+                    self.to_c(k, z-q, y, start)
+                @pl.when(ok & (z + q <= 3))
+                def _():
+                    self.arrived(k, self.dev(z+q, y, c))
+                    @pl.when(z > 0)
+                    def _(): self.to_down(k, z+q, start)
+                    self.to_y(k, z+q, start)
+                    self.to_c(k, z+q, y, start)
+            e = q - 1
+            def side(zo):
+                self.arrived(k, self.dev(zo, 1-y, c))
+                self.to_c(k, zo, 1-y, start)
+            if e == 0:
+                @pl.when(ok)
+                def _(): side(z)
+            else:
+                @pl.when(ok & (z - e >= 0))
+                def _(): side(z-e)
+                @pl.when(ok & (z + e <= 3))
+                def _(): side(z+e)
+    def complete(self, k):
+        for i in range(8):
+            self.arrived(k, 2*i + 1-self.c)
+    def drain(self):
+        fin = lambda cp: cp.wait_send()
+        z, y = self.z, self.y
+        @pl.loop(0, NP)
+        def _(k):
+            for zo in range(4):
+                @pl.when((zo <= z) & (z < 3))
+                def _(): self.to_up(k, zo, fin)
+                @pl.when((zo >= z) & (z > 0))
+                def _(): self.to_down(k, zo, fin)
+                self.to_y(k, zo, fin)
+                for yo in range(2): self.to_c(k, zo, yo, fin)
+
+def own_copies(wq, wo, wf, wp, g, sem):
+    out = []
+    for k in range(NP):
+        if k < 3: src = wq.at[0, :, pl.ds(1024*k, 1024)]
+        elif k == 3: src = wo.at[0]
+        elif k < 8: src = wf.at[0, :, pl.ds(1024*(k-4), 1024)]
+        else: src = wp.at[0, pl.ds(64*(k-8), 64)]
+        out.append(pltpu.make_async_copy(src, g.blk(jnp.int32(k), g.d), sem.at[k]))
+    return out
+
+
+HALF = 256
+STAGES = 12
+GELU_C = math.sqrt(2.0 / math.pi)
+
+
+def dot_nn(a, b):
+    return lax.dot_general(a, b, (((1,), (0,)), ((), ())), preferred_element_type=F32)
+
+
+def dot_nt(a, b):
+    return lax.dot_general(a, b, (((1,), (1,)), ((), ())), preferred_element_type=F32)
+
+
+def dot_tn(a, b):
+    return lax.dot_general(a, b, (((0,), (0,)), ((), ())), preferred_element_type=F32)
+
+
+def whiten(v):
+    mean = jnp.mean(v, axis=-1, keepdims=True)
+    cent = v - mean
+    rstd = lax.rsqrt(jnp.mean(cent * cent, axis=-1, keepdims=True) + EPS)
+    return cent * rstd, rstd
+
+
+def split_heads(pair):
+    left = lax.broadcasted_iota(jnp.int32, pair.shape, 1) < 64
+    zero = jnp.zeros_like(pair)
+    return jnp.concatenate([jnp.where(left, pair, zero), jnp.where(left, zero, pair)], axis=0)
+
+
+def forward_kernel(
+    wq, wo, wf, wp, tokens, small, mask, pkey, pval,
+    W_o, out_o, h_o, a1_o, qkv_o, prob_o, ppre_o, att_o, res_o, a2_o, gp_o, act_o,
+    W, H, A1, QKV, PROB, PPRE, ATT, RES, A2, GP, ACT, OUT, SPRE, ACC,
+    own_sem, ssem, rsem, hsem, xs, xr, save_sem,
+):
+    g = Gather(W, ssem, rsem)
+    s = g.s
+    for cp in own_copies(wq, wo, wf, wp, g, own_sem):
+        cp.start()
+    greet(s, g.z, g.y, g.c, cross=True)
+
+    def tokens_in():
+        return pltpu.make_async_copy(tokens, H, hsem)
+
+    def half(b):
+        return pl.ds(pl.multiple_of(b * HALF, HALF), HALF)
+
+    def cross(b):
+        return pltpu.make_async_remote_copy(
+            OUT.at[half(b)], H.at[half(b)], xs.at[b], xr.at[b], device_id=(1 - s, g.d), device_id_type=MESH
+        )
+
+    @pl.when(s == 0)
+    def _():
+        tokens_in().start()
+
+    def own(t):
+        b = g.blk(t, g.d)
+        pltpu.make_async_copy(b, b, own_sem.at[t]).wait()
+
+    def rows_of(k):
+        return pl.ds(pl.multiple_of(k * 1024, 1024), 1024)
+
+    def saves(b):
+        r = half(b)
+        pairs = [
+            (H.at[r], h_o.at[r]), (A1.at[r], a1_o.at[r]), (QKV.at[:, r], qkv_o.at[:, r]), (PROB.at[pl.ds(2 * b, 2)], prob_o.at[pl.ds(2 * b, 2)]),
+            (PPRE.at[b], ppre_o.at[b]), (ATT.at[r], att_o.at[r]), (RES.at[r], res_o.at[r]), (A2.at[r], a2_o.at[r]),
+            (GP.at[:, r], gp_o.at[:, r]), (ACT.at[:, r], act_o.at[:, r]), (OUT.at[r], out_o.at[r]),
+        ]
+        return [pltpu.make_async_copy(src, dst, save_sem.at[b, i]) for i, (src, dst) in enumerate(pairs)]
+
+    def piece_out(k):
+        return pltpu.make_async_copy(W.at[rows_of(k)], W_o.at[rows_of(k)], save_sem.at[2, k])
+
+    def norm_in(b):
+        @pl.when(s == 0)
+        def _():
+            @pl.when(b == 0)
+            def _():
+                tokens_in().wait()
+
+        @pl.when(s == 1)
+        def _():
+            cross(b).wait_recv()
+
+        xhat, _ = whiten(H[half(b)].astype(F32))
+        A1[half(b)] = (xhat * small[11:12] + small[9:10]).astype(B16)
+        saves(b)[0].start()
+        saves(b)[1].start()
+
+    def project(i, b):
+        v = dot_nn(A1[half(b)], W[rows_of(i)]) + small[pl.ds(i, 1)]
+        v = v.astype(B16)
+        QKV[i, half(b)] = v * jnp.where(i == 0, 0.125, 1.0).astype(B16)
+
+        @pl.when(i == 2)
+        def _():
+            saves(b)[2].start()
+
+    def attend(part, b):
+        @pl.when(part == 0)
+        def _():
+            sp = dot_nt(pkey[...], QKV[0, half(b)])
+            there = lax.broadcasted_iota(jnp.int32, sp.shape, 0) % 16 < 10
+            SPRE[b] = jnp.where(there, sp, NEG)
+
+        @pl.loop(part * 4, part * 4 + 4)
+        def _(p):
+            cols = pl.ds(pl.multiple_of(p * 128, 128), 128)
+            q2, k2, v2 = QKV[0, half(b), cols], QKV[1, half(b), cols], QKV[2, half(b), cols]
+            st = dot_nt(split_heads(k2), q2)
+            probs, pres = [], []
+            for e in range(2):
+                sh = st[e * HALF : (e + 1) * HALF] + mask[b]
+                sp = SPRE[b, pl.ds(pl.multiple_of(p * 32 + e * 16, 16), 16)]
+                top = jnp.maximum(jnp.max(sh, axis=0, keepdims=True), jnp.max(sp, axis=0, keepdims=True))
+                et, ep = jnp.exp(sh - top), jnp.exp(sp - top)
+                inv = 1.0 / (jnp.sum(et, axis=0, keepdims=True) + jnp.sum(ep, axis=0, keepdims=True))
+                probs.append((et * inv).astype(B16))
+                pres.append((ep * inv).astype(B16))
+            pr = jnp.concatenate(probs, axis=0)
+            PROB[2 * b + p // 4, :, pl.ds(pl.multiple_of((p % 4) * HALF, HALF), HALF)] = pr
+            PPRE[b, pl.ds(pl.multiple_of(p * 32, 32), 32)] = jnp.concatenate(pres, axis=0)
+            ACC[half(b), cols] = dot_tn(pr, split_heads(v2))
+
+        @pl.when(part == 1)
+        def _():
+            ATT[half(b)] = (ACC[half(b)] + dot_tn(PPRE[b], pval[...])).astype(B16)
+            saves(b)[3].start()
+            saves(b)[4].start()
+            saves(b)[5].start()
+
+    def mix(b):
+        r = H[half(b)].astype(F32) + (dot_nn(ATT[half(b)], W[rows_of(3)]) + small[3:4])
+        RES[half(b)] = r
+        xhat, _ = whiten(r)
+        A2[half(b)] = (xhat * small[12:13] + small[10:11]).astype(B16)
+        saves(b)[6].start()
+        saves(b)[7].start()
+
+    def widen(j, b):
+        x = dot_nn(A2[half(b)], W[rows_of(4 + j)]) + small[pl.ds(4 + j, 1)]
+        x2 = x * x
+        t = jnp.tanh(GELU_C * (x + 0.044715 * (x2 * x)))
+        ACT[j, half(b)] = (0.5 * x * (1.0 + t)).astype(B16)
+        GP[j, half(b)] = (
+            0.5 * (1.0 + t) + (0.5 * GELU_C) * x * (1.0 - t * t) * (1.0 + (3 * 0.044715) * x2)
+        ).astype(B16)
+
+        @pl.when(j == 3)
+        def _():
+            saves(b)[8].start()
+            saves(b)[9].start()
+
+    def narrow(b):
+        v = RES[half(b)] + small[8:9]
+        for j in range(4):
+            v = v + dot_nn(ACT[j, half(b)], W[rows_of(8 + j)])
+        OUT[half(b)] = v.astype(B16)
+
+        @pl.when(s == 0)
+        def _():
+            cross(b).start()
+
+        saves(b)[10].start()
+
+    @pl.loop(0, NP + 5 + 2 * STAGES)
+    def _(tick):
+        @pl.when(tick < NP + 5)
+        def _():
+            g.step(tick, own)
+
+            @pl.when(tick >= 5)
+            def _():
+                g.complete(tick - 5)
+
+                @pl.when(tick < 13)
+                def _():
+                    piece_out(tick - 5).start()
+
+                @pl.when(tick == NP + 4)
+                def _():
+                    for k in range(8, NP):
+                        piece_out(k).start()
+
+        late = tick - (NP + 5)
+        stage = (1 - s) * (tick - 5) + s * ((late + STAGES) % STAGES - STAGES * (late < 0).astype(jnp.int32))
+        lo = s * (late // STAGES)
+        hi = (1 - s) * 2 + s * (late // STAGES + 1)
+
+        def when(i, body):
+            @pl.when(stage == i)
+            def _():
+                pl.loop(lo, hi)(body)
+
+        when(0, norm_in)
+
+        @pl.when((stage >= 1) & (stage < 4))
+        def _():
+            pl.loop(lo, hi)(lambda b: project(stage - 1, b))
+
+        @pl.when((stage >= 4) & (stage < 6))
+        def _():
+            pl.loop(lo, hi)(lambda b: attend(stage - 4, b))
+
+        when(6, mix)
+
+        @pl.when((stage >= 7) & (stage < 11))
+        def _():
+            pl.loop(lo, hi)(lambda b: widen(stage - 7, b))
+
+        when(11, narrow)
+
+    g.drain()
+
+    @pl.loop(0, NP)
+    def _(k):
+        piece_out(k).wait()
+
+    @pl.loop(0, 2)
+    def _(b):
+        for cp in saves(b):
+            cp.wait()
+
+        @pl.when(s == 0)
+        def _():
+            cross(b).wait_send()
+
+
+def forward_call(wq, wo, wf, wp, tokens, small, mask, pkey, pval):
+    any_, vm = pl.BlockSpec(memory_space=pl.ANY), pl.BlockSpec(memory_space=pltpu.VMEM)
+    n, d = tokens.shape
+    kept = [
+        ((NP * d, d), B16), ((n, d), B16), ((n, d), B16), ((n, d), B16), ((3, n, d), B16), ((4, n, d), B16),
+        ((2, HALF, HALF), B16), ((n, d), B16), ((n, d), F32), ((n, d), B16), ((4, n, d), B16), ((4, n, d), B16),
+    ]
+    dma = pltpu.SemaphoreType.DMA
+    order = [0, 2, 3, 4, 5, 6, 7, 8, 9, 10, 11, 1]
+    scratch = [pltpu.VMEM(*kept[i]) for i in order]
+    return pl.pallas_call(
+        forward_kernel,
+        out_shape=[jax.ShapeDtypeStruct(*k) for k in kept],
+        in_specs=[any_] * 5 + [vm] * 4,
+        out_specs=[any_] * len(kept),
+        scratch_shapes=scratch
+        + [pltpu.VMEM((2, HALF, HALF), F32), pltpu.VMEM((n, d), F32)]
+        + [dma((NP,)), dma((NP, 20)), dma((NP, 16)), dma, dma((2,)), dma((2,)), dma((3, NP))],
+        compiler_params=pltpu.CompilerParams(collective_id=0, has_side_effects=True, vmem_limit_bytes=62 << 20),
+    )(wq, wo, wf, wp, tokens, small, mask, pkey, pval)
+
+SPLIT = 6
+BACK_TICKS = 2 + 2 * SPLIT + NP + 6
+
+
+def unwhiten(grad, xhat, rstd):
+    return rstd * (
+        grad
+        - jnp.mean(grad, axis=-1, keepdims=True)
+        - xhat * jnp.mean(grad * xhat, axis=-1, keepdims=True)
+    )
+
+
+def column_sum(v):
+    return jnp.sum(v.astype(F32), axis=0, keepdims=True)
+
+
+def backward_kernel(
+    W_i, h_i, a1_i, qkv_i, prob_i, ppre_i, att_i, res_i, a2_i, gp_i, act_i, cot, small, pkey, pval,
+    dh_o, oq, oo, of, op_, SG, DKV,
+    WG, H, A1, QKV, BIG, PPRE, ATT, RES, A2, GP, DM, DAT, DATT, DPP, DSP, ACC,
+    RC, RY, RU, RD, T,
+    wsem, lsem, osem, cs, cr, ys, yr, us, ur, ds_, dr, xs, xr, hs,
+):
+    s, d, z, y, c = place()
+    for k in (8, 9, 10, 11, 4, 5, 6, 7, 3, 2, 1, 0):
+        pltpu.make_async_copy(W_i.at[k], WG.at[k], wsem.at[k]).start()
+
+    def loads():
+        pairs = [
+            (gp_i, GP), (a2_i, A2), (res_i, RES), (att_i, ATT), (qkv_i, QKV), (ppre_i, PPRE), (a1_i, A1), (h_i, H),
+            (act_i, BIG), (prob_i, BIG), (cot, DM),
+        ]
+        return [pltpu.make_async_copy(a, b, lsem.at[i]) for i, (a, b) in enumerate(pairs)]
+
+    L_GP, L_A2, L_RES, L_ATT, L_QKV, L_PPRE, L_A1, L_H, L_ACT, L_PROB, L_COT = range(11)
+
+    @pl.when(s == 1)
+    def _():
+        loads()[L_COT].start()
+
+    loads()[L_GP].start()
+    for i in (L_A2, L_RES, L_ATT, L_QKV, L_PPRE):
+        loads()[i].start()
+
+    @pl.when(s == 0)
+    def _():
+        loads()[L_ACT].start()
+
+    @pl.when(s == 1)
+    def _():
+        loads()[L_PROB].start()
+
+    for i in (L_A1, L_H):
+        loads()[i].start()
+    SG[...] = jnp.zeros_like(SG)
+    DKV[...] = jnp.zeros_like(DKV)
+    greet(s, z, y, c, cross=True)
+
+    def weights(ks):
+        for k in ks:
+            pltpu.make_async_copy(W_i.at[k], WG.at[k], wsem.at[k]).wait()
+
+    def half(b):
+        return pl.ds(pl.multiple_of(b * HALF, HALF), HALF)
+
+    def weight(k):
+        return WG[k].reshape(1024, 1024)
+
+    def cross(b):
+        return pltpu.make_async_remote_copy(
+            H.at[half(b)], DM.at[half(b)], xs.at[b], xr.at[b], device_id=(1 - s, d), device_id_type=MESH
+        )
+
+    def dh_out(b):
+        return pltpu.make_async_copy(H.at[half(b)], dh_o.at[half(b)], hs.at[b])
+
+    def ffn_in(b):
+        first = (b == 0)
+
+        @pl.when(first)
+        def _():
+            @pl.when(s == 1)
+            def _():
+                loads()[L_COT].wait()
+
+            weights((8, 9, 10, 11))
+            loads()[L_GP].wait()
+
+        @pl.when(s == 0)
+        def _():
+            cross(b).wait_recv()
+
+        for j in range(4):
+            GP[j, half(b)] = (dot_nt(DM[half(b)], weight(8 + j)) * GP[j, half(b)].astype(F32)).astype(B16)
+
+    def ffn_norm(b):
+        @pl.when(b == 0)
+        def _():
+            weights((4, 5, 6, 7))
+            loads()[L_A2].wait()
+            loads()[L_RES].wait()
+
+        grad = dot_nt(GP[0, half(b)], weight(4))
+        for j in range(1, 4):
+            grad = grad + dot_nt(GP[j, half(b)], weight(4 + j))
+        xhat, rstd = whiten(RES[half(b)])
+        SG[10:11] += jnp.sum(grad, axis=0, keepdims=True)
+        SG[12:13] += jnp.sum(grad * xhat, axis=0, keepdims=True)
+        res = DM[half(b)].astype(F32) + unwhiten(grad * small[12:13], xhat, rstd)
+        RES[half(b)] = res
+        DAT[half(b)] = res.astype(B16)
+
+    def attn_out(b):
+        @pl.when(b == 0)
+        def _():
+            weights((3,))
+            for i in (L_ATT, L_QKV, L_PPRE):
+                loads()[i].wait()
+
+            loads()[L_PROB].wait()
+
+        DATT[...] = dot_nt(DAT[half(b)], weight(3)).astype(B16)
+        DPP[...] = dot_nt(pval[...], DATT[...])
+
+    def attn_back(part, b):
+        @pl.loop(part * 4, part * 4 + 4)
+        def _(p):
+            cols = pl.ds(pl.multiple_of(p * 128, 128), 128)
+            q2, k2, v2 = QKV[0, half(b), cols], QKV[1, half(b), cols], QKV[2, half(b), cols]
+            do2 = DATT[:, cols]
+            pr = BIG[2 * b + p // 4, :, pl.ds(pl.multiple_of((p % 4) * HALF, HALF), HALF)]
+            dp = dot_nt(split_heads(v2), do2)
+            dss, pres = [], []
+            for e in range(2):
+                ph = pr[e * HALF : (e + 1) * HALF].astype(F32)
+                dh = dp[e * HALF : (e + 1) * HALF]
+                at = pl.ds(pl.multiple_of(p * 32 + e * 16, 16), 16)
+                pp, dpp = PPRE[b, at].astype(F32), DPP[at]
+                dot = jnp.sum(ph * dh, axis=0, keepdims=True) + jnp.sum(pp * dpp, axis=0, keepdims=True)
+                dss.append((ph * (dh - dot)).astype(B16))
+                pres.append((pp * (dpp - dot)).astype(B16))
+            ds = jnp.concatenate(dss, axis=0)
+            DSP[pl.ds(pl.multiple_of(p * 32, 32), 32)] = jnp.concatenate(pres, axis=0)
+            left = lax.broadcasted_iota(jnp.int32, (HALF, 128), 1) < 64
+            ACC[:, cols] = dot_tn(ds, split_heads(k2))
+            dk = dot_nn(ds, q2)
+            dv = dot_nn(pr, do2)
+            QKV[1, half(b), cols] = jnp.where(left, dk[:HALF], dk[HALF:]).astype(B16)
+            QKV[2, half(b), cols] = jnp.where(left, dv[:HALF], dv[HALF:]).astype(B16)
+
+        @pl.when(part == 1)
+        def _():
+            def own_rows(full):
+                out = jnp.zeros((16, 1024), F32)
+                head = lax.broadcasted_iota(jnp.int32, (16, 1024), 1) // 64
+                for i in range(16):
+                    out = out + jnp.where(head == i, full[16 * i : 16 * i + 16], 0.0)
+                return out
+
+            DKV[0:16] += own_rows(dot_nn(DSP[...], QKV[0, half(b)]))
+            DKV[16:32] += own_rows(dot_nn(PPRE[b], DATT[...]))
+            QKV[0, half(b)] = ((ACC[...] + dot_tn(DSP[...], pkey[...])) * 0.125).astype(B16)
+
+    def attn_norm(b):
+        @pl.when(b == 0)
+        def _():
+            weights((0, 1, 2))
+            loads()[L_A1].wait()
+            loads()[L_H].wait()
+
+        @pl.when((s == 1) & (b == 1))
+        def _():
+            loads()[L_ACT].start()
+
+        grad = dot_nt(QKV[0, half(b)], weight(0))
+        for i in range(1, 3):
+            grad = grad + dot_nt(QKV[i, half(b)], weight(i))
+        xhat, rstd = whiten(H[half(b)].astype(F32))
+        SG[9:10] += jnp.sum(grad, axis=0, keepdims=True)
+        SG[11:12] += jnp.sum(grad * xhat, axis=0, keepdims=True)
+        H[half(b)] = (RES[half(b)] + unwhiten(grad * small[11:12], xhat, rstd)).astype(B16)
+
+        @pl.when(s == 1)
+        def _():
+            cross(b).start()
+
+        dh_out(b).start()
+
+    def grad_proj():
+        loads()[L_ACT].wait()
+        SG[8:9] = column_sum(DM[...])
+
+        @pl.loop(0, 4)
+        def _(i):
+            for u in range(2):
+                v = dot_tn(BIG[i, :, 512 * u : 512 * (u + 1)], DM[...]).astype(B16).reshape(2, 4, 64, 1024)
+                for j in range(4):
+                    WG[8 + j, i, u] = v[:, j]
+
+        @pl.when(s == 0)
+        def _():
+            loads()[L_PROB].start()
+
+    def put(k, a, v):
+        for i in range(2):
+            part = dot_tn(a[:, 512 * i : 512 * (i + 1)], v[...])
+            WG[k, 2 * i : 2 * i + 2] = part.astype(B16).reshape(2, 2, 2, 64, 1024)
+
+    def grad_fc(j):
+        SG[pl.ds(4 + j, 1)] = column_sum(GP[j])
+        put(4 + j, A2, GP.at[j])
+
+    def grad_out():
+        SG[3:4] = column_sum(DAT[...])
+        put(3, ATT, DAT)
+
+    def grad_qkv(i):
+        SG[pl.ds(i, 1)] = column_sum(QKV[i])
+        put(i, A1, QKV.at[i])
+
+    def held(r):
+        a = r // 4
+        return ((2 - a) * (1 - a) // 2) * (r + 8) + a * (2 - a) * r + (a * (a - 1) // 2) * (11 - r)
+
+    def across_c(r):
+        return pltpu.make_async_remote_copy(
+            WG.at[held(r), :, :, 1 - c], RC.at[r % 4], cs.at[r], cr.at[r],
+            device_id=(s, z * 4 + y * 2 + 1 - c), device_id_type=MESH,
+        )
+
+    def across_y(r):
+        return pltpu.make_async_remote_copy(
+            WG.at[held(r), :, 1 - y, c], RY.at[r % 4], ys.at[r], yr.at[r],
+            device_id=(s, z * 4 + (1 - y) * 2 + c), device_id_type=MESH,
+        )
+
+    def up(r, n, first):
+        return pltpu.make_async_remote_copy(
+            WG.at[held(r), pl.ds(first, n), y, c], RU.at[r % 7, pl.ds(first - 1, n)], us.at[r], ur.at[r],
+            device_id=(s, (z + 1) * 4 + y * 2 + c), device_id_type=MESH,
+        )
+
+    def down(r, n):
+        return pltpu.make_async_remote_copy(
+            WG.at[held(r), pl.ds(0, n), y, c], RD.at[r % 7, pl.ds(0, n)], ds_.at[r], dr.at[r],
+            device_id=(s, (z - 1) * 4 + y * 2 + c), device_id_type=MESH,
+        )
+
+    def each_out(r, act):
+        k = held(r)
+        src = T.at[r % 2]
+
+        @pl.when(r < 4)
+        def _():
+            act(pltpu.make_async_copy(src, op_.at[0, pl.ds(pl.multiple_of(64 * r, 64), 64)], osem.at[r]))
+
+        @pl.when((r >= 4) & (r < 8))
+        def _():
+            act(pltpu.make_async_copy(src, of.at[0, :, pl.ds(pl.multiple_of(1024 * (r - 4), 1024), 1024)], osem.at[r]))
+
+        @pl.when(r == 8)
+        def _():
+            act(pltpu.make_async_copy(src, oo.at[0], osem.at[r]))
+
+        @pl.when(r > 8)
+        def _():
+            act(pltpu.make_async_copy(src, oq.at[0, :, pl.ds(pl.multiple_of(1024 * (11 - r), 1024), 1024)], osem.at[r]))
+
+    def start(cp):
+        cp.start()
+
+    def add(k, i, j, other):
+        WG[k, i, j, c] = (WG[k, i, j, c].astype(F32) + other.astype(F32)).astype(B16)
+
+    def live(r):
+        return (r >= 0) & (r < NP)
+
+    def scatter_step(t):
+        @pl.when(live(t))
+        def _():
+            across_c(t).start()
+
+        @pl.when(live(t - 1))
+        def _():
+            r = t - 1
+            k = held(r)
+            across_c(r).wait_recv()
+
+            @pl.loop(0, 4)
+            def _(i):
+                add(k, i, 1 - y, RC[r % 4, i, 1 - y])
+
+            across_y(r).start()
+
+            @pl.loop(0, 4)
+            def _(i):
+                add(k, i, y, RC[r % 4, i, y])
+
+        @pl.when(live(t - 2))
+        def _():
+            r = t - 2
+            k = held(r)
+            across_y(r).wait_recv()
+
+            @pl.loop(0, 4)
+            def _(i):
+                add(k, i, y, RY[r % 4, i])
+
+            @pl.when(z == 0)
+            def _():
+                up(r, 3, 1).start()
+
+            @pl.when(z == 3)
+            def _():
+                down(r, 3).start()
+
+        for q in (1, 2, 3):
+            n = 4 - q
+
+            @pl.when(live(t - 2 - q))
+            def _():
+                r = t - 2 - q
+                k = held(r)
+
+                @pl.when(z == q)
+                def _():
+                    up_here = pltpu.make_async_remote_copy(
+                        WG.at[k, pl.ds(q, n), y, c], RU.at[r % 7, pl.ds(q - 1, n)], us.at[r], ur.at[r],
+                        device_id=(s, d), device_id_type=MESH,
+                    )
+                    up_here.wait_recv()
+                    for i in range(q + 1, 4):
+                        add(k, i, y, RU[r % 7, i - 1])
+                    if n > 1:
+                        up(r, n - 1, q + 1).start()
+
+                @pl.when(z == 3 - q)
+                def _():
+                    down(r, n).wait_recv()
+                    for i in range(n - 1):
+                        add(k, i, y, RD[r % 7, i])
+                    if n > 1:
+                        down(r, n - 1).start()
+
+        @pl.when(live(t - 5))
+        def _():
+            r = t - 5
+            k = held(r)
+
+            @pl.when(r >= 2)
+            def _():
+                each_out(r - 2, lambda cp: cp.wait())
+
+            T[r % 2] = WG[k, z, y, c].astype(F32)
+
+            @pl.when(z > 0)
+            def _():
+                T[r % 2] += RU[r % 7, z - 1].astype(F32)
+
+            @pl.when(z < 3)
+            def _():
+                T[r % 2] += RD[r % 7, z].astype(F32)
+
+            each_out(r, start)
+
+    @pl.loop(0, BACK_TICKS)
+    def _(tick):
+        turn = tick // SPLIT
+
+        def when(i, at, body):
+            mine = ((s == 0) & (tick == at)) | ((s == 1) & ((tick == i) | (tick == SPLIT + i)))
+
+            @pl.when(mine)
+            def _():
+                pl.loop(s * turn, (1 - s) * 2 + s * (turn + 1))(body)
+
+        @pl.when(((s == 0) & (tick < 2)) | ((s == 1) & ((tick == 0) | (tick == SPLIT))))
+        def _():
+            ffn_in((1 - s) * tick + s * turn)
+
+        when(1, 3, ffn_norm)
+        first = 5 - 3 * s + 3 * (1 - s) * ((tick - 5) // 3) + s * SPLIT * turn
+        b0 = (1 - s) * ((tick - 5) // 3) + s * turn
+        in_turn = ((s == 0) & (tick >= 5) & (tick < 11)) | ((s == 1) & (tick < 2 * SPLIT))
+
+        @pl.when(in_turn & (tick == first))
+        def _():
+            attn_out(b0)
+
+        @pl.when(in_turn & ((tick == first + 1) | (tick == first + 2)))
+        def _():
+            attn_back(tick - first - 1, b0)
+
+        when(5, 11, attn_norm)
+        r = tick - 2 - (2 * SPLIT - 2) * s
+
+        @pl.when(r == 0)
+        def _():
+            grad_proj()
+
+        @pl.when((r >= 4) & (r < 8))
+        def _():
+            grad_fc(r - 4)
+
+        @pl.when(r == 8)
+        def _():
+            grad_out()
+
+        @pl.when((r > 8) & (r < 12))
+        def _():
+            grad_qkv(11 - r)
+
+        scatter_step(r)
+
+    @pl.loop(0, NP)
+    def _(r):
+        @pl.when(r >= NP - 2)
+        def _():
+            each_out(r, lambda cp: cp.wait())
+
+        across_c(r).wait_send()
+        across_y(r).wait_send()
+        for q in range(3):
+
+            @pl.when(z == q)
+            def _():
+                up(r, 3 - q, q + 1).wait_send()
+
+            @pl.when(z == q + 1)
+            def _():
+                down(r, q + 1).wait_send()
+
+    @pl.loop(0, 2)
+    def _(b):
+        dh_out(b).wait()
+
+        @pl.when(s == 1)
+        def _():
+            cross(b).wait_send()
+
+
+def backward_call(kept, cot, small, pkey, pval):
+    W, h, a1, qkv, prob, ppre, att, res, a2, gp, act = kept
+    any_, vm = pl.BlockSpec(memory_space=pl.ANY), pl.BlockSpec(memory_space=pltpu.VMEM)
+    n, d = h.shape
+    dma = pltpu.SemaphoreType.DMA
+    wide = (4, 2, 2, 64, d)
+    prob = prob.reshape(4, 512, 1024)
+    outs = [((n, d), B16), ((1, 64, 3 * d), F32), ((1, 64, d), F32), ((1, 64, 4 * d), F32), ((1, 256, d), F32), ((16, d), F32), ((32, d), F32)]
+    scratch = [
+        ((NP,) + wide, B16), ((n, d), B16), ((n, d), B16), ((3, n, d), B16), ((4, n, d), B16), ((2, HALF, HALF), B16), ((n, d), B16),
+        ((n, d), F32), ((n, d), B16), ((4, n, d), B16), ((n, d), B16), ((n, d), B16), ((HALF, d), B16), ((HALF, HALF), F32),
+        ((HALF, HALF), B16), ((HALF, d), F32),
+        ((4, 4, 2, 64, d), B16), ((4, 4, 64, d), B16), ((7, 3, 64, d), B16), ((7, 3, 64, d), B16), ((2, 64, d), F32),
+    ]
+    return pl.pallas_call(
+        backward_kernel,
+        out_shape=[jax.ShapeDtypeStruct(*o) for o in outs],
+        in_specs=[any_] * 12 + [vm] * 3,
+        out_specs=[any_] * 5 + [vm] * 2,
+        scratch_shapes=[pltpu.VMEM(*v) for v in scratch] + [dma((NP,))] * 11 + [dma((2,))] * 3,
+        compiler_params=pltpu.CompilerParams(collective_id=1, has_side_effects=True, vmem_limit_bytes=64 << 20),
+    )(W.reshape((NP,) + wide), h, a1, qkv, prob, ppre, att, res, a2, gp, act, cot, small, pkey, pval)
+
+def swap_kernel(src, dst, ss, rs):
+    s, d = lax.axis_index("section"), lax.axis_index("dp")
+    bar = pltpu.get_barrier_semaphore()
+    for i in range(1, 16):
+        pl.semaphore_signal(bar, 1, device_id=(s, (d + i) % 16), device_id_type=MESH)
+    dst[d] = src[d]
+    pl.semaphore_wait(bar, 15)
+
+    def cp(i, frm):
+        return pltpu.make_async_remote_copy(
+            src.at[(d + i) % 16], dst.at[frm], ss.at[i], rs.at[i], device_id=(s, (d + i) % 16), device_id_type=MESH
+        )
+
+    for i in range(1, 16):
+        cp(i, d).start()
+    for i in range(1, 16):
+        cp(i, (d + 16 - i) % 16).wait()
+
+
+def swap_blocks(x, cid):
+    vm = pl.BlockSpec(memory_space=pltpu.VMEM)
+    return pl.pallas_call(
+        swap_kernel,
+        out_shape=jax.ShapeDtypeStruct(x.shape, x.dtype),
+        in_specs=[vm],
+        out_specs=vm,
+        scratch_shapes=[pltpu.SemaphoreType.DMA((16,))] * 2,
+        compiler_params=pltpu.CompilerParams(collective_id=cid, has_side_effects=True),
+    )(x)
+
+
+def gather_small(gains, biases):
+    own = jnp.concatenate([biases.reshape(704), gains.reshape(128)])
+    own = jnp.pad(own, (0, 2048 - 832)).reshape(1, 16, 128)
+    got = swap_blocks(jnp.broadcast_to(own, (16, 16, 128)), 2).reshape(16, 2048).astype(F32)
+    bias = got[:, :704].reshape(11, 1024)
+    gain = got[:, 704:832].reshape(16, 2, 64).transpose(1, 0, 2).reshape(2, 1024)
+    return jnp.concatenate([bias, gain, jnp.zeros((3, 1024), F32)])
+
+
+def prefix_blocks(rows):
+    rows = jnp.pad(rows, ((0, 6), (0, 0)))
+    big = jnp.broadcast_to(rows[None], (16, 16, 1024)).reshape(256, 1024)
+    head = lax.broadcasted_iota(jnp.int32, (256, 1024), 0) // 16
+    return jnp.where(head == lax.broadcasted_iota(jnp.int32, (256, 1024), 1) // 64, big, jnp.zeros_like(big))
+
+
+def row_mask(segs):
+    at = jnp.arange(segs.shape[1])
+    ok = (segs[:, :, None] == segs[:, None, :]) & (at[:, None] <= at[None, :])
+    return jnp.where(ok, 0.0, NEG).astype(F32)
+
+def small_sums(sums, dkv):
+    bias = sums[:11].reshape(16, 704)
+    gain = sums[11:13].reshape(2, 16, 64).transpose(1, 0, 2).reshape(16, 128)
+    both = jnp.concatenate([dkv[:10], dkv[16:26]], axis=1)
+    pref = both.reshape(10, 16, 128).transpose(1, 0, 2).reshape(16, 1280)
+    parts = jnp.concatenate([bias, gain, pref], axis=1)
+    parts = jnp.pad(parts, ((0, 0), (0, 3072 - 2112))).reshape(16, 24, 128)
+    mine = jnp.sum(swap_blocks(parts, 3), axis=0).reshape(3072)
+    pref = mine[832:2112].reshape(10, 128).astype(B16)
+    pref = jnp.pad(pref, ((0, 6), (0, 0)))
+    got = swap_blocks(jnp.broadcast_to(pref[None], (16, 16, 128)), 4)
+    got = got[:, :10].transpose(1, 0, 2).reshape(10, 2048)
+    return mine[:704].reshape(1, 704), mine[704:832].reshape(1, 2, 64), got
+
+
+def on_device(
+    tokens,
+    segment_ids,
+    cotangent,
+    w_qkv,
+    w_attn_out,
+    w_fc,
+    w_proj,
+    gains,
+    biases,
+    prefix_embed,
+    reparam_in,
+    reparam_in_bias,
+    reparam_out,
+    reparam_out_bias,
+):
+    pre_hidden = jnp.dot(prefix_embed, reparam_in, preferred_element_type=F32) + reparam_in_bias.astype(F32)
+    hidden = jnp.tanh(pre_hidden)
+    hidden_b = hidden.astype(B16)
+    prefix_kv = (
+        jnp.dot(hidden_b, reparam_out, preferred_element_type=F32) + reparam_out_bias.astype(F32)
+    ).astype(B16)
+    pkey, pval = prefix_blocks(prefix_kv[:, :1024]), prefix_blocks(prefix_kv[:, 1024:])
+    small = gather_small(gains, biases)
+    kept = forward_call(w_qkv, w_attn_out, w_fc, w_proj, tokens, small, row_mask(segment_ids), pkey, pval)
+    dh, gq, go, gf, gp, sums, dkv = backward_call(kept[:1] + kept[2:], cotangent, small, pkey, pval)
+    grad_biases, grad_gains, prefix_grad_b = small_sums(sums, dkv)
+    grad_reparam_out = jnp.einsum("pr,pc->rc", hidden_b, prefix_grad_b, preferred_element_type=F32)
+    grad_reparam_out_bias = jnp.sum(prefix_grad_b.astype(F32), axis=0)
+    hidden_part = jnp.dot(prefix_grad_b, reparam_out.T, preferred_element_type=F32)
+    hidden_grad = hidden_part + lax.ppermute(hidden_part, "section", [(0, 1), (1, 0)])
+    dpre_hidden_b = (hidden_grad * (1.0 - hidden * hidden)).astype(B16)
+    grad_reparam_in = jnp.einsum("pd,pr->dr", prefix_embed, dpre_hidden_b, preferred_element_type=F32)
+    grad_reparam_in_bias = jnp.sum(dpre_hidden_b.astype(F32), axis=0)
+    grad_prefix_embed = jnp.dot(dpre_hidden_b, reparam_in.T, preferred_element_type=F32)
+    return (
+        kept[1][None],
+        dh[None],
+        gq,
+        go,
+        gf,
+        gp,
+        grad_gains,
+        grad_biases,
+        grad_prefix_embed,
+        grad_reparam_in,
+        grad_reparam_in_bias,
+        grad_reparam_out,
+        grad_reparam_out_bias,
+    )
 
 
 def passed_along(shard, axis, by):
@@ -158,7 +1105,7 @@
     return (attn_mats[0], attn_mats[1], ffn_mats[0], ffn_mats[1], grad_gains, grad_bias)
 
 
-def on_device(
+def on_device_general(
     tokens,
     segment_ids,
     cotangent,
@@ -312,7 +1259,7 @@
 
 def solution(mesh):
     return jax.shard_map(
-        on_device,
+        on_device if mesh.shape["dp"] == 16 else on_device_general,
         mesh=mesh,
         in_specs=(
             P("dp", None),

time: 1330 us -> 483 us (0.36)
  waiting for transfers between devices: 641 us -> 0.01 us
  Pallas kernels: 0 us -> 448 us
  matrix products: 300 us -> 8.33 us
  blocking collectives: 168 us -> 0 us
  other arithmetic: 106 us -> 7.26 us
  local copies, waits for them, and re-layouts: 72.2 us -> 18 us
  between operations: 18 us -> 0.95 us
    reduce_scatter x4 -> x0, waiting for transfers between devices: 481 us -> none  [the longest x1 182 us: on_device(): lax.psum_scatter(lifted[2], 'dp', scatter_dimension=1, tiled=True)]
    pallas_call x0 -> x5, Pallas kernels: none -> 448 us  [the longest x1 247 us: backward_call(): pl.pallas_call(backward_kernel, out_shape=[jax.ShapeDtypeStruct(*o) for o...]
    dot_general x77 -> x5, matrix products: 298 us -> 7.88 us  [the longest x1 2.74 us: on_device(): jnp.einsum('pr,pc->rc', hidden_b, prefix_grad_b, preferred_element_type=F32)]
    all_gather x4 -> x0, waiting for transfers between devices: 122 us -> none  [the longest x1 67.3 us: on_device(): lax.all_gather(w_proj, 'dp', axis=1, tiled=True)]
    psum x2 -> x0, blocking collectives: 83.8 us -> none  [the longest x1 59.7 us: on_device(): prefix_grad = lax.psum(prefix_total, 'dp')]
    unnamed x1 -> x0, blocking collectives: 64.3 us -> none
    another operation x24 -> x0, other arithmetic: 55.5 us -> none  [the longest x23 54.7 us: on_device(): stacked = jax.tree.map(lambda *items: jnp.stack(items), *stored)]
    ppermute x4 -> x1, waiting for transfers between devices: 35.3 us -> 0.01 us  [on_device(): lax.ppermute(hidden_part, 'section', [(0, 1), (1, 0)])]
  transfers between devices with their start and end apart: 14 -> 1, of which waited for: 9 -> 0; matrix products, arithmetic and copies ran while one was open for 16% -> 1% of each run, Pallas kernels for 0% -> 0%
where the time goes in v2:
time: 483 us; the launch traced here: 482 us
  Pallas kernels  448 us (93%)
  local copies, waits for them, and re-layouts  18 us (4%)
  matrix products  8.33 us (2%)
  other arithmetic  7.26 us (2%)
    pallas_call x1, Pallas kernels, backward_call(): pl.pallas_call(backward_kernel, out_shape=[jax.ShapeDtypeStruct(*o) for o...  247 us
    pallas_call x1, Pallas kernels, forward_call(): pl.pallas_call(forward_kernel, out_shape=[jax.ShapeDtypeStruct(*k) for k...  172 us
    pallas_call x3, Pallas kernels, swap_blocks(): pl.pallas_call(swap_kernel, out_shape=jax.ShapeDtypeStruct(x.shape, x.dty...  28.5 us
    unnamed x40, local copies, waits for them, and re-layouts  10.2 us
  transfers between devices with their start and end apart: 1, of which 0 were waited for; matrix products, arithmetic and copies ran while one was open for 1% of the time, Pallas kernels for 0%

profile of v2, /device:TPU:0, one launch (start us, length us, event | category | flops | bytes accessed | tf_op | source)
XLA Modules:
  0.0 482.2 jit_solution(594015017566035852)
XLA Ops:
  0.7 0.7 reshape.108
  1.4 0.7 reduce.1
  2.1 0.1 fusion.12
  2.2 0.6 broadcast_in_dim.25.src
  2.9 10.3 %shard_map.237 = bf16[16,16,128]{2,1,0:T(8,128)(2,1)} custom-call(bf16[16,16,128]{2,1,0:T(8,128)(2,1)} %broadcast_in_dim.25.src), custom_call_target="tpu_custom_call" | custom-call | tf_op jit(solution)/shard_map/pallas_call | solution.py:864
  13.2 0.0 copy-start.12
  13.2 0.9 copy.42
  14.1 0.1 slice.50
  14.2 0.7 convert_element_type.43
  14.9 0.7 convert_element_type.45
  15.5 1.5 fusion.1
  17.0 0.0 copy-start.8
  17.1 0.6 copy-done.8
  17.7 2.0 fusion
  19.7 0.1 reshape.110
  19.8 0.1 reshape.111
  19.9 0.1 reshape.109
  20.0 0.1 pad.28.clone
  20.0 0.0 copy-done.12
  20.0 1.0 and_select_fusion.mask
  21.0 0.7 maximum_maximum_fusion.small
  21.7 1.2 fusion.2
  22.9 172.1 %shard_map.238 = (bf16[12288,1024]{1,0:T(8,128)(2,1)}, bf16[512,1024]{1,0:T(8,128)(2,1)}, bf16[512,1024]{1,0:T(8,128)(2,1)}, bf16[512,1024]{1,0:T(8,128)(2,1)}, ...) custom-call(bf16[1,64,3072]{2,1,0:T(8,128)(2,1)} %wq.1, ...), custom_call_target="tpu_custom_call" | custom-call | tf_op jit(solution)/shard_map/pallas_call | solution.py:368
  195.0 247.0 %shard_map.239 = (bf16[512,1024]{1,0:T(8,128)(2,1)}, f32[1,64,3072]{2,1,0:T(8,128)}, f32[1,64,1024]{2,1,0:T(8,128)}, f32[1,64,4096]{2,1,0:T(8,128)}, f32[1,256,1...) custom-call(bf16[12,4,2,2,64,1024]{5,4,3,2,1,0:T(8,128)(2,1)} %bitcast.51, ...), custom_call_target="tpu_custom_call" | custom-call | tf_op jit(solution)/shard_map/pallas_call | solution.py:834
  442.0 0.0 copy-start
  442.1 0.9 slice.42
  443.0 0.1 reshape.116
  443.1 0.1 reshape.117
  443.1 0.9 reshape.115
  444.1 0.9 fusion.15
  445.1 0.1 concatenate.15
  445.2 0.0 copy-start.9
  445.2 0.7 copy.38
  446.0 8.6 %shard_map.240 = f32[16,24,128]{2,1,0:T(8,128)} custom-call(f32[16,24,128]{2,1,0:T(8,128)} %bitcast.54), custom_call_target="tpu_custom_call" | custom-call | tf_op jit(solution)/shard_map/pallas_call | solution.py:864
  454.6 1.0 reduce_sum.29
  455.5 0.1 fusion.13
  455.6 0.6 broadcast_in_dim.58.src
  456.2 9.6 %shard_map.241 = bf16[16,16,128]{2,1,0:T(8,128)(2,1)} custom-call(bf16[16,16,128]{2,1,0:T(8,128)(2,1)} %broadcast_in_dim.58.src), custom_call_target="tpu_custom_call" | custom-call | tf_op jit(solution)/shard_map/pallas_call | solution.py:864
  465.8 0.8 slice_bitcast_fusion
  466.7 0.0 copy-done
  466.7 0.6 fusion.17
  467.4 0.0 copy-start.11
  467.4 0.1 collective-permute-start
  467.5 0.0 copy-done.9
  467.5 2.7 fusion.6
  470.2 0.0 copy-done.7
  470.2 0.6 convert_reduce_fusion
  470.8 0.1 slice.53
  470.9 0.6 reshape.122
  471.6 0.6 reshape.123
  472.1 0.0 collective-permute-done
  472.1 0.6 convert_reduce_fusion.1
  472.7 1.0 fusion.18
  473.8 0.0 copy-done.11
  473.8 0.5 convolution_bitcast_fusion
  474.2 1.8 copy.34
  476.1 0.0 copy-done.3
  476.1 1.0 copy.50
  477.0 0.6 copy-done.5
  477.7 1.0 copy.51
  478.6 0.9 copy.52
  479.5 0.7 copy.53
  480.2 1.0 copy.54
  481.2 1.0 copy.55
  (36 shorter events, 0.3 us)
Async XLA Ops:
  13.2 6.9 %copy-start.12 = (s32[2,256]{1,0:T(2,128)S(1)}, s32[2,256]{1,0:T(2,128)}, u32[]{:S(2)}) copy-start(s32[2,256]{1,0:T(2,128)} %param.15) | copy-start | bytes 6148
  17.0 0.6 copy-start.8
  442.0 24.7 %copy-start = (bf16[512,2048]{1,0:T(8,128)(2,1)S(1)}, bf16[512,2048]{1,0:T(8,128)(2,1)}, u32[]{:S(2)}) copy-start(bf16[512,2048]{1,0:T(8,128)(2,1)} %param.26) | copy-start | bytes 6291460
  445.2 22.2 %copy-start.9 = (f32[10,512]{1,0:T(8,128)S(1)}, f32[10,512]{1,0:T(8,128)}, u32[]{:S(2)}) copy-start(f32[10,512]{1,0:T(8,128)} %copy-done.8) | copy-start | bytes 61444
  467.4 2.9 copy-start.7
  467.4 5.4 %copy-start.1 = (bf16[1024,512]{1,0:T(8,128)(2,1)S(1)}, bf16[1024,512]{1,0:T(8,128)(2,1)}, u32[]{:S(2)}) copy-start(bf16[1024,512]{1,0:T(8,128)(2,1)} %param.24) | copy-start | bytes 3145732
  467.4 6.4 %copy-start.11 = (bf16[10,1024]{1,0:T(8,128)(2,1)S(1)}, bf16[10,1024]{1,0:T(8,128)(2,1)}, u32[]{:S(2)}) copy-start(bf16[10,1024]{1,0:T(8,128)(2,1)} %param.23) | copy-start | bytes 61444
  467.4 4.8 collective-permute-start
  474.2 1.8 copy-start.3
  476.0 1.6 copy-start.5
  476.1 2.6 copy-start.6
  477.7 1.9 copy-start.10
  477.7 2.6 copy-start.4
  478.6 2.6 copy-start.2

commit v3 on v2

--- a/solution.py
+++ b/solution.py
@@ -20,18 +20,37 @@
     s = lax.axis_index("section"); d = lax.axis_index("dp")
     return s, d, d // 4, (d // 2) % 2, d % 2
 
-def greet(s, z, y, c, cross=False):
+def greet(s, d):
     bar = pltpu.get_barrier_semaphore()
-    def hello(dev):
-        pl.semaphore_signal(bar, 1, device_id=dev, device_id_type=MESH)
-    hello((s, z*4+y*2+(1-c)))
-    hello((s, z*4+(1-y)*2+c))
-    if cross: hello((1-s, z*4+y*2+c))
-    @pl.when(z > 0)
-    def _(): hello((s, (z-1)*4+y*2+c))
-    @pl.when(z < 3)
-    def _(): hello((s, (z+1)*4+y*2+c))
-    pl.semaphore_wait(bar, 3 + (1 if cross else 0) + ((z + 1) // 2) % 2)
+    for i in range(1, 16):
+        pl.semaphore_signal(bar, 1, device_id=(s, (d + i) % 16), device_id_type=MESH)
+    pl.semaphore_signal(bar, 1, device_id=(1 - s, d), device_id_type=MESH)
+    pl.semaphore_wait(bar, 16)
+
+
+def to_all(src, dst, ss, rs):
+    s, d = lax.axis_index("section"), lax.axis_index("dp")
+
+    def cp(i, frm):
+        to = (d + i) % 16
+        return pltpu.make_async_remote_copy(
+            src(to), dst.at[frm], ss.at[i], rs.at[i], device_id=(s, to), device_id_type=MESH
+        )
+
+    def start():
+        for i in range(1, 16):
+            cp(i, d).start()
+
+    def arrive():
+        for i in range(1, 16):
+            cp(i, (d + 16 - i) % 16).wait_recv()
+
+    def finish():
+        for i in range(1, 16):
+            cp(i, d).wait_send()
+
+    return start, arrive, finish
+
 
 class Gather:
     def __init__(self, W, ssem, rsem):
@@ -155,16 +174,59 @@
 
 
 def forward_kernel(
-    wq, wo, wf, wp, tokens, small, mask, pkey, pval,
-    W_o, out_o, h_o, a1_o, qkv_o, prob_o, ppre_o, att_o, res_o, a2_o, gp_o, act_o,
-    W, H, A1, QKV, PROB, PPRE, ATT, RES, A2, GP, ACT, OUT, SPRE, ACC,
-    own_sem, ssem, rsem, hsem, xs, xr, save_sem,
+    wq, wo, wf, wp, tokens, segs, pack, aux, r_in, r_out,
+    W_o, out_o, h_o, a1_o, qkv_o, prob_o, ppre_o, att_o, res_o, a2_o, gp_o, act_o, small_o, pkey_o, pval_o, hid_o,
+    W, H, A1, QKV, PROB, PPRE, ATT, RES, A2, GP, ACT, OUT, SPRE, ACC, small, pkey, pval, hid, mask, PACKS, ROWS,
+    own_sem, ssem, rsem, hsem, xs, xr, save_sem, ps, pr, psem,
 ):
     g = Gather(W, ssem, rsem)
     s = g.s
     for cp in own_copies(wq, wo, wf, wp, g, own_sem):
         cp.start()
-    greet(s, g.z, g.y, g.c, cross=True)
+    r_in_parts = [pltpu.make_async_copy(r_in.at[pl.ds(512 * i, 512)], ACT.at[2, :, pl.ds(512 * i, 512)], psem.at[i]) for i in range(2)]
+    r_out_parts = [pltpu.make_async_copy(r_out.at[:, pl.ds(1024 * i, 1024)], ACT.at[i], psem.at[2 + i]) for i in range(2)]
+    for cp in r_in_parts + r_out_parts:
+        cp.start()
+    greet(s, g.d)
+    send_packs, packs_in, packs_out = to_all(lambda to: pack, PACKS, ps, pr)
+
+    def prep_saves():
+        pairs = [(small, small_o), (pkey, pkey_o), (pval, pval_o), (hid, hid_o)]
+        return [pltpu.make_async_copy(a, b, psem.at[4 + i]) for i, (a, b) in enumerate(pairs)]
+
+    def prepare():
+        for cp in r_in_parts + r_out_parts:
+            cp.wait()
+        ph = dot_nn(aux[:, :512], ACT[2, :, :512]) + dot_nn(aux[:, 512:], ACT[2, :, 512:])
+        hid[...] = jnp.tanh(ph + aux[10:11, :512].astype(F32))
+        hb = hid[...].astype(B16)
+        head = lax.broadcasted_iota(jnp.int32, (16, 1024), 1) // 64
+        for i, big in enumerate((pkey, pval)):
+            kv = (dot_nn(hb, ACT[i]) + aux[11 + i : 12 + i].astype(F32)).astype(B16)
+            for h in range(16):
+                big[16 * h : 16 * h + 16] = jnp.where(head == h, kv, jnp.zeros_like(kv))
+        key = lax.broadcasted_iota(jnp.int32, (HALF, HALF), 0)
+        query = lax.broadcasted_iota(jnp.int32, (HALF, HALF), 1)
+        for b in range(2):
+            by_query = jnp.broadcast_to(segs[b : b + 1].astype(F32), (HALF, HALF))
+            ok = (by_query.T == by_query) & (key <= query)
+            mask[b] = jnp.where(ok, 0.0, NEG)
+        packs_in()
+        ROWS[...] = PACKS[...].astype(F32)
+        left = lax.broadcasted_iota(jnp.int32, (1, 128), 1) < 64
+        small[...] = jnp.zeros_like(small)
+        for n in range(104):
+            row, at = n // 8, 128 * (n % 8)
+            if row < 11:
+                (d0, r0), (d1, r1) = divmod(2 * n, 11), divmod(2 * n + 1, 11)
+            else:
+                (d0, r0), (d1, r1) = (2 * (n % 8), row), (2 * (n % 8) + 1, row)
+            small[row : row + 1, at : at + 128] = jnp.where(left, ROWS[d0, r0 : r0 + 1], ROWS[d1, r1 : r1 + 1])
+        for cp in prep_saves():
+            cp.start()
+
+    send_packs()
+    PACKS[g.d] = pack[...]
 
     def tokens_in():
         return pltpu.make_async_copy(tokens, H, hsem)
@@ -298,6 +360,10 @@
         def _():
             g.step(tick, own)
 
+            @pl.when(tick == 3)
+            def _():
+                prepare()
+
             @pl.when(tick >= 5)
             def _():
                 g.complete(tick - 5)
@@ -340,6 +406,9 @@
         when(11, narrow)
 
     g.drain()
+    packs_out()
+    for cp in prep_saves():
+        cp.wait()
 
     @pl.loop(0, NP)
     def _(k):
@@ -355,26 +424,38 @@
             cross(b).wait_send()
 
 
-def forward_call(wq, wo, wf, wp, tokens, small, mask, pkey, pval):
+def forward_call(wq, wo, wf, wp, tokens, segs, pack, aux, r_in, r_out):
     any_, vm = pl.BlockSpec(memory_space=pl.ANY), pl.BlockSpec(memory_space=pltpu.VMEM)
     n, d = tokens.shape
     kept = [
         ((NP * d, d), B16), ((n, d), B16), ((n, d), B16), ((n, d), B16), ((3, n, d), B16), ((4, n, d), B16),
         ((2, HALF, HALF), B16), ((n, d), B16), ((n, d), F32), ((n, d), B16), ((4, n, d), B16), ((4, n, d), B16),
     ]
+    shared = [((16, d), F32), ((HALF, d), B16), ((HALF, d), B16), ((16, 512), F32)]
     dma = pltpu.SemaphoreType.DMA
     order = [0, 2, 3, 4, 5, 6, 7, 8, 9, 10, 11, 1]
-    scratch = [pltpu.VMEM(*kept[i]) for i in order]
+    scratch = [kept[i] for i in order] + [((2, HALF, HALF), F32), ((n, d), F32)] + shared
+    scratch += [((2, HALF, HALF), F32), ((16, 16, 128), B16), ((16, 16, 128), F32)]
     return pl.pallas_call(
         forward_kernel,
-        out_shape=[jax.ShapeDtypeStruct(*k) for k in kept],
-        in_specs=[any_] * 5 + [vm] * 4,
-        out_specs=[any_] * len(kept),
-        scratch_shapes=scratch
-        + [pltpu.VMEM((2, HALF, HALF), F32), pltpu.VMEM((n, d), F32)]
-        + [dma((NP,)), dma((NP, 20)), dma((NP, 16)), dma, dma((2,)), dma((2,)), dma((3, NP))],
+        out_shape=[jax.ShapeDtypeStruct(*k) for k in kept + shared],
+        in_specs=[any_] * 5 + [vm] * 3 + [any_] * 2,
+        out_specs=[any_] * len(kept + shared),
+        scratch_shapes=[pltpu.VMEM(*v) for v in scratch]
+        + [dma((NP,)), dma((NP, 20)), dma((NP, 16)), dma, dma((2,)), dma((2,)), dma((3, NP)), dma((16,)), dma((16,)), dma((8,))],
         compiler_params=pltpu.CompilerParams(collective_id=0, has_side_effects=True, vmem_limit_bytes=62 << 20),
-    )(wq, wo, wf, wp, tokens, small, mask, pkey, pval)
+    )(wq, wo, wf, wp, tokens, segs, pack, aux, r_in, r_out)
+
+
+def own_pack(gains, biases):
+    rows = jnp.concatenate([biases.reshape(11, 64), gains.reshape(2, 64), jnp.zeros((3, 64), B16)])
+    return jnp.concatenate([rows, rows], axis=1)
+
+
+def prefix_rows(embed, in_bias, out_bias):
+    in_bias = jnp.pad(in_bias, (0, 512)).reshape(1, 1024)
+    return jnp.concatenate([embed, in_bias, out_bias.reshape(2, 1024), jnp.zeros((3, 1024), B16)])
+
 
 SPLIT = 6
 BACK_TICKS = 2 + 2 * SPLIT + NP + 6
@@ -393,11 +474,11 @@
 
 
 def backward_kernel(
-    W_i, h_i, a1_i, qkv_i, prob_i, ppre_i, att_i, res_i, a2_i, gp_i, act_i, cot, small, pkey, pval,
-    dh_o, oq, oo, of, op_, SG, DKV,
+    W_i, h_i, a1_i, qkv_i, prob_i, ppre_i, att_i, res_i, a2_i, gp_i, act_i, cot, r_out, small, pkey, pval,
+    dh_o, oq, oo, of, op_, own_sums, KVB, HSUM,
     WG, H, A1, QKV, BIG, PPRE, ATT, RES, A2, GP, DM, DAT, DATT, DPP, DSP, ACC,
-    RC, RY, RU, RD, T,
-    wsem, lsem, osem, cs, cr, ys, yr, us, ur, ds_, dr, xs, xr, hs,
+    RC, RY, RU, RD, T, SG, DKV, SB, RB, PF, PG, HP, HPR,
+    wsem, lsem, osem, cs, cr, ys, yr, us, ur, ds_, dr, xs, xr, hs, bs, br, ps, pr, hx,
 ):
     s, d, z, y, c = place()
     for k in (8, 9, 10, 11, 4, 5, 6, 7, 3, 2, 1, 0):
@@ -432,7 +513,8 @@
         loads()[i].start()
     SG[...] = jnp.zeros_like(SG)
     DKV[...] = jnp.zeros_like(DKV)
-    greet(s, z, y, c, cross=True)
+    SB[...] = jnp.zeros_like(SB)
+    greet(s, d)
 
     def weights(ks):
         for k in ks:
@@ -566,8 +648,6 @@
 
     def grad_proj():
         loads()[L_ACT].wait()
-        SG[8:9] = column_sum(DM[...])
-
         @pl.loop(0, 4)
         def _(i):
             for u in range(2):
@@ -585,16 +665,65 @@
             WG[k, 2 * i : 2 * i + 2] = part.astype(B16).reshape(2, 2, 2, 64, 1024)
 
     def grad_fc(j):
-        SG[pl.ds(4 + j, 1)] = column_sum(GP[j])
         put(4 + j, A2, GP.at[j])
 
     def grad_out():
+        put(3, ATT, DAT)
+
+    def grad_qkv(i):
+        put(i, A1, QKV.at[i])
+
+    send_sums, sums_in, sums_out = to_all(lambda to: SB.at[to], RB, bs, br)
+    send_pref, pref_in, pref_out = to_all(lambda to: PF, PG, ps, pr)
+
+    def r_out_in():
+        return [pltpu.make_async_copy(r_out.at[:, pl.ds(1024 * i, 1024)], BIG.at[i], hx.at[i]) for i in range(2)]
+
+    def hidden_across():
+        return pltpu.make_async_remote_copy(HP, HPR, hx.at[2], hx.at[3], device_id=(1 - s, d), device_id_type=MESH)
+
+    def small_first():
+        for cp in r_out_in():
+            cp.start()
+        for i in range(3):
+            SG[i : i + 1] = column_sum(QKV[i])
         SG[3:4] = column_sum(DAT[...])
-        put(3, ATT, DAT)
-
-    def grad_qkv(i):
-        SG[pl.ds(i, 1)] = column_sum(QKV[i])
-        put(i, A1, QKV.at[i])
+        for j in range(4):
+            SG[4 + j : 5 + j] = column_sum(GP[j])
+        SG[8:9] = column_sum(DM[...])
+        for i in range(16):
+            for n in range(13):
+                m = 11 * i + n
+                row, at = (m // 16, 128 * (m % 16 // 2)) if n < 11 else (n, 128 * (i // 2))
+                SB[i, n : n + 1] = SG[row : row + 1, at : at + 128]
+            SB[i, 16:32] = DKV[16 * (i // 8) : 16 * (i // 8) + 16, 128 * (i % 8) : 128 * (i % 8) + 128]
+        send_sums()
+        RB[d] = SB[d]
+
+    def small_second():
+        sums_in()
+        total = RB[0]
+        for i in range(1, 16):
+            total = total + RB[i]
+        row = lax.broadcasted_iota(jnp.int32, (16, 128), 0)
+        odd = jnp.where(row < 11, d + row, d) % 2 == 1
+        own_sums[...] = jnp.where(odd, pltpu.roll(total[:16], 64, 1), total[:16])
+        PF[...] = total[16:].astype(B16)
+        send_pref()
+        PG[d] = PF[...]
+
+    def small_third():
+        pref_in()
+        for i in range(16):
+            KVB[:, 128 * i : 128 * i + 128] = PG[i]
+        for cp in r_out_in():
+            cp.wait()
+        HP[...] = dot_nt(KVB[:, :1024], BIG[0]) + dot_nt(KVB[:, 1024:], BIG[1])
+        hidden_across().start()
+
+    def small_last():
+        hidden_across().wait()
+        HSUM[...] = HP[...] + HPR[...]
 
     def held(r):
         a = r // 4
@@ -789,6 +918,8 @@
             grad_qkv(11 - r)
 
         scatter_step(r)
+        for at, body in ((10, small_first), (11, small_second), (13, small_third), (16, small_last)):
+            pl.when(r == at)(body)
 
     @pl.loop(0, NP)
     def _(r):
@@ -808,6 +939,9 @@
             def _():
                 down(r, q + 1).wait_send()
 
+    sums_out()
+    pref_out()
+
     @pl.loop(0, 2)
     def _(b):
         dh_out(b).wait()
@@ -817,94 +951,71 @@
             cross(b).wait_send()
 
 
-def backward_call(kept, cot, small, pkey, pval):
+def backward_call(kept, cot, r_out, small, pkey, pval):
     W, h, a1, qkv, prob, ppre, att, res, a2, gp, act = kept
     any_, vm = pl.BlockSpec(memory_space=pl.ANY), pl.BlockSpec(memory_space=pltpu.VMEM)
     n, d = h.shape
     dma = pltpu.SemaphoreType.DMA
     wide = (4, 2, 2, 64, d)
-    prob = prob.reshape(4, 512, 1024)
-    outs = [((n, d), B16), ((1, 64, 3 * d), F32), ((1, 64, d), F32), ((1, 64, 4 * d), F32), ((1, 256, d), F32), ((16, d), F32), ((32, d), F32)]
+    outs = [
+        ((n, d), B16), ((1, 64, 3 * d), F32), ((1, 64, d), F32), ((1, 64, 4 * d), F32), ((1, 256, d), F32),
+        ((16, 128), F32), ((16, 2 * d), B16), ((16, 512), F32),
+    ]
     scratch = [
         ((NP,) + wide, B16), ((n, d), B16), ((n, d), B16), ((3, n, d), B16), ((4, n, d), B16), ((2, HALF, HALF), B16), ((n, d), B16),
         ((n, d), F32), ((n, d), B16), ((4, n, d), B16), ((n, d), B16), ((n, d), B16), ((HALF, d), B16), ((HALF, HALF), F32),
         ((HALF, HALF), B16), ((HALF, d), F32),
         ((4, 4, 2, 64, d), B16), ((4, 4, 64, d), B16), ((7, 3, 64, d), B16), ((7, 3, 64, d), B16), ((2, 64, d), F32),
+        ((16, d), F32), ((32, d), F32), ((16, 32, 128), F32), ((16, 32, 128), F32), ((16, 128), B16), ((16, 16, 128), B16),
+        ((16, 512), F32), ((16, 512), F32),
     ]
     return pl.pallas_call(
         backward_kernel,
         out_shape=[jax.ShapeDtypeStruct(*o) for o in outs],
-        in_specs=[any_] * 12 + [vm] * 3,
-        out_specs=[any_] * 5 + [vm] * 2,
-        scratch_shapes=[pltpu.VMEM(*v) for v in scratch] + [dma((NP,))] * 11 + [dma((2,))] * 3,
+        in_specs=[any_] * 13 + [vm] * 3,
+        out_specs=[any_] * 5 + [vm] * 3,
+        scratch_shapes=[pltpu.VMEM(*v) for v in scratch] + [dma((NP,))] * 11 + [dma((2,))] * 3 + [dma((16,))] * 4 + [dma((4,))],
         compiler_params=pltpu.CompilerParams(collective_id=1, has_side_effects=True, vmem_limit_bytes=64 << 20),
-    )(W.reshape((NP,) + wide), h, a1, qkv, prob, ppre, att, res, a2, gp, act, cot, small, pkey, pval)
-
-def swap_kernel(src, dst, ss, rs):
-    s, d = lax.axis_index("section"), lax.axis_index("dp")
-    bar = pltpu.get_barrier_semaphore()
-    for i in range(1, 16):
-        pl.semaphore_signal(bar, 1, device_id=(s, (d + i) % 16), device_id_type=MESH)
-    dst[d] = src[d]
-    pl.semaphore_wait(bar, 15)
-
-    def cp(i, frm):
-        return pltpu.make_async_remote_copy(
-            src.at[(d + i) % 16], dst.at[frm], ss.at[i], rs.at[i], device_id=(s, (d + i) % 16), device_id_type=MESH
-        )
-
-    for i in range(1, 16):
-        cp(i, d).start()
-    for i in range(1, 16):
-        cp(i, (d + 16 - i) % 16).wait()
-
-
-def swap_blocks(x, cid):
-    vm = pl.BlockSpec(memory_space=pltpu.VMEM)
+    )(W.reshape((NP,) + wide), h, a1, qkv, prob, ppre, att, res, a2, gp, act, cot, r_out, small, pkey, pval)
+
+
+def finish_kernel(
+    o0, o1, o2, o3, o4, o5, hid, kvb, hsum, aux, r_in,
+    c0, c1, c2, c3, c4, c5, g_embed, g_in, g_in_bias, g_out, g_out_bias,
+    G_IN, G_OUT, sem,
+):
+    moves = [pltpu.make_async_copy(a, b, sem.at[i]) for i, (a, b) in enumerate(zip((o0, o1, o2, o3, o4, o5), (c0, c1, c2, c3, c4, c5)))]
+    for cp in moves:
+        cp.start()
+    h = hid[...]
+    kv = kvb[...]
+    G_OUT[...] = dot_tn(h.astype(B16), kv)
+    out_cp = pltpu.make_async_copy(G_OUT, g_out, sem.at[6])
+    out_cp.start()
+    g_out_bias[...] = column_sum(kv)
+    dp = (hsum[...] * (1.0 - h * h)).astype(B16)
+    G_IN[...] = dot_tn(aux[...], dp)
+    in_cp = pltpu.make_async_copy(G_IN, g_in, sem.at[7])
+    in_cp.start()
+    g_in_bias[...] = column_sum(dp)
+    g_embed[...] = dot_nt(dp, r_in[...])[:10]
+    for cp in moves + [out_cp, in_cp]:
+        cp.wait()
+
+
+def finish_call(large, hid, kvb, hsum, aux, r_in):
+    any_, vm = pl.BlockSpec(memory_space=pl.ANY), pl.BlockSpec(memory_space=pltpu.VMEM)
+    d = r_in.shape[0]
+    outs = [jax.ShapeDtypeStruct(x.shape, x.dtype) for x in large]
+    outs += [jax.ShapeDtypeStruct(x, F32) for x in ((10, d), (d, 512), (1, 512), (512, 2 * d), (1, 2 * d))]
     return pl.pallas_call(
-        swap_kernel,
-        out_shape=jax.ShapeDtypeStruct(x.shape, x.dtype),
-        in_specs=[vm],
-        out_specs=vm,
-        scratch_shapes=[pltpu.SemaphoreType.DMA((16,))] * 2,
-        compiler_params=pltpu.CompilerParams(collective_id=cid, has_side_effects=True),
-    )(x)
-
-
-def gather_small(gains, biases):
-    own = jnp.concatenate([biases.reshape(704), gains.reshape(128)])
-    own = jnp.pad(own, (0, 2048 - 832)).reshape(1, 16, 128)
-    got = swap_blocks(jnp.broadcast_to(own, (16, 16, 128)), 2).reshape(16, 2048).astype(F32)
-    bias = got[:, :704].reshape(11, 1024)
-    gain = got[:, 704:832].reshape(16, 2, 64).transpose(1, 0, 2).reshape(2, 1024)
-    return jnp.concatenate([bias, gain, jnp.zeros((3, 1024), F32)])
-
-
-def prefix_blocks(rows):
-    rows = jnp.pad(rows, ((0, 6), (0, 0)))
-    big = jnp.broadcast_to(rows[None], (16, 16, 1024)).reshape(256, 1024)
-    head = lax.broadcasted_iota(jnp.int32, (256, 1024), 0) // 16
-    return jnp.where(head == lax.broadcasted_iota(jnp.int32, (256, 1024), 1) // 64, big, jnp.zeros_like(big))
-
-
-def row_mask(segs):
-    at = jnp.arange(segs.shape[1])
-    ok = (segs[:, :, None] == segs[:, None, :]) & (at[:, None] <= at[None, :])
-    return jnp.where(ok, 0.0, NEG).astype(F32)
-
-def small_sums(sums, dkv):
-    bias = sums[:11].reshape(16, 704)
-    gain = sums[11:13].reshape(2, 16, 64).transpose(1, 0, 2).reshape(16, 128)
-    both = jnp.concatenate([dkv[:10], dkv[16:26]], axis=1)
-    pref = both.reshape(10, 16, 128).transpose(1, 0, 2).reshape(16, 1280)
-    parts = jnp.concatenate([bias, gain, pref], axis=1)
-    parts = jnp.pad(parts, ((0, 0), (0, 3072 - 2112))).reshape(16, 24, 128)
-    mine = jnp.sum(swap_blocks(parts, 3), axis=0).reshape(3072)
-    pref = mine[832:2112].reshape(10, 128).astype(B16)
-    pref = jnp.pad(pref, ((0, 6), (0, 0)))
-    got = swap_blocks(jnp.broadcast_to(pref[None], (16, 16, 128)), 4)
-    got = got[:, :10].transpose(1, 0, 2).reshape(10, 2048)
-    return mine[:704].reshape(1, 704), mine[704:832].reshape(1, 2, 64), got
+        finish_kernel,
+        out_shape=outs,
+        in_specs=[any_] * 6 + [vm] * 5,
+        out_specs=[any_] * 6 + [vm, any_, vm, any_, vm],
+        scratch_shapes=[pltpu.VMEM((d, 512), F32), pltpu.VMEM((512, 2 * d), F32), pltpu.SemaphoreType.DMA((8,))],
+        compiler_params=pltpu.CompilerParams(vmem_limit_bytes=40 << 20),
+    )(*large, hid, kvb, hsum, aux, r_in)
 
 
 def on_device(
@@ -923,39 +1034,23 @@
     reparam_out,
     reparam_out_bias,
 ):
-    pre_hidden = jnp.dot(prefix_embed, reparam_in, preferred_element_type=F32) + reparam_in_bias.astype(F32)
-    hidden = jnp.tanh(pre_hidden)
-    hidden_b = hidden.astype(B16)
-    prefix_kv = (
-        jnp.dot(hidden_b, reparam_out, preferred_element_type=F32) + reparam_out_bias.astype(F32)
-    ).astype(B16)
-    pkey, pval = prefix_blocks(prefix_kv[:, :1024]), prefix_blocks(prefix_kv[:, 1024:])
-    small = gather_small(gains, biases)
-    kept = forward_call(w_qkv, w_attn_out, w_fc, w_proj, tokens, small, row_mask(segment_ids), pkey, pval)
-    dh, gq, go, gf, gp, sums, dkv = backward_call(kept[:1] + kept[2:], cotangent, small, pkey, pval)
-    grad_biases, grad_gains, prefix_grad_b = small_sums(sums, dkv)
-    grad_reparam_out = jnp.einsum("pr,pc->rc", hidden_b, prefix_grad_b, preferred_element_type=F32)
-    grad_reparam_out_bias = jnp.sum(prefix_grad_b.astype(F32), axis=0)
-    hidden_part = jnp.dot(prefix_grad_b, reparam_out.T, preferred_element_type=F32)
-    hidden_grad = hidden_part + lax.ppermute(hidden_part, "section", [(0, 1), (1, 0)])
-    dpre_hidden_b = (hidden_grad * (1.0 - hidden * hidden)).astype(B16)
-    grad_reparam_in = jnp.einsum("pd,pr->dr", prefix_embed, dpre_hidden_b, preferred_element_type=F32)
-    grad_reparam_in_bias = jnp.sum(dpre_hidden_b.astype(F32), axis=0)
-    grad_prefix_embed = jnp.dot(dpre_hidden_b, reparam_in.T, preferred_element_type=F32)
+    aux = prefix_rows(prefix_embed, reparam_in_bias, reparam_out_bias)
+    pack = own_pack(gains, biases)
+    kept = forward_call(w_qkv, w_attn_out, w_fc, w_proj, tokens, segment_ids, pack, aux, reparam_in, reparam_out)
+    small, pkey, pval, hid = kept[12:]
+    *large, sums, kvb, hsum = backward_call(kept[:1] + kept[2:12], cotangent, reparam_out, small, pkey, pval)
+    done = finish_call([kept[1]] + large, hid, kvb, hsum, aux, reparam_in)
     return (
-        kept[1][None],
-        dh[None],
-        gq,
-        go,
-        gf,
-        gp,
-        grad_gains,
-        grad_biases,
-        grad_prefix_embed,
-        grad_reparam_in,
-        grad_reparam_in_bias,
-        grad_reparam_out,
-        grad_reparam_out_bias,
+        done[0][None],
+        done[1][None],
+        *done[2:6],
+        sums[11:13, :64][None],
+        sums[:11, :64].reshape(1, 704),
+        done[6],
+        done[7],
+        done[8][0],
+        done[9],
+        done[10][0],
     )
 
 

time: 483 us -> 455 us (0.942)
  Pallas kernels: 448 us -> 434 us
  matrix products: 8.33 us -> 0 us
    pallas_call x3 -> x1, Pallas kernels: 28.5 us -> 5.25 us  [finish_call(): pl.pallas_call(finish_kernel, out_shape=outs, in_specs=[any_] * 6 + [vm]...]
    dot_general x6 -> x0, matrix products: 8.33 us -> none  [the longest x1 2.74 us: on_device(): jnp.einsum('pr,pc->rc', hidden_b, prefix_grad_b, preferred_element_type=F32)]
    pallas_call x1, Pallas kernels: 247 us -> 252 us  [backward_call(): pl.pallas_call(backward_kernel, out_shape=[jax.ShapeDtypeStruct(*o) for o...]
    pallas_call x1, Pallas kernels: 172 us -> 177 us  [forward_call(): pl.pallas_call(forward_kernel, out_shape=[jax.ShapeDtypeStruct(*k) for k...]
    unnamed x40 -> x22, local copies, waits for them, and re-layouts: 10.2 us -> 11.3 us
  transfers between devices with their start and end apart: 1 -> 0, of which waited for: 0 -> 0; matrix products, arithmetic and copies ran while one was open for 1% -> 0% of each run, Pallas kernels for 0% -> 0%
where the time goes in v3:
time: 455 us; the launch traced here: 454 us
  Pallas kernels  434 us (95%)
  local copies, waits for them, and re-layouts  15.5 us (3%)
    pallas_call x1, Pallas kernels, backward_call(): pl.pallas_call(backward_kernel, out_shape=[jax.ShapeDtypeStruct(*o) for o...  252 us
    pallas_call x1, Pallas kernels, forward_call(): pl.pallas_call(forward_kernel, out_shape=[jax.ShapeDtypeStruct(*k) for k...  177 us
    unnamed x22, local copies, waits for them, and re-layouts  11.3 us

profile of v3, /device:TPU:0, one launch (start us, length us, event | category | flops | bytes accessed | tf_op | source)
XLA Modules:
  0.0 454.2 jit_solution(13403944569957090715)
XLA Ops:
  0.7 0.1 pad.8.clone
  0.7 0.7 reduce
  1.4 0.1 reshape.44
  1.5 1.4 maximum_maximum_fusion.1.pack
  2.9 0.7 pad.4
  3.6 0.7 reshape.47
  4.3 1.4 maximum_maximum_fusion.aux
  5.8 176.9 %shard_map.237 = (bf16[12288,1024]{1,0:T(8,128)(2,1)}, bf16[512,1024]{1,0:T(8,128)(2,1)}, bf16[512,1024]{1,0:T(8,128)(2,1)}, bf16[512,1024]{1,0:T(8,128)(2,1)}, ...) custom-call(bf16[1,64,3072]{2,1,0:T(8,128)(2,1)} %wq.1, ...), custom_call_target="tpu_custom_call" | custom-call | tf_op jit(solution)/shard_map/pallas_call | solution.py:439
  182.7 252.2 %shard_map.238 = (bf16[512,1024]{1,0:T(8,128)(2,1)}, f32[1,64,3072]{2,1,0:T(8,128)}, f32[1,64,1024]{2,1,0:T(8,128)}, f32[1,64,4096]{2,1,0:T(8,128)}, f32[1,256,1...) custom-call(bf16[12,4,2,2,64,1024]{5,4,3,2,1,0:T(8,128)(2,1)} %bitcast.9, ...), custom_call_target="tpu_custom_call" | custom-call | tf_op jit(solution)/shard_map/pallas_call | solution.py:972
  434.9 1.2 slice_bitcast_fusion
  436.1 1.3 reshape.49
  437.5 0.0 copy-start
  437.5 1.2 copy-done
  438.7 0.0 copy-start.1
  438.7 1.2 copy-done.1
  440.0 0.0 copy-start.2
  440.0 1.2 copy-done.2
  441.2 0.0 copy-start.3
  441.2 1.2 copy-done.3
  442.4 0.0 copy-start.4
  442.4 1.2 copy-done.4
  443.6 0.0 copy-start.5
  443.6 1.1 copy-done.5
  444.8 0.0 copy-start.6
  444.8 0.8 copy-done.6
  445.5 0.0 copy-start.7
  445.5 0.9 copy-done.7
  446.5 0.0 copy-start.8
  446.5 0.8 copy-done.8
  447.3 0.0 copy-start.9
  447.3 0.8 copy-done.9
  448.1 0.0 copy-start.10
  448.1 0.8 copy-done.10
  448.8 5.3 %shard_map.239 = (bf16[512,1024]{1,0:T(8,128)(2,1)}, bf16[512,1024]{1,0:T(8,128)(2,1)}, f32[1,64,3072]{2,1,0:T(8,128)}, f32[1,64,1024]{2,1,0:T(8,128)}, f32[1,64...) custom-call(bf16[512,1024]{1,0:T(8,128)(2,1)S(1)} %copy-done.1, ...), custom_call_target="tpu_custom_call" | custom-call | tf_op jit(solution)/shard_map/pallas_call | solution.py:1011
  (3 shorter events, 0.0 us)
Async XLA Ops:
  437.5 1.2 copy-start
  438.7 1.2 copy-start.1
  440.0 1.2 copy-start.2
  441.2 1.2 copy-start.3
  442.4 1.2 copy-start.4
  443.6 1.1 copy-start.5
  444.8 0.8 copy-start.6
  445.5 0.9 copy-start.7
  446.5 0.8 copy-start.8
  447.3 0.8 copy-start.9
  448.1 0.8 copy-start.10

commit v4 on v3

--- a/solution.py
+++ b/solution.py
@@ -14,6 +14,7 @@
 F32 = jnp.float32
 B16 = jnp.bfloat16
 NP = 12
+AHEAD = 1
 
 
 def place():
@@ -77,15 +78,19 @@
     def step(self, t, own):
         z, y, c = self.z, self.y, self.c
         start = lambda cp: cp.start()
-        @pl.when(t < NP)
-        def _():
-            own(t)
-            self.to_y(t, z, start)
+        def fresh(k):
+            own(k)
+            self.to_y(k, z, start)
             @pl.when(z < 3)
-            def _(): self.to_up(t, z, start)
+            def _(): self.to_up(k, z, start)
             @pl.when(z > 0)
-            def _(): self.to_down(t, z, start)
-            self.to_c(t, z, y, start)
+            def _(): self.to_down(k, z, start)
+            self.to_c(k, z, y, start)
+        @pl.when(t == 0)
+        def _():
+            for k in range(AHEAD): fresh(k)
+        @pl.when(t + AHEAD < NP)
+        def _(): fresh(t + AHEAD)
         for q in (1, 2, 3, 4):
             k = t - q
             ok = (k >= 0) & (k < NP)
@@ -294,8 +299,7 @@
             there = lax.broadcasted_iota(jnp.int32, sp.shape, 0) % 16 < 10
             SPRE[b] = jnp.where(there, sp, NEG)
 
-        @pl.loop(part * 4, part * 4 + 4)
-        def _(p):
+        def pair(p):
             cols = pl.ds(pl.multiple_of(p * 128, 128), 128)
             q2, k2, v2 = QKV[0, half(b), cols], QKV[1, half(b), cols], QKV[2, half(b), cols]
             st = dot_nt(split_heads(k2), q2)
@@ -313,6 +317,9 @@
             PPRE[b, pl.ds(pl.multiple_of(p * 32, 32), 32)] = jnp.concatenate(pres, axis=0)
             ACC[half(b), cols] = dot_tn(pr, split_heads(v2))
 
+        for p in range(4):
+            pair(part * 4 + p)
+
         @pl.when(part == 1)
         def _():
             ATT[half(b)] = (ACC[half(b)] + dot_tn(PPRE[b], pval[...])).astype(B16)
@@ -331,11 +338,10 @@
     def widen(j, b):
         x = dot_nn(A2[half(b)], W[rows_of(4 + j)]) + small[pl.ds(4 + j, 1)]
         x2 = x * x
-        t = jnp.tanh(GELU_C * (x + 0.044715 * (x2 * x)))
-        ACT[j, half(b)] = (0.5 * x * (1.0 + t)).astype(B16)
-        GP[j, half(b)] = (
-            0.5 * (1.0 + t) + (0.5 * GELU_C) * x * (1.0 - t * t) * (1.0 + (3 * 0.044715) * x2)
-        ).astype(B16)
+        h = 0.5 + 0.5 * jnp.tanh(x * (GELU_C + (0.044715 * GELU_C) * x2))
+        act = x * h
+        ACT[j, half(b)] = act.astype(B16)
+        GP[j, half(b)] = (h + act * (1.0 - h) * (2.0 * GELU_C + (6 * 0.044715 * GELU_C) * x2)).astype(B16)
 
         @pl.when(j == 3)
         def _():
@@ -481,8 +487,16 @@
     wsem, lsem, osem, cs, cr, ys, yr, us, ur, ds_, dr, xs, xr, hs, bs, br, ps, pr, hx,
 ):
     s, d, z, y, c = place()
-    for k in (8, 9, 10, 11, 4, 5, 6, 7, 3, 2, 1, 0):
-        pltpu.make_async_copy(W_i.at[k], WG.at[k], wsem.at[k]).start()
+
+    def slot(k):
+        return k + 8 * (1 - s) if k < 4 else k
+
+    def fetch(ks):
+        return [pltpu.make_async_copy(W_i.at[k], WG.at[slot(k)], wsem.at[k]) for k in ks]
+
+    def begin(cps):
+        for cp in cps:
+            cp.start()
 
     def loads():
         pairs = [
@@ -493,38 +507,27 @@
 
     L_GP, L_A2, L_RES, L_ATT, L_QKV, L_PPRE, L_A1, L_H, L_ACT, L_PROB, L_COT = range(11)
 
-    @pl.when(s == 1)
-    def _():
-        loads()[L_COT].start()
-
-    loads()[L_GP].start()
-    for i in (L_A2, L_RES, L_ATT, L_QKV, L_PPRE):
-        loads()[i].start()
-
-    @pl.when(s == 0)
-    def _():
-        loads()[L_ACT].start()
-
-    @pl.when(s == 1)
-    def _():
-        loads()[L_PROB].start()
-
-    for i in (L_A1, L_H):
-        loads()[i].start()
+    def begin_loads(which):
+        begin([loads()[i] for i in which])
+
+    pl.when(s == 1)(lambda: begin_loads((L_COT,)))
+    begin(fetch((8, 9, 10, 11)))
+    begin_loads((L_GP,))
+    pl.when(s == 0)(lambda: begin_loads((L_ACT,)))
     SG[...] = jnp.zeros_like(SG)
     DKV[...] = jnp.zeros_like(DKV)
     SB[...] = jnp.zeros_like(SB)
     greet(s, d)
 
     def weights(ks):
-        for k in ks:
-            pltpu.make_async_copy(W_i.at[k], WG.at[k], wsem.at[k]).wait()
+        for cp in fetch(ks):
+            cp.wait()
 
     def half(b):
         return pl.ds(pl.multiple_of(b * HALF, HALF), HALF)
 
     def weight(k):
-        return WG[k].reshape(1024, 1024)
+        return WG[slot(k)].reshape(1024, 1024)
 
     def cross(b):
         return pltpu.make_async_remote_copy(
@@ -545,13 +548,24 @@
 
             weights((8, 9, 10, 11))
             loads()[L_GP].wait()
-
-        @pl.when(s == 0)
-        def _():
-            cross(b).wait_recv()
+            begin(fetch((4, 5, 6, 7)))
+            begin_loads((L_A2, L_RES))
+
+            @pl.when(s == 1)
+            def _():
+                begin(fetch((3,)))
+                begin_loads((L_QKV, L_PPRE, L_PROB))
+
+            @pl.when(s == 0)
+            def _():
+                cross(0).wait_recv()
 
         for j in range(4):
             GP[j, half(b)] = (dot_nt(DM[half(b)], weight(8 + j)) * GP[j, half(b)].astype(F32)).astype(B16)
+
+        @pl.when((s == 0) & (b == 1))
+        def _():
+            begin(fetch((3, 0, 1, 2)))
 
     def ffn_norm(b):
         @pl.when(b == 0)
@@ -559,6 +573,15 @@
             weights((4, 5, 6, 7))
             loads()[L_A2].wait()
             loads()[L_RES].wait()
+            begin_loads((L_ATT, L_A1, L_H))
+
+            @pl.when(s == 0)
+            def _():
+                begin_loads((L_QKV, L_PPRE))
+
+            @pl.when(s == 1)
+            def _():
+                begin(fetch((0, 1, 2)))
 
         grad = dot_nt(GP[0, half(b)], weight(4))
         for j in range(1, 4):
@@ -648,12 +671,16 @@
 
     def grad_proj():
         loads()[L_ACT].wait()
+
+        @pl.when(s == 0)
+        def _():
+            cross(1).wait_recv()
         @pl.loop(0, 4)
         def _(i):
             for u in range(2):
                 v = dot_tn(BIG[i, :, 512 * u : 512 * (u + 1)], DM[...]).astype(B16).reshape(2, 4, 64, 1024)
                 for j in range(4):
-                    WG[8 + j, i, u] = v[:, j]
+                    WG[8 * s + j, i, u] = v[:, j]
 
         @pl.when(s == 0)
         def _():
@@ -668,10 +695,10 @@
         put(4 + j, A2, GP.at[j])
 
     def grad_out():
-        put(3, ATT, DAT)
+        put(slot(3), ATT, DAT)
 
     def grad_qkv(i):
-        put(i, A1, QKV.at[i])
+        put(i + 8 * (1 - s), A1, QKV.at[i])
 
     send_sums, sums_in, sums_out = to_all(lambda to: SB.at[to], RB, bs, br)
     send_pref, pref_in, pref_out = to_all(lambda to: PF, PG, ps, pr)
@@ -727,7 +754,7 @@
 
     def held(r):
         a = r // 4
-        return ((2 - a) * (1 - a) // 2) * (r + 8) + a * (2 - a) * r + (a * (a - 1) // 2) * (11 - r)
+        return ((2 - a) * (1 - a) // 2) * (r + 8 * s) + a * (2 - a) * r + (a * (a - 1) // 2) * (11 - r + 8 * (1 - s))
 
     def across_c(r):
         return pltpu.make_async_remote_copy(
@@ -741,15 +768,15 @@
             device_id=(s, z * 4 + (1 - y) * 2 + c), device_id_type=MESH,
         )
 
-    def up(r, n, first):
+    def up(r, i):
         return pltpu.make_async_remote_copy(
-            WG.at[held(r), pl.ds(first, n), y, c], RU.at[r % 7, pl.ds(first - 1, n)], us.at[r], ur.at[r],
+            WG.at[held(r), i, y, c], RU.at[r % 7, i - 1], us.at[r, i - 1], ur.at[r, i - 1],
             device_id=(s, (z + 1) * 4 + y * 2 + c), device_id_type=MESH,
         )
 
-    def down(r, n):
+    def down(r, i):
         return pltpu.make_async_remote_copy(
-            WG.at[held(r), pl.ds(0, n), y, c], RD.at[r % 7, pl.ds(0, n)], ds_.at[r], dr.at[r],
+            WG.at[held(r), i, y, c], RD.at[r % 7, i], ds_.at[r, i], dr.at[r, i],
             device_id=(s, (z - 1) * 4 + y * 2 + c), device_id_type=MESH,
         )
 
@@ -815,11 +842,13 @@
 
             @pl.when(z == 0)
             def _():
-                up(r, 3, 1).start()
+                for i in (3, 2, 1):
+                    up(r, i).start()
 
             @pl.when(z == 3)
             def _():
-                down(r, 3).start()
+                for i in (0, 1, 2):
+                    down(r, i).start()
 
         for q in (1, 2, 3):
             n = 4 - q
@@ -831,23 +860,19 @@
 
                 @pl.when(z == q)
                 def _():
-                    up_here = pltpu.make_async_remote_copy(
-                        WG.at[k, pl.ds(q, n), y, c], RU.at[r % 7, pl.ds(q - 1, n)], us.at[r], ur.at[r],
-                        device_id=(s, d), device_id_type=MESH,
-                    )
-                    up_here.wait_recv()
-                    for i in range(q + 1, 4):
-                        add(k, i, y, RU[r % 7, i - 1])
-                    if n > 1:
-                        up(r, n - 1, q + 1).start()
+                    for i in range(3, q - 1, -1):
+                        up(r, i).wait_recv()
+                        if i > q:
+                            add(k, i, y, RU[r % 7, i - 1])
+                            up(r, i).start()
 
                 @pl.when(z == 3 - q)
                 def _():
-                    down(r, n).wait_recv()
-                    for i in range(n - 1):
-                        add(k, i, y, RD[r % 7, i])
-                    if n > 1:
-                        down(r, n - 1).start()
+                    for i in range(n):
+                        down(r, i).wait_recv()
+                        if i < n - 1:
+                            add(k, i, y, RD[r % 7, i])
+                            down(r, i).start()
 
         @pl.when(live(t - 5))
         def _():
@@ -874,32 +899,28 @@
     def _(tick):
         turn = tick // SPLIT
 
-        def when(i, at, body):
-            mine = ((s == 0) & (tick == at)) | ((s == 1) & ((tick == i) | (tick == SPLIT + i)))
-
-            @pl.when(mine)
-            def _():
-                pl.loop(s * turn, (1 - s) * 2 + s * (turn + 1))(body)
-
-        @pl.when(((s == 0) & (tick < 2)) | ((s == 1) & ((tick == 0) | (tick == SPLIT))))
-        def _():
-            ffn_in((1 - s) * tick + s * turn)
-
-        when(1, 3, ffn_norm)
-        first = 5 - 3 * s + 3 * (1 - s) * ((tick - 5) // 3) + s * SPLIT * turn
-        b0 = (1 - s) * ((tick - 5) // 3) + s * turn
-        in_turn = ((s == 0) & (tick >= 5) & (tick < 11)) | ((s == 1) & (tick < 2 * SPLIT))
-
-        @pl.when(in_turn & (tick == first))
-        def _():
-            attn_out(b0)
-
-        @pl.when(in_turn & ((tick == first + 1) | (tick == first + 2)))
-        def _():
-            attn_back(tick - first - 1, b0)
-
-        when(5, 11, attn_norm)
-        r = tick - 2 - (2 * SPLIT - 2) * s
+        @pl.when((tick == 0) | (tick == 2 * (1 - s) + SPLIT * s))
+        def _():
+            ffn_in((tick > 0).astype(jnp.int32))
+
+        def when(i, at0, at1, body):
+            early = (1 - s) * at0 + s * i
+            late = (1 - s) * at1 + s * (SPLIT + i)
+
+            @pl.when((tick == early) | (tick == late))
+            def _():
+                body((tick == late).astype(jnp.int32))
+
+        when(1, 3, 4, ffn_norm)
+        when(2, 5, 7, attn_out)
+        first = (tick - 3) % SPLIT * s + (tick - 5) % 2 * (1 - s)
+
+        @pl.when(((s == 0) & (tick >= 5) & (tick < 9)) | ((s == 1) & (tick < 2 * SPLIT) & (first < 2)))
+        def _():
+            attn_back(first, (1 - s) * ((tick - 5) // 2) + s * turn)
+
+        when(5, 9, 10, attn_norm)
+        r = tick - 1 - (2 * SPLIT - 1) * s
 
         @pl.when(r == 0)
         def _():
@@ -933,11 +954,13 @@
 
             @pl.when(z == q)
             def _():
-                up(r, 3 - q, q + 1).wait_send()
+                for i in range(q + 1, 4):
+                    up(r, i).wait_send()
 
             @pl.when(z == q + 1)
             def _():
-                down(r, q + 1).wait_send()
+                for i in range(q + 1):
+                    down(r, i).wait_send()
 
     sums_out()
     pref_out()
@@ -974,18 +997,20 @@
         out_shape=[jax.ShapeDtypeStruct(*o) for o in outs],
         in_specs=[any_] * 13 + [vm] * 3,
         out_specs=[any_] * 5 + [vm] * 3,
-        scratch_shapes=[pltpu.VMEM(*v) for v in scratch] + [dma((NP,))] * 11 + [dma((2,))] * 3 + [dma((16,))] * 4 + [dma((4,))],
+        scratch_shapes=[pltpu.VMEM(*v) for v in scratch] + [dma((NP,))] * 7 + [dma((NP, 3))] * 4 + [dma((2,))] * 3 + [dma((16,))] * 4 + [dma((4,))],
         compiler_params=pltpu.CompilerParams(collective_id=1, has_side_effects=True, vmem_limit_bytes=64 << 20),
     )(W.reshape((NP,) + wide), h, a1, qkv, prob, ppre, att, res, a2, gp, act, cot, r_out, small, pkey, pval)
 
 
 def finish_kernel(
-    o0, o1, o2, o3, o4, o5, hid, kvb, hsum, aux, r_in,
-    c0, c1, c2, c3, c4, c5, g_embed, g_in, g_in_bias, g_out, g_out_bias,
-    G_IN, G_OUT, sem,
+    o0, o1, o2, o3, o4, o5, hid, kvb, hsum, aux, r_in, sums,
+    c0, c1, c2, c3, c4, c5, g_embed, g_in, g_in_bias, g_out, g_out_bias, g_gains, g_bias,
+    G_IN, G_OUT, M0, M1, M2, M3, M4, M5, sem,
 ):
-    moves = [pltpu.make_async_copy(a, b, sem.at[i]) for i, (a, b) in enumerate(zip((o0, o1, o2, o3, o4, o5), (c0, c1, c2, c3, c4, c5)))]
-    for cp in moves:
+    held = (M0, M1, M2, M3, M4, M5)
+    here = [pltpu.make_async_copy(a, m, sem.at[i]) for i, (a, m) in enumerate(zip((o0, o1, o2, o3, o4, o5), held))]
+    away = [pltpu.make_async_copy(m, c, sem.at[8 + i]) for i, (m, c) in enumerate(zip(held, (c0, c1, c2, c3, c4, c5)))]
+    for cp in here:
         cp.start()
     h = hid[...]
     kv = kvb[...]
@@ -993,29 +1018,37 @@
     out_cp = pltpu.make_async_copy(G_OUT, g_out, sem.at[6])
     out_cp.start()
     g_out_bias[...] = column_sum(kv)
+    for cp, out in zip(here, away):
+        cp.wait()
+        out.start()
     dp = (hsum[...] * (1.0 - h * h)).astype(B16)
     G_IN[...] = dot_tn(aux[...], dp)
     in_cp = pltpu.make_async_copy(G_IN, g_in, sem.at[7])
     in_cp.start()
     g_in_bias[...] = column_sum(dp)
     g_embed[...] = dot_nt(dp, r_in[...])[:10]
-    for cp in moves + [out_cp, in_cp]:
+    g_gains[0] = sums[11:13, :64]
+    for i in range(11):
+        g_bias[:, 64 * i : 64 * i + 64] = sums[i : i + 1, :64]
+    for cp in away + [out_cp, in_cp]:
         cp.wait()
 
 
-def finish_call(large, hid, kvb, hsum, aux, r_in):
+def finish_call(large, hid, kvb, hsum, aux, r_in, sums):
     any_, vm = pl.BlockSpec(memory_space=pl.ANY), pl.BlockSpec(memory_space=pltpu.VMEM)
     d = r_in.shape[0]
     outs = [jax.ShapeDtypeStruct(x.shape, x.dtype) for x in large]
-    outs += [jax.ShapeDtypeStruct(x, F32) for x in ((10, d), (d, 512), (1, 512), (512, 2 * d), (1, 2 * d))]
+    outs += [jax.ShapeDtypeStruct(x, F32) for x in ((10, d), (d, 512), (1, 512), (512, 2 * d), (1, 2 * d), (1, 2, 64), (1, 704))]
     return pl.pallas_call(
         finish_kernel,
         out_shape=outs,
-        in_specs=[any_] * 6 + [vm] * 5,
-        out_specs=[any_] * 6 + [vm, any_, vm, any_, vm],
-        scratch_shapes=[pltpu.VMEM((d, 512), F32), pltpu.VMEM((512, 2 * d), F32), pltpu.SemaphoreType.DMA((8,))],
-        compiler_params=pltpu.CompilerParams(vmem_limit_bytes=40 << 20),
-    )(*large, hid, kvb, hsum, aux, r_in)
+        in_specs=[any_] * 6 + [vm] * 6,
+        out_specs=[any_] * 6 + [vm, any_, vm, any_, vm, vm, vm],
+        scratch_shapes=[pltpu.VMEM((d, 512), F32), pltpu.VMEM((512, 2 * d), F32)]
+        + [pltpu.VMEM(x.shape, x.dtype) for x in large]
+        + [pltpu.SemaphoreType.DMA((14,))],
+        compiler_params=pltpu.CompilerParams(vmem_limit_bytes=63 << 20),
+    )(*large, hid, kvb, hsum, aux, r_in, sums)
 
 
 def on_device(
@@ -1039,13 +1072,13 @@
     kept = forward_call(w_qkv, w_attn_out, w_fc, w_proj, tokens, segment_ids, pack, aux, reparam_in, reparam_out)
     small, pkey, pval, hid = kept[12:]
     *large, sums, kvb, hsum = backward_call(kept[:1] + kept[2:12], cotangent, reparam_out, small, pkey, pval)
-    done = finish_call([kept[1]] + large, hid, kvb, hsum, aux, reparam_in)
+    done = finish_call([kept[1]] + large, hid, kvb, hsum, aux, reparam_in, sums)
     return (
         done[0][None],
         done[1][None],
         *done[2:6],
-        sums[11:13, :64][None],
-        sums[:11, :64].reshape(1, 704),
+        done[11],
+        done[12],
         done[6],
         done[7],
         done[8][0],

time: 455 us -> 439 us (0.965)
  local copies, waits for them, and re-layouts: 15.5 us -> 1.55 us
    unnamed x22 -> x0, local copies, waits for them, and re-layouts: 11.3 us -> none
where the time goes in v4:
time: 439 us; the launch traced here: 438 us
  Pallas kernels  433 us (99%)
    pallas_call x1, Pallas kernels, backward_call(): pl.pallas_call(backward_kernel, out_shape=[jax.ShapeDtypeStruct(*o) for o...  248 us
    pallas_call x1, Pallas kernels, forward_call(): pl.pallas_call(forward_kernel, out_shape=[jax.ShapeDtypeStruct(*k) for k...  176 us

profile of v4, /device:TPU:0, one launch (start us, length us, event | category | flops | bytes accessed | tf_op | source)
XLA Modules:
  0.0 438.5 jit_solution(10704126146517659177)
XLA Ops:
  0.7 0.1 pad.8.clone
  0.7 0.7 reduce
  1.4 0.1 reshape.41
  1.5 1.4 maximum_maximum_fusion.1.pack
  2.9 0.7 pad.4
  3.6 0.7 reshape.44
  4.3 1.4 maximum_maximum_fusion.aux
  5.8 176.4 %shard_map.237 = (bf16[12288,1024]{1,0:T(8,128)(2,1)}, bf16[512,1024]{1,0:T(8,128)(2,1)}, bf16[512,1024]{1,0:T(8,128)(2,1)}, bf16[512,1024]{1,0:T(8,128)(2,1)}, ...) custom-call(bf16[1,64,3072]{2,1,0:T(8,128)(2,1)} %wq.1, ...), custom_call_target="tpu_custom_call" | custom-call | tf_op jit(solution)/shard_map/pallas_call | solution.py:445
  182.1 247.8 %shard_map.238 = (bf16[512,1024]{1,0:T(8,128)(2,1)}, f32[1,64,3072]{2,1,0:T(8,128)}, f32[1,64,1024]{2,1,0:T(8,128)}, f32[1,64,4096]{2,1,0:T(8,128)}, f32[1,256,1...) custom-call(bf16[12,4,2,2,64,1024]{5,4,3,2,1,0:T(8,128)(2,1)} %bitcast.6, ...), custom_call_target="tpu_custom_call" | custom-call | tf_op jit(solution)/shard_map/pallas_call | solution.py:995
  429.9 8.4 %shard_map.239 = (bf16[512,1024]{1,0:T(8,128)(2,1)}, bf16[512,1024]{1,0:T(8,128)(2,1)}, f32[1,64,3072]{2,1,0:T(8,128)}, f32[1,64,1024]{2,1,0:T(8,128)}, f32[1,64...) custom-call(bf16[512,1024]{1,0:T(8,128)(2,1)} %get-tuple-element.50., ...), custom_call_target="tpu_custom_call" | custom-call | tf_op jit(solution)/shard_map/pallas_call | solution.py:1042
  (3 shorter events, 0.0 us)

commit v5 on v4

--- a/solution.py
+++ b/solution.py
@@ -14,6 +14,7 @@
 F32 = jnp.float32
 B16 = jnp.bfloat16
 NP = 12
+MAIN = 896
 AHEAD = 1
 
 
@@ -54,15 +55,16 @@
 
 
 class Gather:
-    def __init__(self, W, ssem, rsem):
-        self.W, self.ssem, self.rsem = W, ssem, rsem
+    def __init__(self, W, ssem, rsem, tsem, qsem):
+        self.W, self.ssem, self.rsem, self.tsem, self.qsem = W, ssem, rsem, tsem, qsem
         self.s, self.d, self.z, self.y, self.c = place()
     def blk(self, k, d):
         i = k // 8
         row = (1-i)*(1024*k+64*d) + i*(8192+256*d+64*(k-8))
         return self.W.at[pl.ds(pl.multiple_of(row, 64), 64)]
-    def cp(self, k, origin, target, slot):
+    def cp(self, k, origin, target, slot, width=1024):
         b = self.blk(k, origin)
+        if width < 1024: b = b.at[:, pl.ds(0, width)]
         return pltpu.make_async_remote_copy(src_ref=b, dst_ref=b, send_sem=self.ssem.at[k, slot], recv_sem=self.rsem.at[k, origin],
             device_id=(self.s, target), device_id_type=MESH)
     def dev(self, z, y, c): return z*4+y*2+c
@@ -71,8 +73,14 @@
         op(self.cp(k, self.dev(zo, self.y, self.c), self.dev(self.z+1, self.y, self.c), zo))
     def to_down(self, k, zo, op):
         op(self.cp(k, self.dev(zo, self.y, self.c), self.dev(self.z-1, self.y, self.c), 4+zo))
-    def to_y(self, k, zo, op):
-        op(self.cp(k, self.dev(zo, self.y, self.c), self.dev(self.z, 1-self.y, self.c), 8+zo))
+    def to_y(self, k, zo, op, width=MAIN):
+        op(self.cp(k, self.dev(zo, self.y, self.c), self.dev(self.z, 1-self.y, self.c), 8+zo, width))
+    def strip(self, k, zo, to, slot):
+        b = self.blk(k, self.dev(zo, 1-self.y, self.c)).at[:, pl.ds(MAIN, 1024-MAIN)]
+        return pltpu.make_async_remote_copy(src_ref=b, dst_ref=b, send_sem=self.tsem.at[k, slot], recv_sem=self.qsem.at[k, zo],
+            device_id=(self.s, self.dev(to, self.y, self.c)), device_id_type=MESH)
+    def strip_up(self, k, zo, op): op(self.strip(k, zo, self.z+1, zo))
+    def strip_down(self, k, zo, op): op(self.strip(k, zo, self.z-1, 4+zo))
     def to_c(self, k, zo, yo, op):
         op(self.cp(k, self.dev(zo, yo, self.c), self.dev(self.z, self.y, 1-self.c), 12+zo*2+yo))
     def step(self, t, own):
@@ -80,7 +88,7 @@
         start = lambda cp: cp.start()
         def fresh(k):
             own(k)
-            self.to_y(k, z, start)
+            self.to_y(k, z, start, 1024)
             @pl.when(z < 3)
             def _(): self.to_up(k, z, start)
             @pl.when(z > 0)
@@ -111,16 +119,31 @@
                     self.to_c(k, z+q, y, start)
             e = q - 1
             def side(zo):
-                self.arrived(k, self.dev(zo, 1-y, c))
+                o = self.dev(zo, 1-y, c)
+                self.cp(k, o, o, 0, MAIN).wait_recv()
                 self.to_c(k, zo, 1-y, start)
             if e == 0:
                 @pl.when(ok)
-                def _(): side(z)
+                def _():
+                    self.arrived(k, self.dev(z, 1-y, c))
+                    @pl.when(z < 3)
+                    def _(): self.strip_up(k, z, start)
+                    @pl.when(z > 0)
+                    def _(): self.strip_down(k, z, start)
+                    self.to_c(k, z, 1-y, start)
             else:
                 @pl.when(ok & (z - e >= 0))
-                def _(): side(z-e)
+                def _():
+                    self.strip(k, z-e, z, 0).wait_recv()
+                    @pl.when(z < 3)
+                    def _(): self.strip_up(k, z-e, start)
+                    side(z-e)
                 @pl.when(ok & (z + e <= 3))
-                def _(): side(z+e)
+                def _():
+                    self.strip(k, z+e, z, 0).wait_recv()
+                    @pl.when(z > 0)
+                    def _(): self.strip_down(k, z+e, start)
+                    side(z+e)
     def complete(self, k):
         for i in range(8):
             self.arrived(k, 2*i + 1-self.c)
@@ -134,7 +157,14 @@
                 def _(): self.to_up(k, zo, fin)
                 @pl.when((zo >= z) & (z > 0))
                 def _(): self.to_down(k, zo, fin)
-                self.to_y(k, zo, fin)
+                @pl.when(zo == z)
+                def _(): self.to_y(k, zo, fin, 1024)
+                @pl.when(zo != z)
+                def _(): self.to_y(k, zo, fin)
+                @pl.when((zo <= z) & (z < 3))
+                def _(): self.strip_up(k, zo, fin)
+                @pl.when((zo >= z) & (z > 0))
+                def _(): self.strip_down(k, zo, fin)
                 for yo in range(2): self.to_c(k, zo, yo, fin)
 
 def own_copies(wq, wo, wf, wp, g, sem):
@@ -182,9 +212,9 @@
     wq, wo, wf, wp, tokens, segs, pack, aux, r_in, r_out,
     W_o, out_o, h_o, a1_o, qkv_o, prob_o, ppre_o, att_o, res_o, a2_o, gp_o, act_o, small_o, pkey_o, pval_o, hid_o,
     W, H, A1, QKV, PROB, PPRE, ATT, RES, A2, GP, ACT, OUT, SPRE, ACC, small, pkey, pval, hid, mask, PACKS, ROWS,
-    own_sem, ssem, rsem, hsem, xs, xr, save_sem, ps, pr, psem,
+    own_sem, ssem, rsem, tsem, qsem, hsem, xs, xr, save_sem, ps, pr, psem,
 ):
-    g = Gather(W, ssem, rsem)
+    g = Gather(W, ssem, rsem, tsem, qsem)
     s = g.s
     for cp in own_copies(wq, wo, wf, wp, g, own_sem):
         cp.start()
@@ -448,7 +478,7 @@
         in_specs=[any_] * 5 + [vm] * 3 + [any_] * 2,
         out_specs=[any_] * len(kept + shared),
         scratch_shapes=[pltpu.VMEM(*v) for v in scratch]
-        + [dma((NP,)), dma((NP, 20)), dma((NP, 16)), dma, dma((2,)), dma((2,)), dma((3, NP)), dma((16,)), dma((16,)), dma((8,))],
+        + [dma((NP,)), dma((NP, 20)), dma((NP, 16)), dma((NP, 8)), dma((NP, 4)), dma, dma((2,)), dma((2,)), dma((3, NP)), dma((16,)), dma((16,)), dma((8,))],
         compiler_params=pltpu.CompilerParams(collective_id=0, has_side_effects=True, vmem_limit_bytes=62 << 20),
     )(wq, wo, wf, wp, tokens, segs, pack, aux, r_in, r_out)
 
@@ -483,8 +513,8 @@
     W_i, h_i, a1_i, qkv_i, prob_i, ppre_i, att_i, res_i, a2_i, gp_i, act_i, cot, r_out, small, pkey, pval,
     dh_o, oq, oo, of, op_, own_sums, KVB, HSUM,
     WG, H, A1, QKV, BIG, PPRE, ATT, RES, A2, GP, DM, DAT, DATT, DPP, DSP, ACC,
-    RC, RY, RU, RD, T, SG, DKV, SB, RB, PF, PG, HP, HPR,
-    wsem, lsem, osem, cs, cr, ys, yr, us, ur, ds_, dr, xs, xr, hs, bs, br, ps, pr, hx,
+    RC, RY, RU, RD, RUS, RDS, RYS, T, SG, DKV, SB, RB, PF, PG, HP, HPR,
+    wsem, lsem, osem, cs, cr, ys, yr, us, ur, ds_, dr, yss, ysr, xs, xr, hs, bs, br, ps, pr, hx,
 ):
     s, d, z, y, c = place()
 
@@ -764,7 +794,7 @@
 
     def across_y(r):
         return pltpu.make_async_remote_copy(
-            WG.at[held(r), :, 1 - y, c], RY.at[r % 4], ys.at[r], yr.at[r],
+            WG.at[held(r), :, 1 - y, c, :, pl.ds(0, MAIN)], RY.at[r % 4], ys.at[r], yr.at[r],
             device_id=(s, z * 4 + (1 - y) * 2 + c), device_id_type=MESH,
         )
 
@@ -780,6 +810,24 @@
             device_id=(s, (z - 1) * 4 + y * 2 + c), device_id_type=MESH,
         )
 
+    def strip_up(r, i):
+        return pltpu.make_async_remote_copy(
+            WG.at[held(r), i, 1 - y, c, :, pl.ds(MAIN, 1024 - MAIN)], RUS.at[r % 7, i - 1], us.at[r, 2 + i], ur.at[r, 2 + i],
+            device_id=(s, (z + 1) * 4 + y * 2 + c), device_id_type=MESH,
+        )
+
+    def strip_down(r, i):
+        return pltpu.make_async_remote_copy(
+            WG.at[held(r), i, 1 - y, c, :, pl.ds(MAIN, 1024 - MAIN)], RDS.at[r % 7, i], ds_.at[r, 3 + i], dr.at[r, 3 + i],
+            device_id=(s, (z - 1) * 4 + y * 2 + c), device_id_type=MESH,
+        )
+
+    def strip_y(r):
+        return pltpu.make_async_remote_copy(
+            WG.at[held(r), z, 1 - y, c, :, pl.ds(MAIN, 1024 - MAIN)], RYS.at[r % 4], yss.at[r], ysr.at[r],
+            device_id=(s, z * 4 + (1 - y) * 2 + c), device_id_type=MESH,
+        )
+
     def each_out(r, act):
         k = held(r)
         src = T.at[r % 2]
@@ -806,6 +854,15 @@
     def add(k, i, j, other):
         WG[k, i, j, c] = (WG[k, i, j, c].astype(F32) + other.astype(F32)).astype(B16)
 
+    def add_main(k, i, other):
+        WG[k, i, y, c, :, :MAIN] = (WG[k, i, y, c, :, :MAIN].astype(F32) + other.astype(F32)).astype(B16)
+
+    def add_strip(k, i, *others):
+        total = WG[k, i, 1 - y, c, :, MAIN:].astype(F32)
+        for other in others:
+            total = total + other.astype(F32)
+        WG[k, i, 1 - y, c, :, MAIN:] = total.astype(B16)
+
     def live(r):
         return (r >= 0) & (r < NP)
 
@@ -838,17 +895,19 @@
 
             @pl.loop(0, 4)
             def _(i):
-                add(k, i, y, RY[r % 4, i])
+                add_main(k, i, RY[r % 4, i])
 
             @pl.when(z == 0)
             def _():
                 for i in (3, 2, 1):
                     up(r, i).start()
+                    strip_up(r, i).start()
 
             @pl.when(z == 3)
             def _():
                 for i in (0, 1, 2):
                     down(r, i).start()
+                    strip_down(r, i).start()
 
         for q in (1, 2, 3):
             n = 4 - q
@@ -865,6 +924,10 @@
                         if i > q:
                             add(k, i, y, RU[r % 7, i - 1])
                             up(r, i).start()
+                        strip_up(r, i).wait_recv()
+                        if i > q:
+                            add_strip(k, i, RUS[r % 7, i - 1])
+                            strip_up(r, i).start()
 
                 @pl.when(z == 3 - q)
                 def _():
@@ -873,12 +936,26 @@
                         if i < n - 1:
                             add(k, i, y, RD[r % 7, i])
                             down(r, i).start()
+                        strip_down(r, i).wait_recv()
+                        if i < n - 1:
+                            add_strip(k, i, RDS[r % 7, i])
+                            strip_down(r, i).start()
 
         @pl.when(live(t - 5))
         def _():
             r = t - 5
             k = held(r)
 
+            @pl.when(z > 0)
+            def _():
+                add_strip(k, z, RUS[r % 7, z - 1])
+
+            @pl.when(z < 3)
+            def _():
+                add_strip(k, z, RDS[r % 7, z])
+
+            strip_y(r).start()
+
             @pl.when(r >= 2)
             def _():
                 each_out(r - 2, lambda cp: cp.wait())
@@ -893,6 +970,11 @@
             def _():
                 T[r % 2] += RD[r % 7, z].astype(F32)
 
+        @pl.when(live(t - 6))
+        def _():
+            r = t - 6
+            strip_y(r).wait_recv()
+            T[r % 2, :, MAIN:] += RYS[r % 4].astype(F32)
             each_out(r, start)
 
     @pl.loop(0, BACK_TICKS)
@@ -950,17 +1032,20 @@
 
         across_c(r).wait_send()
         across_y(r).wait_send()
+        strip_y(r).wait_send()
         for q in range(3):
 
             @pl.when(z == q)
             def _():
                 for i in range(q + 1, 4):
                     up(r, i).wait_send()
+                    strip_up(r, i).wait_send()
 
             @pl.when(z == q + 1)
             def _():
                 for i in range(q + 1):
                     down(r, i).wait_send()
+                    strip_down(r, i).wait_send()
 
     sums_out()
     pref_out()
@@ -988,7 +1073,8 @@
         ((NP,) + wide, B16), ((n, d), B16), ((n, d), B16), ((3, n, d), B16), ((4, n, d), B16), ((2, HALF, HALF), B16), ((n, d), B16),
         ((n, d), F32), ((n, d), B16), ((4, n, d), B16), ((n, d), B16), ((n, d), B16), ((HALF, d), B16), ((HALF, HALF), F32),
         ((HALF, HALF), B16), ((HALF, d), F32),
-        ((4, 4, 2, 64, d), B16), ((4, 4, 64, d), B16), ((7, 3, 64, d), B16), ((7, 3, 64, d), B16), ((2, 64, d), F32),
+        ((4, 4, 2, 64, d), B16), ((4, 4, 64, MAIN), B16), ((7, 3, 64, d), B16), ((7, 3, 64, d), B16),
+        ((7, 3, 64, d - MAIN), B16), ((7, 3, 64, d - MAIN), B16), ((4, 64, d - MAIN), B16), ((2, 64, d), F32),
         ((16, d), F32), ((32, d), F32), ((16, 32, 128), F32), ((16, 32, 128), F32), ((16, 128), B16), ((16, 16, 128), B16),
         ((16, 512), F32), ((16, 512), F32),
     ]
@@ -997,7 +1083,7 @@
         out_shape=[jax.ShapeDtypeStruct(*o) for o in outs],
         in_specs=[any_] * 13 + [vm] * 3,
         out_specs=[any_] * 5 + [vm] * 3,
-        scratch_shapes=[pltpu.VMEM(*v) for v in scratch] + [dma((NP,))] * 7 + [dma((NP, 3))] * 4 + [dma((2,))] * 3 + [dma((16,))] * 4 + [dma((4,))],
+        scratch_shapes=[pltpu.VMEM(*v) for v in scratch] + [dma((NP,))] * 7 + [dma((NP, 6))] * 4 + [dma((NP,))] * 2 + [dma((2,))] * 3 + [dma((16,))] * 4 + [dma((4,))],
         compiler_params=pltpu.CompilerParams(collective_id=1, has_side_effects=True, vmem_limit_bytes=64 << 20),
     )(W.reshape((NP,) + wide), h, a1, qkv, prob, ppre, att, res, a2, gp, act, cot, r_out, small, pkey, pval)
 

time: 439 us -> 419 us (0.954)
  Pallas kernels: 433 us -> 412 us
    pallas_call x1, Pallas kernels: 248 us -> 237 us  [backward_call(): pl.pallas_call(backward_kernel, out_shape=[jax.ShapeDtypeStruct(*o) for o...]
    pallas_call x1, Pallas kernels: 176 us -> 167 us  [forward_call(): pl.pallas_call(forward_kernel, out_shape=[jax.ShapeDtypeStruct(*k) for k...]
where the time goes in v5:
time: 419 us; the launch traced here: 418 us
  Pallas kernels  412 us (98%)
    pallas_call x1, Pallas kernels, backward_call(): pl.pallas_call(backward_kernel, out_shape=[jax.ShapeDtypeStruct(*o) for o...  237 us
    pallas_call x1, Pallas kernels, forward_call(): pl.pallas_call(forward_kernel, out_shape=[jax.ShapeDtypeStruct(*k) for k...  167 us
    pallas_call x1, Pallas kernels, finish_call(): pl.pallas_call(finish_kernel, out_shape=outs, in_specs=[any_] * 6 + [vm]...  8.4 us

profile of v5, /device:TPU:0, one launch (start us, length us, event | category | flops | bytes accessed | tf_op | source)
XLA Modules:
  0.0 418.2 jit_solution(9816952748884044000)
XLA Ops:
  0.7 0.1 pad.8.clone
  0.7 0.7 reduce
  1.4 0.1 reshape.41
  1.5 1.4 maximum_maximum_fusion.1.pack
  2.9 0.7 pad.4
  3.6 0.7 reshape.44
  4.3 1.4 maximum_maximum_fusion.aux
  5.8 166.7 %shard_map.237 = (bf16[12288,1024]{1,0:T(8,128)(2,1)}, bf16[512,1024]{1,0:T(8,128)(2,1)}, bf16[512,1024]{1,0:T(8,128)(2,1)}, bf16[512,1024]{1,0:T(8,128)(2,1)}, ...) custom-call(bf16[1,64,3072]{2,1,0:T(8,128)(2,1)} %wq.1, ...), custom_call_target="tpu_custom_call" | custom-call | tf_op jit(solution)/shard_map/pallas_call | solution.py:475
  172.5 237.2 %shard_map.238 = (bf16[512,1024]{1,0:T(8,128)(2,1)}, f32[1,64,3072]{2,1,0:T(8,128)}, f32[1,64,1024]{2,1,0:T(8,128)}, f32[1,64,4096]{2,1,0:T(8,128)}, f32[1,256,1...) custom-call(bf16[12,4,2,2,64,1024]{5,4,3,2,1,0:T(8,128)(2,1)} %bitcast.6, ...), custom_call_target="tpu_custom_call" | custom-call | tf_op jit(solution)/shard_map/pallas_call | solution.py:1081
  409.7 8.4 %shard_map.239 = (bf16[512,1024]{1,0:T(8,128)(2,1)}, bf16[512,1024]{1,0:T(8,128)(2,1)}, f32[1,64,3072]{2,1,0:T(8,128)}, f32[1,64,1024]{2,1,0:T(8,128)}, f32[1,64...) custom-call(bf16[512,1024]{1,0:T(8,128)(2,1)} %get-tuple-element.50., ...), custom_call_target="tpu_custom_call" | custom-call | tf_op jit(solution)/shard_map/pallas_call | solution.py:1128
  (3 shorter events, 0.0 us)

commit v6 on v5

--- a/solution.py
+++ b/solution.py
@@ -27,7 +27,10 @@
     for i in range(1, 16):
         pl.semaphore_signal(bar, 1, device_id=(s, (d + i) % 16), device_id_type=MESH)
     pl.semaphore_signal(bar, 1, device_id=(1 - s, d), device_id_type=MESH)
-    pl.semaphore_wait(bar, 16)
+
+
+def greeted():
+    pl.semaphore_wait(pltpu.get_barrier_semaphore(), 16)
 
 
 def to_all(src, dst, ss, rs):
@@ -209,10 +212,10 @@
 
 
 def forward_kernel(
-    wq, wo, wf, wp, tokens, segs, pack, aux, r_in, r_out,
+    wq, wo, wf, wp, tokens, segs, gains, biases, aux, r_in, r_out,
     W_o, out_o, h_o, a1_o, qkv_o, prob_o, ppre_o, att_o, res_o, a2_o, gp_o, act_o, small_o, pkey_o, pval_o, hid_o,
-    W, H, A1, QKV, PROB, PPRE, ATT, RES, A2, GP, ACT, OUT, SPRE, ACC, small, pkey, pval, hid, mask, PACKS, ROWS,
-    own_sem, ssem, rsem, tsem, qsem, hsem, xs, xr, save_sem, ps, pr, psem,
+    W, H, A1, QKV, PROB, PPRE, ATT, RES, A2, GP, ACT, OUT, SPRE, ACC, small, pkey, pval, hid, mask, pack, PACKS, ROWS,
+    own_sem, ssem, rsem, tsem, qsem, hsem, xs, xr, save_sem, fs, ps, pr, psem,
 ):
     g = Gather(W, ssem, rsem, tsem, qsem)
     s = g.s
@@ -223,6 +226,14 @@
     for cp in r_in_parts + r_out_parts:
         cp.start()
     greet(s, g.d)
+    own_bias = biases[...].astype(F32)
+    for n in range(2):
+        for r in range(11):
+            ROWS[0, r : r + 1, 64 * n : 64 * n + 64] = own_bias[:, 64 * r : 64 * r + 64]
+        ROWS[0, 11:13, 64 * n : 64 * n + 64] = gains[0].astype(F32)
+    ROWS[0, 13:16] = jnp.zeros((3, 128), F32)
+    pack[...] = ROWS[0].astype(B16)
+    greeted()
     send_packs, packs_in, packs_out = to_all(lambda to: pack, PACKS, ps, pr)
 
     def prep_saves():
@@ -290,9 +301,16 @@
         pairs = [
             (H.at[r], h_o.at[r]), (A1.at[r], a1_o.at[r]), (QKV.at[:, r], qkv_o.at[:, r]), (PROB.at[pl.ds(2 * b, 2)], prob_o.at[pl.ds(2 * b, 2)]),
             (PPRE.at[b], ppre_o.at[b]), (ATT.at[r], att_o.at[r]), (RES.at[r], res_o.at[r]), (A2.at[r], a2_o.at[r]),
-            (GP.at[:, r], gp_o.at[:, r]), (ACT.at[:, r], act_o.at[:, r]), (OUT.at[r], out_o.at[r]),
+            (OUT.at[r], out_o.at[r]),
         ]
         return [pltpu.make_async_copy(src, dst, save_sem.at[b, i]) for i, (src, dst) in enumerate(pairs)]
+
+    def ffn_saves(b, j):
+        r = half(b)
+        return [
+            pltpu.make_async_copy(GP.at[j, r], gp_o.at[j, r], fs.at[b, j]),
+            pltpu.make_async_copy(ACT.at[j, r], act_o.at[j, r], fs.at[b, 4 + j]),
+        ]
 
     def piece_out(k):
         return pltpu.make_async_copy(W.at[rows_of(k)], W_o.at[rows_of(k)], save_sem.at[2, k])
@@ -373,10 +391,8 @@
         ACT[j, half(b)] = act.astype(B16)
         GP[j, half(b)] = (h + act * (1.0 - h) * (2.0 * GELU_C + (6 * 0.044715 * GELU_C) * x2)).astype(B16)
 
-        @pl.when(j == 3)
-        def _():
-            saves(b)[8].start()
-            saves(b)[9].start()
+        for cp in ffn_saves(b, j):
+            cp.start()
 
     def narrow(b):
         v = RES[half(b)] + small[8:9]
@@ -388,7 +404,7 @@
         def _():
             cross(b).start()
 
-        saves(b)[10].start()
+        saves(b)[8].start()
 
     @pl.loop(0, NP + 5 + 2 * STAGES)
     def _(tick):
@@ -452,7 +468,7 @@
 
     @pl.loop(0, 2)
     def _(b):
-        for cp in saves(b):
+        for cp in saves(b) + [cp for j in range(4) for cp in ffn_saves(b, j)]:
             cp.wait()
 
         @pl.when(s == 0)
@@ -460,7 +476,7 @@
             cross(b).wait_send()
 
 
-def forward_call(wq, wo, wf, wp, tokens, segs, pack, aux, r_in, r_out):
+def forward_call(wq, wo, wf, wp, tokens, segs, gains, biases, aux, r_in, r_out):
     any_, vm = pl.BlockSpec(memory_space=pl.ANY), pl.BlockSpec(memory_space=pltpu.VMEM)
     n, d = tokens.shape
     kept = [
@@ -471,21 +487,16 @@
     dma = pltpu.SemaphoreType.DMA
     order = [0, 2, 3, 4, 5, 6, 7, 8, 9, 10, 11, 1]
     scratch = [kept[i] for i in order] + [((2, HALF, HALF), F32), ((n, d), F32)] + shared
-    scratch += [((2, HALF, HALF), F32), ((16, 16, 128), B16), ((16, 16, 128), F32)]
+    scratch += [((2, HALF, HALF), F32), ((16, 128), B16), ((16, 16, 128), B16), ((16, 16, 128), F32)]
     return pl.pallas_call(
         forward_kernel,
         out_shape=[jax.ShapeDtypeStruct(*k) for k in kept + shared],
-        in_specs=[any_] * 5 + [vm] * 3 + [any_] * 2,
+        in_specs=[any_] * 5 + [vm] * 4 + [any_] * 2,
         out_specs=[any_] * len(kept + shared),
         scratch_shapes=[pltpu.VMEM(*v) for v in scratch]
-        + [dma((NP,)), dma((NP, 20)), dma((NP, 16)), dma((NP, 8)), dma((NP, 4)), dma, dma((2,)), dma((2,)), dma((3, NP)), dma((16,)), dma((16,)), dma((8,))],
+        + [dma((NP,)), dma((NP, 20)), dma((NP, 16)), dma((NP, 8)), dma((NP, 4)), dma, dma((2,)), dma((2,)), dma((3, NP)), dma((2, 8)), dma((16,)), dma((16,)), dma((8,))],
         compiler_params=pltpu.CompilerParams(collective_id=0, has_side_effects=True, vmem_limit_bytes=62 << 20),
-    )(wq, wo, wf, wp, tokens, segs, pack, aux, r_in, r_out)
-
-
-def own_pack(gains, biases):
-    rows = jnp.concatenate([biases.reshape(11, 64), gains.reshape(2, 64), jnp.zeros((3, 64), B16)])
-    return jnp.concatenate([rows, rows], axis=1)
+    )(wq, wo, wf, wp, tokens, segs, gains, biases, aux, r_in, r_out)
 
 
 def prefix_rows(embed, in_bias, out_bias):
@@ -514,7 +525,7 @@
     dh_o, oq, oo, of, op_, own_sums, KVB, HSUM,
     WG, H, A1, QKV, BIG, PPRE, ATT, RES, A2, GP, DM, DAT, DATT, DPP, DSP, ACC,
     RC, RY, RU, RD, RUS, RDS, RYS, T, SG, DKV, SB, RB, PF, PG, HP, HPR,
-    wsem, lsem, osem, cs, cr, ys, yr, us, ur, ds_, dr, yss, ysr, xs, xr, hs, bs, br, ps, pr, hx,
+    wsem, lsem, osem, cs, cr, ys, yr, us, ur, ds_, dr, yss, ysr, xs, xr, hs, bs, br, ps, pr, hx, gs,
 ):
     s, d, z, y, c = place()
 
@@ -530,19 +541,24 @@
 
     def loads():
         pairs = [
-            (gp_i, GP), (a2_i, A2), (res_i, RES), (att_i, ATT), (qkv_i, QKV), (ppre_i, PPRE), (a1_i, A1), (h_i, H),
+            (a2_i, A2), (res_i, RES), (att_i, ATT), (qkv_i, QKV), (ppre_i, PPRE), (a1_i, A1), (h_i, H),
             (act_i, BIG), (prob_i, BIG), (cot, DM),
         ]
         return [pltpu.make_async_copy(a, b, lsem.at[i]) for i, (a, b) in enumerate(pairs)]
 
-    L_GP, L_A2, L_RES, L_ATT, L_QKV, L_PPRE, L_A1, L_H, L_ACT, L_PROB, L_COT = range(11)
+    L_A2, L_RES, L_ATT, L_QKV, L_PPRE, L_A1, L_H, L_ACT, L_PROB, L_COT = range(10)
 
     def begin_loads(which):
         begin([loads()[i] for i in which])
 
     pl.when(s == 1)(lambda: begin_loads((L_COT,)))
-    begin(fetch((8, 9, 10, 11)))
-    begin_loads((L_GP,))
+
+    def slope(j):
+        return pltpu.make_async_copy(gp_i.at[j], GP.at[j], gs.at[j])
+
+    for j in range(4):
+        begin(fetch((8 + j,)) + [slope(j)])
+
     pl.when(s == 0)(lambda: begin_loads((L_ACT,)))
     SG[...] = jnp.zeros_like(SG)
     DKV[...] = jnp.zeros_like(DKV)
@@ -567,35 +583,30 @@
     def dh_out(b):
         return pltpu.make_async_copy(H.at[half(b)], dh_o.at[half(b)], hs.at[b])
 
+    def more(j):
+        if j < 2:
+            begin(fetch((4 + 2 * j, 5 + 2 * j)))
+        elif j == 2:
+            begin_loads((L_A2, L_RES))
+            pl.when(s == 1)(lambda: begin(fetch((3,))))
+        else:
+            pl.when(s == 1)(lambda: begin_loads((L_QKV, L_PPRE, L_PROB)))
+
     def ffn_in(b):
-        first = (b == 0)
-
-        @pl.when(first)
-        def _():
-            @pl.when(s == 1)
-            def _():
-                loads()[L_COT].wait()
-
-            weights((8, 9, 10, 11))
-            loads()[L_GP].wait()
-            begin(fetch((4, 5, 6, 7)))
-            begin_loads((L_A2, L_RES))
-
-            @pl.when(s == 1)
-            def _():
-                begin(fetch((3,)))
-                begin_loads((L_QKV, L_PPRE, L_PROB))
+        if b == 0:
+            pl.when(s == 1)(lambda: loads()[L_COT].wait())
+            pl.when(s == 0)(lambda: cross(0).wait_recv())
+        for j in range(4):
+            if b == 0:
+                weights((8 + j,))
+                slope(j).wait()
+                more(j)
+            GP[j, half(b)] = (dot_nt(DM[half(b)], weight(8 + j)) * GP[j, half(b)].astype(F32)).astype(B16)
+        if b == 1:
 
             @pl.when(s == 0)
             def _():
-                cross(0).wait_recv()
-
-        for j in range(4):
-            GP[j, half(b)] = (dot_nt(DM[half(b)], weight(8 + j)) * GP[j, half(b)].astype(F32)).astype(B16)
-
-        @pl.when((s == 0) & (b == 1))
-        def _():
-            begin(fetch((3, 0, 1, 2)))
+                begin(fetch((3, 0, 1, 2)))
 
     def ffn_norm(b):
         @pl.when(b == 0)
@@ -699,22 +710,16 @@
 
         dh_out(b).start()
 
-    def grad_proj():
-        loads()[L_ACT].wait()
-
-        @pl.when(s == 0)
-        def _():
-            cross(1).wait_recv()
-        @pl.loop(0, 4)
-        def _(i):
-            for u in range(2):
-                v = dot_tn(BIG[i, :, 512 * u : 512 * (u + 1)], DM[...]).astype(B16).reshape(2, 4, 64, 1024)
-                for j in range(4):
-                    WG[8 * s + j, i, u] = v[:, j]
-
-        @pl.when(s == 0)
-        def _():
-            loads()[L_PROB].start()
+    def grad_proj(j):
+        if j == 0:
+            loads()[L_ACT].wait()
+            pl.when(s == 0)(lambda: cross(1).wait_recv())
+        for i in range(4):
+            cols = [BIG[i, :, 256 * q + 64 * j : 256 * q + 64 * j + 64] for q in range(4)]
+            part = dot_tn(jnp.concatenate(cols, axis=1), DM[...])
+            WG[8 * s + j, i] = part.astype(B16).reshape(2, 2, 64, 1024)
+        if j == 3:
+            pl.when(s == 0)(lambda: loads()[L_PROB].start())
 
     def put(k, a, v):
         for i in range(2):
@@ -977,13 +982,16 @@
             T[r % 2, :, MAIN:] += RYS[r % 4].astype(F32)
             each_out(r, start)
 
-    @pl.loop(0, BACK_TICKS)
+    ffn_in(0)
+    greeted()
+
+    @pl.loop(1, BACK_TICKS)
     def _(tick):
         turn = tick // SPLIT
 
-        @pl.when((tick == 0) | (tick == 2 * (1 - s) + SPLIT * s))
-        def _():
-            ffn_in((tick > 0).astype(jnp.int32))
+        @pl.when(tick == 2 * (1 - s) + SPLIT * s)
+        def _():
+            ffn_in(1)
 
         def when(i, at0, at1, body):
             early = (1 - s) * at0 + s * i
@@ -1004,9 +1012,8 @@
         when(5, 9, 10, attn_norm)
         r = tick - 1 - (2 * SPLIT - 1) * s
 
-        @pl.when(r == 0)
-        def _():
-            grad_proj()
+        for j in range(4):
+            pl.when(r == j)(lambda j=j: grad_proj(j))
 
         @pl.when((r >= 4) & (r < 8))
         def _():
@@ -1021,7 +1028,7 @@
             grad_qkv(11 - r)
 
         scatter_step(r)
-        for at, body in ((10, small_first), (11, small_second), (13, small_third), (16, small_last)):
+        for at, body in ((9, small_first), (11, small_second), (13, small_third), (17, small_last)):
             pl.when(r == at)(body)
 
     @pl.loop(0, NP)
@@ -1083,7 +1090,7 @@
         out_shape=[jax.ShapeDtypeStruct(*o) for o in outs],
         in_specs=[any_] * 13 + [vm] * 3,
         out_specs=[any_] * 5 + [vm] * 3,
-        scratch_shapes=[pltpu.VMEM(*v) for v in scratch] + [dma((NP,))] * 7 + [dma((NP, 6))] * 4 + [dma((NP,))] * 2 + [dma((2,))] * 3 + [dma((16,))] * 4 + [dma((4,))],
+        scratch_shapes=[pltpu.VMEM(*v) for v in scratch] + [dma((NP,))] * 7 + [dma((NP, 6))] * 4 + [dma((NP,))] * 2 + [dma((2,))] * 3 + [dma((16,))] * 4 + [dma((4,))] * 2,
         compiler_params=pltpu.CompilerParams(collective_id=1, has_side_effects=True, vmem_limit_bytes=64 << 20),
     )(W.reshape((NP,) + wide), h, a1, qkv, prob, ppre, att, res, a2, gp, act, cot, r_out, small, pkey, pval)
 
@@ -1154,8 +1161,7 @@
     reparam_out_bias,
 ):
     aux = prefix_rows(prefix_embed, reparam_in_bias, reparam_out_bias)
-    pack = own_pack(gains, biases)
-    kept = forward_call(w_qkv, w_attn_out, w_fc, w_proj, tokens, segment_ids, pack, aux, reparam_in, reparam_out)
+    kept = forward_call(w_qkv, w_attn_out, w_fc, w_proj, tokens, segment_ids, gains, biases, aux, reparam_in, reparam_out)
     small, pkey, pval, hid = kept[12:]
     *large, sums, kvb, hsum = backward_call(kept[:1] + kept[2:12], cotangent, reparam_out, small, pkey, pval)
     done = finish_call([kept[1]] + large, hid, kvb, hsum, aux, reparam_in, sums)

time: 419 us -> 410 us (0.979)
  Pallas kernels: 412 us -> 405 us
    pallas_call x1, Pallas kernels: 237 us -> 230 us  [backward_call(): pl.pallas_call(backward_kernel, out_shape=[jax.ShapeDtypeStruct(*o) for o...]
where the time goes in v6:
time: 410 us; the launch traced here: 409 us
  Pallas kernels  405 us (99%)
    pallas_call x1, Pallas kernels, backward_call(): pl.pallas_call(backward_kernel, out_shape=[jax.ShapeDtypeStruct(*o) for o...  230 us
    pallas_call x1, Pallas kernels, forward_call(): pl.pallas_call(forward_kernel, out_shape=[jax.ShapeDtypeStruct(*k) for k...  167 us
    pallas_call x1, Pallas kernels, finish_call(): pl.pallas_call(finish_kernel, out_shape=outs, in_specs=[any_] * 6 + [vm]...  8.4 us

profile of v6, /device:TPU:0, one launch (start us, length us, event | category | flops | bytes accessed | tf_op | source)
XLA Modules:
  0.0 409.2 jit_solution(16957788929945457124)
XLA Ops:
  0.7 0.1 pad.8.clone
  0.7 0.7 pad.4
  1.4 0.7 reshape.36
  2.1 1.4 maximum_maximum_fusion.aux
  3.5 166.9 %shard_map.237 = (bf16[12288,1024]{1,0:T(8,128)(2,1)}, bf16[512,1024]{1,0:T(8,128)(2,1)}, bf16[512,1024]{1,0:T(8,128)(2,1)}, bf16[512,1024]{1,0:T(8,128)(2,1)}, ...) custom-call(bf16[1,64,3072]{2,1,0:T(8,128)(2,1)} %wq.1, ...), custom_call_target="tpu_custom_call" | custom-call | tf_op jit(solution)/shard_map/pallas_call | solution.py:491
  170.4 230.1 %shard_map.238 = (bf16[512,1024]{1,0:T(8,128)(2,1)}, f32[1,64,3072]{2,1,0:T(8,128)}, f32[1,64,1024]{2,1,0:T(8,128)}, f32[1,64,4096]{2,1,0:T(8,128)}, f32[1,256,1...) custom-call(bf16[12,4,2,2,64,1024]{5,4,3,2,1,0:T(8,128)(2,1)} %bitcast.5, ...), custom_call_target="tpu_custom_call" | custom-call | tf_op jit(solution)/shard_map/pallas_call | solution.py:1088
  400.6 8.4 %shard_map.239 = (bf16[512,1024]{1,0:T(8,128)(2,1)}, bf16[512,1024]{1,0:T(8,128)(2,1)}, f32[1,64,3072]{2,1,0:T(8,128)}, f32[1,64,1024]{2,1,0:T(8,128)}, f32[1,64...) custom-call(bf16[512,1024]{1,0:T(8,128)(2,1)} %get-tuple-element.50., ...), custom_call_target="tpu_custom_call" | custom-call | tf_op jit(solution)/shard_map/pallas_call | solution.py:1135
  (2 shorter events, 0.0 us)

commit v7 on v6

--- a/solution.py
+++ b/solution.py
@@ -647,8 +647,7 @@
         DPP[...] = dot_nt(pval[...], DATT[...])
 
     def attn_back(part, b):
-        @pl.loop(part * 4, part * 4 + 4)
-        def _(p):
+        def pair(p):
             cols = pl.ds(pl.multiple_of(p * 128, 128), 128)
             q2, k2, v2 = QKV[0, half(b), cols], QKV[1, half(b), cols], QKV[2, half(b), cols]
             do2 = DATT[:, cols]
@@ -672,6 +671,9 @@
             QKV[1, half(b), cols] = jnp.where(left, dk[:HALF], dk[HALF:]).astype(B16)
             QKV[2, half(b), cols] = jnp.where(left, dv[:HALF], dv[HALF:]).astype(B16)
 
+        for p in range(4):
+            pair(part * 4 + p)
+
         @pl.when(part == 1)
         def _():
             def own_rows(full):
@@ -1028,7 +1030,7 @@
             grad_qkv(11 - r)
 
         scatter_step(r)
-        for at, body in ((9, small_first), (11, small_second), (13, small_third), (17, small_last)):
+        for at, body in ((9, small_first), (12, small_second), (15, small_third)):
             pl.when(r == at)(body)
 
     @pl.loop(0, NP)
@@ -1054,6 +1056,7 @@
                     down(r, i).wait_send()
                     strip_down(r, i).wait_send()
 
+    small_last()
     sums_out()
     pref_out()
 
@@ -1098,13 +1101,15 @@
 def finish_kernel(
     o0, o1, o2, o3, o4, o5, hid, kvb, hsum, aux, r_in, sums,
     c0, c1, c2, c3, c4, c5, g_embed, g_in, g_in_bias, g_out, g_out_bias, g_gains, g_bias,
-    G_IN, G_OUT, M0, M1, M2, M3, M4, M5, sem,
+    G_IN, G_OUT, M0, M1, M2, M3, M4, M5, R_IN, sem,
 ):
     held = (M0, M1, M2, M3, M4, M5)
     here = [pltpu.make_async_copy(a, m, sem.at[i]) for i, (a, m) in enumerate(zip((o0, o1, o2, o3, o4, o5), held))]
     away = [pltpu.make_async_copy(m, c, sem.at[8 + i]) for i, (m, c) in enumerate(zip(held, (c0, c1, c2, c3, c4, c5)))]
     for cp in here:
         cp.start()
+    weight_in = pltpu.make_async_copy(r_in, R_IN, sem.at[14])
+    weight_in.start()
     h = hid[...]
     kv = kvb[...]
     G_OUT[...] = dot_tn(h.astype(B16), kv)
@@ -1119,7 +1124,8 @@
     in_cp = pltpu.make_async_copy(G_IN, g_in, sem.at[7])
     in_cp.start()
     g_in_bias[...] = column_sum(dp)
-    g_embed[...] = dot_nt(dp, r_in[...])[:10]
+    weight_in.wait()
+    g_embed[...] = dot_nt(dp, R_IN[...])[:10]
     g_gains[0] = sums[11:13, :64]
     for i in range(11):
         g_bias[:, 64 * i : 64 * i + 64] = sums[i : i + 1, :64]
@@ -1135,11 +1141,11 @@
     return pl.pallas_call(
         finish_kernel,
         out_shape=outs,
-        in_specs=[any_] * 6 + [vm] * 6,
+        in_specs=[any_] * 6 + [vm] * 4 + [any_, vm],
         out_specs=[any_] * 6 + [vm, any_, vm, any_, vm, vm, vm],
         scratch_shapes=[pltpu.VMEM((d, 512), F32), pltpu.VMEM((512, 2 * d), F32)]
         + [pltpu.VMEM(x.shape, x.dtype) for x in large]
-        + [pltpu.SemaphoreType.DMA((14,))],
+        + [pltpu.VMEM(r_in.shape, r_in.dtype), pltpu.SemaphoreType.DMA((15,))],
         compiler_params=pltpu.CompilerParams(vmem_limit_bytes=63 << 20),
     )(*large, hid, kvb, hsum, aux, r_in, sums)
 

time: 410 us -> 406 us (level)
  no operation moved by 1% of the time
where the time goes in v7:
time: 406 us; the launch traced here: 405 us
  Pallas kernels  402 us (99%)
    pallas_call x1, Pallas kernels, backward_call(): pl.pallas_call(backward_kernel, out_shape=[jax.ShapeDtypeStruct(*o) for o...  227 us
    pallas_call x1, Pallas kernels, forward_call(): pl.pallas_call(forward_kernel, out_shape=[jax.ShapeDtypeStruct(*k) for k...  167 us

profile of v7, /device:TPU:0, one launch (start us, length us, event | category | flops | bytes accessed | tf_op | source)
XLA Modules:
  0.0 405.3 jit_solution(17126603270895056990)
XLA Ops:
  0.7 0.1 pad.8.clone
  0.7 0.7 pad.4
  1.4 0.7 reshape.36
  2.1 1.4 maximum_maximum_fusion.aux
  3.5 166.9 %shard_map.237 = (bf16[12288,1024]{1,0:T(8,128)(2,1)}, bf16[512,1024]{1,0:T(8,128)(2,1)}, bf16[512,1024]{1,0:T(8,128)(2,1)}, bf16[512,1024]{1,0:T(8,128)(2,1)}, ...) custom-call(bf16[1,64,3072]{2,1,0:T(8,128)(2,1)} %wq.1, ...), custom_call_target="tpu_custom_call" | custom-call | tf_op jit(solution)/shard_map/pallas_call | solution.py:491
  170.4 226.8 %shard_map.238 = (bf16[512,1024]{1,0:T(8,128)(2,1)}, f32[1,64,3072]{2,1,0:T(8,128)}, f32[1,64,1024]{2,1,0:T(8,128)}, f32[1,64,4096]{2,1,0:T(8,128)}, f32[1,256,1...) custom-call(bf16[12,4,2,2,64,1024]{5,4,3,2,1,0:T(8,128)(2,1)} %bitcast.5, ...), custom_call_target="tpu_custom_call" | custom-call | tf_op jit(solution)/shard_map/pallas_call | solution.py:1091
  397.2 7.9 %shard_map.239 = (bf16[512,1024]{1,0:T(8,128)(2,1)}, bf16[512,1024]{1,0:T(8,128)(2,1)}, f32[1,64,3072]{2,1,0:T(8,128)}, f32[1,64,1024]{2,1,0:T(8,128)}, f32[1,64...) custom-call(bf16[512,1024]{1,0:T(8,128)(2,1)} %get-tuple-element.50., ...), custom_call_target="tpu_custom_call" | custom-call | tf_op jit(solution)/shard_map/pallas_call | solution.py:1141
  (2 shorter events, 0.0 us)

commit v8 on v7

--- a/solution.py
+++ b/solution.py
@@ -894,28 +894,6 @@
             def _(i):
                 add(k, i, y, RC[r % 4, i, y])
 
-        @pl.when(live(t - 2))
-        def _():
-            r = t - 2
-            k = held(r)
-            across_y(r).wait_recv()
-
-            @pl.loop(0, 4)
-            def _(i):
-                add_main(k, i, RY[r % 4, i])
-
-            @pl.when(z == 0)
-            def _():
-                for i in (3, 2, 1):
-                    up(r, i).start()
-                    strip_up(r, i).start()
-
-            @pl.when(z == 3)
-            def _():
-                for i in (0, 1, 2):
-                    down(r, i).start()
-                    strip_down(r, i).start()
-
         for q in (1, 2, 3):
             n = 4 - q
 
@@ -947,6 +925,28 @@
                         if i < n - 1:
                             add_strip(k, i, RDS[r % 7, i])
                             strip_down(r, i).start()
+
+        @pl.when(live(t - 2))
+        def _():
+            r = t - 2
+            k = held(r)
+            across_y(r).wait_recv()
+
+            @pl.loop(0, 4)
+            def _(i):
+                add_main(k, i, RY[r % 4, i])
+
+            @pl.when(z == 0)
+            def _():
+                for i in (3, 2, 1):
+                    up(r, i).start()
+                    strip_up(r, i).start()
+
+            @pl.when(z == 3)
+            def _():
+                for i in (0, 1, 2):
+                    down(r, i).start()
+                    strip_down(r, i).start()
 
         @pl.when(live(t - 5))
         def _():

time: 406 us -> 405 us (level)
  no operation moved by 1% of the time
where the time goes in v8:
time: 405 us
  Pallas kernels  401 us (99%)
    pallas_call x1, Pallas kernels, backward_call(): pl.pallas_call(backward_kernel, out_shape=[jax.ShapeDtypeStruct(*o) for o...  227 us
    pallas_call x1, Pallas kernels, forward_call(): pl.pallas_call(forward_kernel, out_shape=[jax.ShapeDtypeStruct(*k) for k...  167 us

profile of v8, /device:TPU:0, one launch (start us, length us, event | category | flops | bytes accessed | tf_op | source)
XLA Modules:
  0.0 405.1 jit_solution(4454025832210944432)
XLA Ops:
  0.7 0.1 pad.8.clone
  0.7 0.7 pad.4
  1.4 0.7 reshape.36
  2.1 1.4 maximum_maximum_fusion.aux
  3.5 166.9 %shard_map.237 = (bf16[12288,1024]{1,0:T(8,128)(2,1)}, bf16[512,1024]{1,0:T(8,128)(2,1)}, bf16[512,1024]{1,0:T(8,128)(2,1)}, bf16[512,1024]{1,0:T(8,128)(2,1)}, ...) custom-call(bf16[1,64,3072]{2,1,0:T(8,128)(2,1)} %wq.1, ...), custom_call_target="tpu_custom_call" | custom-call | tf_op jit(solution)/shard_map/pallas_call | solution.py:491
  170.4 226.5 %shard_map.238 = (bf16[512,1024]{1,0:T(8,128)(2,1)}, f32[1,64,3072]{2,1,0:T(8,128)}, f32[1,64,1024]{2,1,0:T(8,128)}, f32[1,64,4096]{2,1,0:T(8,128)}, f32[1,256,1...) custom-call(bf16[12,4,2,2,64,1024]{5,4,3,2,1,0:T(8,128)(2,1)} %bitcast.5, ...), custom_call_target="tpu_custom_call" | custom-call | tf_op jit(solution)/shard_map/pallas_call | solution.py:1091
  397.0 7.9 %shard_map.239 = (bf16[512,1024]{1,0:T(8,128)(2,1)}, bf16[512,1024]{1,0:T(8,128)(2,1)}, f32[1,64,3072]{2,1,0:T(8,128)}, f32[1,64,1024]{2,1,0:T(8,128)}, f32[1,64...) custom-call(bf16[512,1024]{1,0:T(8,128)(2,1)} %get-tuple-element.50., ...), custom_call_target="tpu_custom_call" | custom-call | tf_op jit(solution)/shard_map/pallas_call | solution.py:1141
  (2 shorter events, 0.0 us)
